TPU v7x, 32 devices: a whole 2x2x4 slice. The times are simulated.
32 devices in a mesh: fsdp: 4 (over y, x), ctx: 4 (over z), tp: 2 (over core).
Axes of the slice: x: 2, y: 2, z: 4, core: 2. Of those that a mesh axis runs over, the one named last changes fastest.
Arguments:
- tokens: bfloat16 [2, 4, 1024, 1152], P(None, 'fsdp', 'ctx'), may hold values from -6 to 6
- segments: int32 [2, 4, 1024], P(None, 'fsdp', 'ctx'), may hold values from 0 to 9, never falling along the last dimension, each value on 1 to 800 neighbouring positions
- cotangent: bfloat16 [2, 4, 1024, 1152], P(None, 'fsdp', 'ctx'), may hold values from -6 to 6
- norm_input: bfloat16 [1152], P(('fsdp', 'ctx')), may hold values from 0.25 to 1.75
- query_weight: bfloat16 [1152, 1024], P(('fsdp', 'ctx'), 'tp'), may hold values from -0.1875 to 0.1875
- key_weight: bfloat16 [1152, 256], P(('fsdp', 'ctx')), may hold values from -0.1875 to 0.1875
- value_weight: bfloat16 [1152, 256], P(('fsdp', 'ctx')), may hold values from -0.1875 to 0.1875
- norm_query: bfloat16 [256], P(('fsdp', 'ctx')), may hold values from 0.25 to 1.75
- norm_key: bfloat16 [256], P(('fsdp', 'ctx')), may hold values from 0.25 to 1.75
- out_weight: bfloat16 [1024, 1152], P('tp', ('fsdp', 'ctx')), may hold values from -0.1875 to 0.1875
- norm_attention: bfloat16 [1152], P(('fsdp', 'ctx')), may hold values from 0.25 to 1.75
- norm_feed: bfloat16 [1152], P(('fsdp', 'ctx')), may hold values from 0.25 to 1.75
- gate_weight: bfloat16 [1152, 6912], P(('fsdp', 'ctx'), 'tp'), may hold values from -0.1875 to 0.1875
- up_weight: bfloat16 [1152, 6912], P(('fsdp', 'ctx'), 'tp'), may hold values from -0.1875 to 0.1875
- down_weight: bfloat16 [6912, 1152], P('tp', ('fsdp', 'ctx')), may hold values from -0.078125 to 0.078125
- norm_feed_out: bfloat16 [1152], P(('fsdp', 'ctx')), may hold values from 0.25 to 1.75
Outputs:
- layer_output: bfloat16 [2, 4, 1024, 1152], P(None, 'fsdp', ('ctx', 'tp'))
- input_grad: float32 [2, 4, 1024, 1152], P(None, 'fsdp', ('ctx', 'tp'))
- grad_norm_input: float32 [1152], P(('fsdp', 'ctx'))
- grad_query_weight: float32 [1152, 1024], P(('fsdp', 'ctx'), 'tp')
- grad_key_weight: float32 [1152, 256], P(('fsdp', 'ctx'))
- grad_value_weight: float32 [1152, 256], P(('fsdp', 'ctx'))
- grad_norm_query: float32 [256], P(('fsdp', 'ctx'))
- grad_norm_key: float32 [256], P(('fsdp', 'ctx'))
- grad_out_weight: float32 [1024, 1152], P('tp', ('fsdp', 'ctx'))
- grad_norm_attention: float32 [1152], P(('fsdp', 'ctx'))
- grad_norm_feed: float32 [1152], P(('fsdp', 'ctx'))
- grad_gate_weight: float32 [1152, 6912], P(('fsdp', 'ctx'), 'tp')
- grad_up_weight: float32 [1152, 6912], P(('fsdp', 'ctx'), 'tp')
- grad_down_weight: float32 [6912, 1152], P('tp', ('fsdp', 'ctx'))
- grad_norm_feed_out: float32 [1152], P(('fsdp', 'ctx'))
Inputs may be any that keep to these rules, and one draw needn't show every extreme that they name: `segments`: along each sequence segment numbers never fall; each number is one document of at most 800 consecutive positions.
All inputs are finite; a program needn't handle non-finite values.
Results may differ from a plain program's by a relative error of at most 0.023.
Values may be sent and summed in bfloat16 or wider, within the bound.
No kernel may reach another device: no remote copies, remote signals or barrier semaphores. Data moves between devices by JAX's collectives and lax.ppermute only.
A program may use at most 256 MiB of HBM per device.

v0:
```python
import jax
import jax.numpy as jnp
from jax import lax
from jax.sharding import PartitionSpec as P

HEAD_DIM = 256
WINDOW = 512


EPSILON = 1e-06
ROPE_BASE = 10000.0
SCORE_SCALE = 0.0625
MASKED = -1e30


def entering(value, axis, join, neutral):
    count, mine = (lax.axis_size(axis), lax.axis_index(axis))
    pieces = jax.tree.map(lambda part: lax.all_gather(part, axis), value)
    so_far = jax.tree.map(
        lambda part, zero: jnp.full_like(part, 0) + jnp.asarray(zero, part.dtype), value, neutral
    )

    def lap(position, so_far):
        longer = join(so_far, jax.tree.map(lambda part: part[position], pieces))
        return jax.tree.map(lambda new, old: jnp.where(position < mine, new, old), longer, so_far)

    return lax.fori_loop(0, count - 1, lap, so_far)


def normed(values, gain):
    return values * lax.rsqrt(jnp.mean(values * values, axis=-1, keepdims=True) + EPSILON) * gain


def turned(values, cosines, sines):
    middle = values.shape[-1] // 2
    first_half = values[..., :middle]
    second_half = values[..., middle:]
    return jnp.concatenate(
        [first_half * cosines - second_half * sines, second_half * cosines + first_half * sines],
        axis=-1,
    )


def rotations(offsets, depth):
    middle = depth // 2
    inverse = ROPE_BASE ** (-2.0 * jnp.arange(middle, dtype=jnp.float32) / depth)
    angle_grid = offsets[..., None] * inverse
    return (jnp.cos(angle_grid), jnp.sin(angle_grid))


def rope_normed(values, gain, cosines, sines):
    return turned(normed(values, gain), cosines, sines)


def feed_inner(gate_act, up_act):
    return jax.nn.gelu(gate_act, approximate=True) * up_act


def joined_runs(earlier, later):
    last_seg, last_start, first_seg, whole_run, empty_flag = earlier
    next_last, next_start, next_first, next_whole, next_empty = later
    continues = (next_whole == 1) & (next_first == last_seg)
    merged = (
        next_last,
        jnp.where(continues, last_start, next_start),
        first_seg,
        whole_run * next_whole * (last_seg == next_first).astype(jnp.int32),
        jnp.zeros_like(empty_flag),
    )
    result = []
    for before_item, after_item, merged_item in zip(earlier, later, merged):
        result.append(
            jnp.where(
                empty_flag == 1, after_item, jnp.where(next_empty == 1, before_item, merged_item)
            )
        )
    return tuple(result)


def doc_starts(segment_ids, offset):
    span_len = segment_ids.shape[-1]
    places = offset + jnp.arange(span_len, dtype=jnp.int32)
    edges = jnp.concatenate(
        [
            jnp.ones(segment_ids.shape[:-1] + (1,), dtype=jnp.bool_),
            segment_ids[..., 1:] != segment_ids[..., :-1],
        ],
        axis=-1,
    )
    local_start = lax.cummax(jnp.where(edges, places, 0), axis=2)
    zero_ints = jnp.zeros(segment_ids.shape[:-1], jnp.int32)
    one_ints = jnp.ones(segment_ids.shape[:-1], jnp.int32)
    whole_flag = (segment_ids[..., -1] == segment_ids[..., 0]).astype(jnp.int32)
    carried = entering(
        (segment_ids[..., -1], local_start[..., -1], segment_ids[..., 0], whole_flag, zero_ints),
        "ctx",
        joined_runs,
        (zero_ints, zero_ints, zero_ints, one_ints, one_ints),
    )
    joined = (carried[4] == 0) & (carried[0] == segment_ids[..., 0])
    first_run = segment_ids == segment_ids[..., :1]
    return jnp.where(first_run & joined[..., None], carried[1][..., None], local_start)


def gather_first(shards):
    (
        gain_input,
        query_proj,
        key_proj,
        value_proj,
        gain_query,
        gain_key,
        out_proj,
        gain_attention,
        gain_feed,
        gate_proj,
        up_proj,
        down_proj,
        gain_feed_out,
    ) = shards
    return (
        lax.all_gather(gain_input, ("fsdp", "ctx"), axis=0, tiled=True),
        lax.all_gather(query_proj, ("fsdp", "ctx"), axis=0, tiled=True),
        lax.all_gather(key_proj, ("fsdp", "ctx"), axis=0, tiled=True),
        lax.all_gather(value_proj, ("fsdp", "ctx"), axis=0, tiled=True),
        lax.all_gather(gain_query, ("fsdp", "ctx"), axis=0, tiled=True),
        lax.all_gather(gain_key, ("fsdp", "ctx"), axis=0, tiled=True),
        lax.all_gather(out_proj, ("fsdp", "ctx"), axis=1, tiled=True),
        lax.all_gather(gain_attention, ("fsdp", "ctx"), axis=0, tiled=True),
        lax.all_gather(gain_feed, ("fsdp", "ctx"), axis=0, tiled=True),
        lax.all_gather(gate_proj, ("fsdp", "ctx"), axis=0, tiled=True),
        lax.all_gather(up_proj, ("fsdp", "ctx"), axis=0, tiled=True),
        lax.all_gather(down_proj, ("fsdp", "ctx"), axis=1, tiled=True),
        lax.all_gather(gain_feed_out, ("fsdp", "ctx"), axis=0, tiled=True),
    )


def gather_again(shards):
    (
        gain_input,
        query_proj,
        key_proj,
        value_proj,
        gain_query,
        gain_key,
        out_proj,
        gain_attention,
        gain_feed,
        gate_proj,
        up_proj,
        down_proj,
        gain_feed_out,
    ) = shards
    return (
        lax.all_gather(gain_input, ("fsdp", "ctx"), axis=0, tiled=True),
        lax.all_gather(query_proj, ("fsdp", "ctx"), axis=0, tiled=True),
        lax.all_gather(key_proj, ("fsdp", "ctx"), axis=0, tiled=True),
        lax.all_gather(value_proj, ("fsdp", "ctx"), axis=0, tiled=True),
        lax.all_gather(gain_query, ("fsdp", "ctx"), axis=0, tiled=True),
        lax.all_gather(gain_key, ("fsdp", "ctx"), axis=0, tiled=True),
        lax.all_gather(out_proj, ("fsdp", "ctx"), axis=1, tiled=True),
        lax.all_gather(gain_attention, ("fsdp", "ctx"), axis=0, tiled=True),
        lax.all_gather(gain_feed, ("fsdp", "ctx"), axis=0, tiled=True),
        lax.all_gather(gate_proj, ("fsdp", "ctx"), axis=0, tiled=True),
        lax.all_gather(up_proj, ("fsdp", "ctx"), axis=0, tiled=True),
        lax.all_gather(down_proj, ("fsdp", "ctx"), axis=1, tiled=True),
        lax.all_gather(gain_feed_out, ("fsdp", "ctx"), axis=0, tiled=True),
    )


def reduce_grads(grads):
    (
        grad_gin,
        grad_query,
        grad_key,
        grad_value,
        grad_gquery,
        grad_gkey,
        grad_out,
        grad_gatt,
        grad_gfeed,
        grad_gate,
        grad_up,
        grad_down,
        grad_gfout,
    ) = grads
    return (
        lax.psum_scatter(grad_gin, ("fsdp", "ctx"), scatter_dimension=0, tiled=True),
        lax.psum_scatter(grad_query, ("fsdp", "ctx"), scatter_dimension=0, tiled=True),
        lax.psum_scatter(grad_key, ("fsdp", "ctx"), scatter_dimension=0, tiled=True),
        lax.psum_scatter(grad_value, ("fsdp", "ctx"), scatter_dimension=0, tiled=True),
        lax.psum_scatter(grad_gquery, ("fsdp", "ctx"), scatter_dimension=0, tiled=True),
        lax.psum_scatter(grad_gkey, ("fsdp", "ctx"), scatter_dimension=0, tiled=True),
        lax.psum_scatter(grad_out, ("fsdp", "ctx"), scatter_dimension=1, tiled=True),
        lax.psum_scatter(grad_gatt, ("fsdp", "ctx"), scatter_dimension=0, tiled=True),
        lax.psum_scatter(grad_gfeed, ("fsdp", "ctx"), scatter_dimension=0, tiled=True),
        lax.psum_scatter(grad_gate, ("fsdp", "ctx"), scatter_dimension=0, tiled=True),
        lax.psum_scatter(grad_up, ("fsdp", "ctx"), scatter_dimension=0, tiled=True),
        lax.psum_scatter(grad_down, ("fsdp", "ctx"), scatter_dimension=1, tiled=True),
        lax.psum_scatter(grad_gfout, ("fsdp", "ctx"), scatter_dimension=0, tiled=True),
    )


def window_pairs(key_rot, value_low, ctx_place, block_len):
    all_keys, all_values = (
        lax.all_gather(key_rot, "ctx", axis=1, tiled=True),
        lax.all_gather(value_low, "ctx", axis=1, tiled=True),
    )
    padding = jnp.zeros((key_rot.shape[0], WINDOW, key_rot.shape[2]), key_rot.dtype)
    keys_seen = lax.dynamic_slice_in_dim(
        jnp.concatenate([padding, all_keys], axis=1), ctx_place * block_len, WINDOW + block_len, 1
    )
    values_seen = lax.dynamic_slice_in_dim(
        jnp.concatenate([padding, all_values], axis=1), ctx_place * block_len, WINDOW + block_len, 1
    )
    return (keys_seen, values_seen)


def return_pairs(d_keys_seen, d_values_seen, ctx_place, block_len):
    local_seqs, span_len, depth = d_keys_seen.shape
    full_len = WINDOW + block_len * lax.axis_size("ctx")
    empty = jnp.zeros((local_seqs, full_len, depth), jnp.float32)
    full_keys = lax.dynamic_update_slice_in_dim(empty, d_keys_seen, ctx_place * block_len, 1)[
        :, WINDOW:
    ]
    full_values = lax.dynamic_update_slice_in_dim(empty, d_values_seen, ctx_place * block_len, 1)[
        :, WINDOW:
    ]
    return (
        lax.psum_scatter(
            full_keys.astype(jnp.bfloat16), "ctx", scatter_dimension=1, tiled=True
        ).astype(jnp.float32),
        lax.psum_scatter(
            full_values.astype(jnp.bfloat16), "ctx", scatter_dimension=1, tiled=True
        ).astype(jnp.float32),
    )


def masked_scores(query_rot, keys_seen, allowed):
    raw_scores = jnp.einsum(
        "sche,ske->shck", query_rot, keys_seen, preferred_element_type=jnp.float32
    )
    return jnp.where(allowed[:, None], raw_scores * SCORE_SCALE, MASKED)


def micro_step(gathered, shards, layer_in, starts, layer_cot, ctx_place, block_len):
    f32 = jnp.float32
    bf16 = jnp.bfloat16
    tp_place = lax.axis_index("tp")
    half_len = block_len // lax.axis_size("tp")
    x_in = layer_in.astype(f32)
    x_half = lax.dynamic_slice_in_dim(x_in, tp_place * half_len, half_len, 1)
    dy_half = lax.dynamic_slice_in_dim(layer_cot, tp_place * half_len, half_len, 1).astype(f32)
    gain_input = gathered[0].astype(f32)
    query_proj = gathered[1]
    key_proj = gathered[2]
    value_proj = gathered[3]
    gain_query = gathered[4].astype(f32)
    gain_key = gathered[5].astype(f32)
    out_proj = gathered[6]
    gain_attention = gathered[7].astype(f32)
    gain_feed = gathered[8].astype(f32)
    gate_proj = gathered[9]
    up_proj = gathered[10]
    down_proj = gathered[11]
    gain_feed_out = gathered[12].astype(f32)
    local_seqs = x_in.shape[0]
    token_place = ctx_place * block_len + jnp.arange(block_len, dtype=jnp.int32)
    offsets = (token_place[None, :] - starts).astype(f32)
    cosines, sines = rotations(offsets, HEAD_DIM)
    cos_heads = cosines[:, :, None, :]
    sin_heads = sines[:, :, None, :]
    hidden_one = normed(x_in, gain_input).astype(bf16)
    query_flat = jnp.einsum("scd,de->sce", hidden_one, query_proj, preferred_element_type=f32)
    local_heads = query_flat.shape[-1] // HEAD_DIM
    query_full = query_flat.reshape(local_seqs, block_len, local_heads, HEAD_DIM)
    key_full = jnp.einsum("scd,de->sce", hidden_one, key_proj, preferred_element_type=f32)
    value_full = jnp.einsum("scd,de->sce", hidden_one, value_proj, preferred_element_type=f32)
    query_rot = rope_normed(query_full, gain_query, cos_heads, sin_heads).astype(bf16)
    key_rot = rope_normed(key_full, gain_key, cosines, sines).astype(bf16)
    value_low = value_full.astype(bf16)
    keys_seen, values_seen = window_pairs(key_rot, value_low, ctx_place, block_len)
    key_place = ctx_place * block_len - WINDOW + jnp.arange(WINDOW + block_len, dtype=jnp.int32)
    allowed = (
        (key_place[None, None, :] <= token_place[None, :, None])
        & (token_place[None, :, None] - key_place[None, None, :] < WINDOW)
        & (key_place[None, None, :] >= starts[:, :, None])
    )
    scores = masked_scores(query_rot, keys_seen, allowed)
    row_max = jnp.max(scores, axis=-1, keepdims=True)
    lifted = jnp.exp(scores - row_max)
    row_total = jnp.sum(lifted, axis=-1, keepdims=True)
    log_total = row_max + jnp.log(row_total)
    prob_low = (lifted / row_total).astype(bf16)
    mixed_heads = jnp.einsum("shck,ske->sche", prob_low, values_seen, preferred_element_type=f32)
    mixed = mixed_heads.astype(bf16).reshape(local_seqs, block_len, local_heads * HEAD_DIM)
    attention = lax.psum_scatter(
        jnp.einsum("sce,ed->scd", mixed, out_proj, preferred_element_type=f32).astype(jnp.bfloat16),
        "tp",
        scatter_dimension=1,
        tiled=True,
    ).astype(jnp.float32)
    middle = x_half + normed(attention, gain_attention)
    hidden_two = lax.all_gather(normed(middle, gain_feed).astype(bf16), "tp", axis=1, tiled=True)
    gate_act = jnp.einsum("scd,du->scu", hidden_two, gate_proj, preferred_element_type=f32)
    up_act = jnp.einsum("scd,du->scu", hidden_two, up_proj, preferred_element_type=f32)
    hidden_units = feed_inner(gate_act, up_act).astype(bf16)
    feed = lax.psum_scatter(
        jnp.einsum("scu,ud->scd", hidden_units, down_proj, preferred_element_type=f32).astype(
            jnp.bfloat16
        ),
        "tp",
        scatter_dimension=1,
        tiled=True,
    ).astype(jnp.float32)
    layer_out = (middle + normed(feed, gain_feed_out)).astype(bf16)
    back_weights = gather_again(shards)
    query_back = back_weights[1]
    key_back = back_weights[2]
    value_back = back_weights[3]
    out_back = back_weights[6]
    gate_back = back_weights[9]
    up_back = back_weights[10]
    down_back = back_weights[11]
    d_feed, d_gain_feed_out = jax.vjp(normed, feed, gain_feed_out)[1](dy_half)
    d_feed_low = lax.all_gather(d_feed.astype(bf16), "tp", axis=1, tiled=True)
    grad_down = jnp.einsum("scu,scd->ud", hidden_units, d_feed_low, preferred_element_type=f32)
    d_hidden = jnp.einsum("scd,ud->scu", d_feed_low, down_back, preferred_element_type=f32)
    d_gate, d_up = jax.vjp(feed_inner, gate_act, up_act)[1](d_hidden)
    d_gate_low = d_gate.astype(bf16)
    d_up_low = d_up.astype(bf16)
    grad_gate = jnp.einsum("scd,scu->du", hidden_two, d_gate_low, preferred_element_type=f32)
    grad_up = jnp.einsum("scd,scu->du", hidden_two, d_up_low, preferred_element_type=f32)
    part_two = jnp.einsum(
        "scu,du->scd", d_gate_low, gate_back, preferred_element_type=f32
    ) + jnp.einsum("scu,du->scd", d_up_low, up_back, preferred_element_type=f32)
    d_hidden_two = lax.psum_scatter(
        part_two.astype(jnp.bfloat16), "tp", scatter_dimension=1, tiled=True
    ).astype(jnp.float32)
    d_mid_norm, d_gain_feed = jax.vjp(normed, middle, gain_feed)[1](d_hidden_two)
    d_middle = dy_half + d_mid_norm
    d_attention, d_gain_attention = jax.vjp(normed, attention, gain_attention)[1](d_middle)
    d_att_low = lax.all_gather(d_attention.astype(bf16), "tp", axis=1, tiled=True)
    grad_out = jnp.einsum("sce,scd->ed", mixed, d_att_low, preferred_element_type=f32)
    d_mixed = jnp.einsum("scd,ed->sce", d_att_low, out_back, preferred_element_type=f32).astype(
        bf16
    )
    d_mixed = d_mixed.reshape(local_seqs, block_len, local_heads, HEAD_DIM)
    scores_again = masked_scores(query_rot, keys_seen, allowed)
    prob_again = jnp.exp(scores_again - log_total)
    d_prob = jnp.einsum("sche,ske->shck", d_mixed, values_seen, preferred_element_type=f32)
    row_delta = jnp.sum(prob_again * d_prob, axis=-1, keepdims=True)
    d_raw = (prob_again * (d_prob - row_delta) * SCORE_SCALE).astype(bf16)
    d_query_rot = jnp.einsum("shck,ske->sche", d_raw, keys_seen, preferred_element_type=f32)
    d_keys_seen = jnp.einsum("shck,sche->ske", d_raw, query_rot, preferred_element_type=f32)
    d_values_seen = jnp.einsum("shck,sche->ske", prob_low, d_mixed, preferred_element_type=f32)
    back_keys, back_values = return_pairs(d_keys_seen, d_values_seen, ctx_place, block_len)

    def rotate_query(values, gain):
        return rope_normed(values, gain, cos_heads, sin_heads)

    def rotate_key(values, gain):
        return rope_normed(values, gain, cosines, sines)

    d_query, d_gain_query = jax.vjp(rotate_query, query_full, gain_query)[1](d_query_rot)
    d_query_low = d_query.astype(bf16).reshape(local_seqs, block_len, local_heads * HEAD_DIM)
    grad_query = jnp.einsum("scd,sce->de", hidden_one, d_query_low, preferred_element_type=f32)
    part_one = jnp.einsum("sce,de->scd", d_query_low, query_back, preferred_element_type=f32)
    d_part, key_sum, value_sum, gain_query_sum, gain_fout_sum, gain_feed_sum, gain_att_sum = (
        lax.psum(part_one.astype(jnp.bfloat16), "tp").astype(jnp.float32),
        lax.psum(back_keys.astype(jnp.bfloat16), "tp").astype(jnp.float32),
        lax.psum(back_values.astype(jnp.bfloat16), "tp").astype(jnp.float32),
        lax.psum(d_gain_query.astype(jnp.bfloat16), "tp").astype(jnp.float32),
        lax.psum(d_gain_feed_out.astype(jnp.bfloat16), "tp").astype(jnp.float32),
        lax.psum(d_gain_feed.astype(jnp.bfloat16), "tp").astype(jnp.float32),
        lax.psum(d_gain_attention.astype(jnp.bfloat16), "tp").astype(jnp.float32),
    )
    d_key, d_gain_key = jax.vjp(rotate_key, key_full, gain_key)[1](key_sum)
    d_key_low = d_key.astype(bf16)
    d_value_low = value_sum.astype(bf16)
    grad_key = jnp.einsum("scd,sce->de", hidden_one, d_key_low, preferred_element_type=f32)
    grad_value = jnp.einsum("scd,sce->de", hidden_one, d_value_low, preferred_element_type=f32)
    d_hidden_one = (
        d_part
        + jnp.einsum("sce,de->scd", d_key_low, key_back, preferred_element_type=f32)
        + jnp.einsum("sce,de->scd", d_value_low, value_back, preferred_element_type=f32)
    )
    d_input_norm, d_gain_input = jax.vjp(normed, x_in, gain_input)[1](d_hidden_one)
    input_grad = d_middle + lax.dynamic_slice_in_dim(d_input_norm, tp_place * half_len, half_len, 1)
    grads = (
        d_gain_input,
        grad_query,
        grad_key,
        grad_value,
        gain_query_sum,
        d_gain_key,
        grad_out,
        gain_att_sum,
        gain_feed_sum,
        grad_gate,
        grad_up,
        grad_down,
        gain_fout_sum,
    )
    return (layer_out, input_grad, grads)


def local(
    tokens,
    segments,
    cotangent,
    norm_input,
    query_weight,
    key_weight,
    value_weight,
    norm_query,
    norm_key,
    out_weight,
    norm_attention,
    norm_feed,
    gate_weight,
    up_weight,
    down_weight,
    norm_feed_out,
):
    shards = (
        norm_input,
        query_weight,
        key_weight,
        value_weight,
        norm_query,
        norm_key,
        out_weight,
        norm_attention,
        norm_feed,
        gate_weight,
        up_weight,
        down_weight,
        norm_feed_out,
    )
    micro_count = tokens.shape[0]
    block_len = tokens.shape[2]
    ctx_place = lax.axis_index("ctx")
    starts_all = doc_starts(segments, ctx_place * block_len)
    outputs = []
    input_grads = []
    summed = None
    for micro_index in range(micro_count):
        gathered = gather_first(shards)
        layer_out, input_grad, grads = micro_step(
            gathered,
            shards,
            tokens[micro_index],
            starts_all[micro_index],
            cotangent[micro_index],
            ctx_place,
            block_len,
        )
        grads = reduce_grads(grads)
        summed = (
            grads if summed is None else tuple((left + right for left, right in zip(summed, grads)))
        )
        outputs.append(layer_out)
        input_grads.append(input_grad)
    return (jnp.stack(outputs), jnp.stack(input_grads)) + tuple(summed)


def solution(mesh):
    return jax.shard_map(
        local,
        mesh=mesh,
        in_specs=(
            P(None, "fsdp", "ctx", None),
            P(None, "fsdp", "ctx"),
            P(None, "fsdp", "ctx", None),
            P(("fsdp", "ctx")),
            P(("fsdp", "ctx"), "tp"),
            P(("fsdp", "ctx"), None),
            P(("fsdp", "ctx"), None),
            P(("fsdp", "ctx")),
            P(("fsdp", "ctx")),
            P("tp", ("fsdp", "ctx")),
            P(("fsdp", "ctx")),
            P(("fsdp", "ctx")),
            P(("fsdp", "ctx"), "tp"),
            P(("fsdp", "ctx"), "tp"),
            P("tp", ("fsdp", "ctx")),
            P(("fsdp", "ctx")),
        ),
        out_specs=(
            P(None, "fsdp", ("ctx", "tp"), None),
            P(None, "fsdp", ("ctx", "tp"), None),
            P(("fsdp", "ctx")),
            P(("fsdp", "ctx"), "tp"),
            P(("fsdp", "ctx"), None),
            P(("fsdp", "ctx"), None),
            P(("fsdp", "ctx")),
            P(("fsdp", "ctx")),
            P("tp", ("fsdp", "ctx")),
            P(("fsdp", "ctx")),
            P(("fsdp", "ctx")),
            P(("fsdp", "ctx"), "tp"),
            P(("fsdp", "ctx"), "tp"),
            P("tp", ("fsdp", "ctx")),
            P(("fsdp", "ctx")),
        ),
        check_vma=False,
    )
```

profile of v0, /device:TPU:0, one launch (start us, length us, event | category | flops | bytes accessed | tf_op | source)
XLA Modules:
  0.0 2164.4 jit_solution(48124915834145830)
XLA Ops:
  18.3 79.1 %all-reduce.34 = (bf16[1152]{0:T(1024)(128)(2,1)S(1)}, bf16[256]{0:T(256)(128)(2,1)S(1)}, bf16[256]{0:T(256)(128)(2,1)S(1)}, bf16[1152]{0:T(1024)(128)(2,1)}, bf...) all-reduce(bf16[1152]{0:T(1024)(128)(2,1)S(1)} %dynamic-update-slic, ...), channel_id=1, replica_groups=mesh['fsdp'=4,'ctx'=4,'tp'=2] {'fsdp','ctx'}, use_global_device_ids=true, to_apply=%add.13 | all-reduce | flops 5120 | bytes 20480
  99.0 45.1 %all_gather.117 = bf16[1152,256]{1,0:T(8,128)(2,1)S(1)} all-gather(bf16[72,256]{1,0:T(8,128)(2,1)} %param.23), channel_id=1, replica_groups=mesh['fsdp'=4,'ctx'=4,'tp'=2] {'fsdp','ctx'}, dimensions={0}, use_global_device_ids=true | all-gather | bytes 626688 | tf_op jit(solution)/shard_map/all_gather | solution.py:124
  145.2 41.5 %all_gather.55 = bf16[1152,256]{1,0:T(8,128)(2,1)S(1)} all-gather(bf16[72,256]{1,0:T(8,128)(2,1)S(1)} %copy-done.89), channel_id=1, replica_groups=mesh['fsdp'=4,'ctx'=4,'tp'=2] {'fsdp','ctx'}, dimensions={0}, use_global_device_ids=true | all-gather | bytes 626688 | tf_op jit(solution)/shard_map/all_gather | solution.py:125
  192.9 5.6 all-reduce.32
  202.2 17.6 all_gather.131
  221.0 15.4 all-gather.4
  236.4 15.4 all_gather.119
  251.8 15.9 all-gather
  267.7 2.7 fusion.235
  279.6 2.8 fusion.27
  296.3 5.9 reduce-scatter.24.cloned.1.call-done
  311.7 103.2 %all-gather.16.cloned.1.call-done = bf16[1152,3456]{1,0:T(8,128)(2,1)} async-done(((bf16[72,3456]{1,0:T(8,128)(2,1)}), bf16[1152,3456]{1,0:T(8,128)(2,1)}) %all-gather.16.cloned.1.call-update) | async-done | bytes 7962640 | tf_op jit(solution)/shard_map/all_gather | solution.py:131
  414.9 7.8 fusion.125
  422.8 102.0 %all-gather.18.cloned.1.call-done = bf16[1152,3456]{1,0:T(8,128)(2,1)} async-done(((bf16[72,3456]{1,0:T(8,128)(2,1)}), bf16[1152,3456]{1,0:T(8,128)(2,1)}) %all-gather.18.cloned.1.call-update) | async-done | bytes 7962640 | tf_op jit(solution)/shard_map/all_gather | solution.py:132
  524.7 9.4 multiply_convert_fusion.3
  534.1 100.5 %all-gather.20.cloned.1.call-done = bf16[3456,1152]{0,1:T(8,128)(2,1)} async-done(((bf16[3456,72]{0,1:T(8,128)(2,1)}), bf16[3456,1152]{0,1:T(8,128)(2,1)}) %all-gather.20.cloned.1.call-update) | async-done | bytes 7962640 | tf_op jit(solution)/shard_map/all_gather | solution.py:133
  634.7 7.2 fusion.24
  642.2 6.1 fusion.117
  648.4 4.5 multiply_convert_fusion.2
  654.1 3.4 fusion.25
  668.6 2.8 all_gather.135
  671.4 9.2 multiply_convert_fusion
  683.2 3.4 fusion.30
  687.9 8.1 reduce-scatter.38.cloned.1.call-done
  698.7 3.8 fusion.72
  704.7 8.7 multiply_convert_fusion.1
  716.1 3.4 fusion.31
  722.2 6.7 reduce-scatter.32.cloned.1.call-done
  731.6 3.3 fusion.76
  745.7 3.9 all_gather.134
  771.8 15.6 reduce-scatter.42.cloned.1.call-done
  787.5 22.1 %reduce-scatter.34.cloned.1.call-done = bf16[1,256,256]{1,2,0:T(8,128)(2,1)} async-done(((bf16[1,1024,256]{1,2,0:T(8,128)(2,1)}), bf16[1,256,256]{1,2,0:T(8,128)(2,1)}) %reduce-scatter.34.cloned.1.call-update) | async-done | bytes 131088 | tf_op jit(solution)/shard_map/reduce_scatter | solution.py:230
  809.6 22.7 %reduce-scatter.36.cloned.1.call-done = bf16[1,256,256]{1,2,0:T(8,128)(2,1)} async-done(((bf16[1,1024,256]{1,2,0:T(8,128)(2,1)}), bf16[1,256,256]{1,2,0:T(8,128)(2,1)}) %reduce-scatter.36.cloned.1.call-update) | async-done | bytes 131088 | tf_op jit(solution)/shard_map/reduce_scatter | solution.py:233
  838.9 16.4 all-reduce.39.cloned.1.call-done
  863.4 4.0 fusion.121
  867.4 7.8 convolution_add_fusion.2
  875.3 4.0 fusion.119
  879.3 7.9 convolution_add_fusion.1
  887.5 4.1 fusion.109
  891.6 8.1 convolution_add_fusion
  902.5 3.5 all-reduce.35
  912.4 77.7 %all-reduce.33 = (f32[1152]{0:T(1024)S(1)}, f32[256]{0:T(256)S(1)}, f32[256]{0:T(256)S(1)}, f32[1152]{0:T(1024)S(1)}, f32[1152]{0:T(1024)S(1)}, /*index=5*/f32[1152]{0:T(1024)S(1)}) all-reduce(f32[1152]{0:T(1024)S(1)} %add.538, f32[256]{0:T(256)S(1)} %convert_add_fusion.5, ...), channel_id=31, replica_groups=mesh['fsdp'=4,'ctx'=4,'tp'=2] {'fsdp','ctx'}, use_global_device_ids=true, to_apply=%region_51.52.clone | all-reduce | flops 5120 | bytes 40960
  997.4 125.0 %reduce-scatter.50.cloned.1.call-done = f32[512,72]{0,1:T(8,128)} async-done(((f32[512,1152]{0,1:T(8,128)}), f32[512,72]{0,1:T(8,128)}) %reduce-scatter.50.cloned.1.call-update) | async-done | bytes 147472 | tf_op jit(solution)/shard_map/reduce_scatter | solution.py:194
  1122.5 128.9 %reduce-scatter.46.cloned.1.call-done = f32[72,256]{1,0:T(8,128)} async-done(((f32[1152,256]{1,0:T(8,128)}), f32[72,256]{1,0:T(8,128)}) %reduce-scatter.46.cloned.1.call-update) | async-done | bytes 73744 | tf_op jit(solution)/shard_map/reduce_scatter | solution.py:190
  1251.3 128.6 %reduce-scatter.48.cloned.1.call-done = f32[72,256]{1,0:T(8,128)} async-done(((f32[1152,256]{1,0:T(8,128)}), f32[72,256]{1,0:T(8,128)}) %reduce-scatter.48.cloned.1.call-update) | async-done | bytes 73744 | tf_op jit(solution)/shard_map/reduce_scatter | solution.py:191
  1380.0 258.7 %reduce-scatter.52.cloned.1.call-done = f32[72,3456]{1,0:T(8,128)} async-done(((f32[1152,3456]{1,0:T(8,128)}), f32[72,3456]{1,0:T(8,128)}) %reduce-scatter.52.cloned.1.call-update) | async-done | bytes 995344
  1638.7 259.4 %reduce-scatter.54.cloned.1.call-done = f32[72,3456]{1,0:T(8,128)} async-done(((f32[1152,3456]{1,0:T(8,128)}), f32[72,3456]{1,0:T(8,128)}) %reduce-scatter.54.cloned.1.call-update) | async-done | bytes 995344
  1898.1 259.3 %reduce-scatter.56.cloned.1.call-done = f32[3456,72]{0,1:T(8,128)} async-done(((f32[3456,1152]{0,1:T(8,128)}), f32[3456,72]{0,1:T(8,128)}) %reduce-scatter.56.cloned.1.call-update) | async-done | bytes 995344
  (584 shorter events, 146.2 us)
Async XLA Ops:
  7.2 137.0 %copy-start = (bf16[2,1,256,1152]{3,2,1,0:T(8,128)(2,1)S(1)}, bf16[2,1,256,1152]{3,2,1,0:T(8,128)(2,1)}, u32[]{:S(2)}) copy-start(bf16[2,1,256,1152]{3,2,1,0:T(8,128)(2,1)} %param.18) | copy-start | bytes 3538948
  7.2 260.5 %all-gather.12.cloned.1.call-start = ((), (), s32[]{:S(2)}) async-start(), calls=%async_computation.17 | async-start | bytes 1253376 | tf_op jit(solution)/shard_map/all_gather | solution.py:123
  7.9 271.7 %all-gather.14.cloned.1.call-start = ((), (), s32[]{:S(2)}) async-start(), calls=%async_computation.18 | async-start | bytes 1253376 | tf_op jit(solution)/shard_map/all_gather | solution.py:128
  8.7 286.0 %reduce-scatter.28.cloned.1.call-start = ((), (), s32[]{:S(2)}) async-start(), calls=%async_computation.24 | async-start | bytes 884736 | tf_op jit(solution)/shard_map/reduce_scatter | solution.py:297
  8.7 192.1 %copy-start.130 = (f32[128]{0:T(128)}, f32[128]{0:T(128)S(1)}, u32[]{:S(2)}) copy-start(f32[128]{0:T(128)S(1)} %multiply_power_fusion) | copy-start | bytes 1540
  99.0 46.2 %copy-start.122 = (f32[256]{0:T(256)}, f32[256]{0:T(256)S(1)}, u32[]{:S(2)}) copy-start(f32[256]{0:T(256)S(1)} %get-tuple-element.330) | copy-start | bytes 3076
  99.0 46.2 %copy-start.124 = (f32[256]{0:T(256)}, f32[256]{0:T(256)S(1)}, u32[]{:S(2)}) copy-start(f32[256]{0:T(256)S(1)} %get-tuple-element.331) | copy-start | bytes 3076
  99.0 168.7 %copy-start.95 = (f32[256]{0:T(256)}, f32[256]{0:T(256)S(1)}, u32[]{:S(2)}) copy-start(f32[256]{0:T(256)S(1)} %fusion.204) | copy-start | bytes 3076
  99.0 172.7 %copy-start.97 = (f32[256]{0:T(256)}, f32[256]{0:T(256)S(1)}, u32[]{:S(2)}) copy-start(f32[256]{0:T(256)S(1)} %fusion.206) | copy-start | bytes 3076
  144.7 54.4 %copy-start.138 = (f32[256]{0:T(256)}, f32[256]{0:T(256)S(1)}, u32[]{:S(2)}) copy-start(f32[256]{0:T(256)S(1)} %get-tuple-element.479) | copy-start | bytes 3076
  145.2 53.9 %copy-start.140 = (f32[256]{0:T(256)}, f32[256]{0:T(256)S(1)}, u32[]{:S(2)}) copy-start(f32[256]{0:T(256)S(1)} %get-tuple-element.481) | copy-start | bytes 3076
  145.2 55.5 %copy-start.37 = (f32[256,256]{0,1:T(8,128)}, f32[256,256]{0,1:T(8,128)S(1)}, u32[]{:S(2)}) copy-start(f32[256,256]{0,1:T(8,128)S(1)} %get-tuple-element.482) | copy-start | bytes 786436
  200.8 75.3 %copy-start.59 = (f32[256,128]{1,0:T(8,128)}, f32[256,128]{1,0:T(8,128)S(1)}, u32[]{:S(2)}) copy-start(f32[256,128]{1,0:T(8,128)S(1)} %get-tuple-element.475) | copy-start | bytes 393220
  200.8 75.3 %copy-start.61 = (f32[256,128]{1,0:T(8,128)}, f32[256,128]{1,0:T(8,128)S(1)}, u32[]{:S(2)}) copy-start(f32[256,128]{1,0:T(8,128)S(1)} %get-tuple-element.476) | copy-start | bytes 393220
  200.8 20.2 copy-start.88
  202.1 49.7 %copy-start.87 = (bf16[256,256]{1,0:T(8,128)(2,1)S(1)}, bf16[256,256]{1,0:T(8,128)(2,1)}, u32[]{:S(2)}) copy-start(bf16[256,256]{1,0:T(8,128)(2,1)} %convolution_convert_fusion.11) | copy-start | bytes 393220
  282.4 19.8 reduce-scatter.24.cloned.1.call-start
  289.0 125.9 %all-gather.16.cloned.1.call-start = ((), (), s32[]{:S(2)}) async-start(), calls=%async_computation.20 | async-start | bytes 8460288 | tf_op jit(solution)/shard_map/all_gather | solution.py:131
  289.6 235.1 %all-gather.18.cloned.1.call-start = ((), (), s32[]{:S(2)}) async-start(), calls=%async_computation.21 | async-start | bytes 8460288 | tf_op jit(solution)/shard_map/all_gather | solution.py:132
  290.2 344.5 %all-gather.20.cloned.1.call-start = ((), (), s32[]{:S(2)}) async-start(), calls=%async_computation.22 | async-start | bytes 8460288 | tf_op jit(solution)/shard_map/all_gather | solution.py:133
  290.9 370.3 %reduce-scatter.26.cloned.1.call-start = ((), (), s32[]{:S(2)}) async-start(), calls=%async_computation.23 | async-start | bytes 884736 | tf_op jit(solution)/shard_map/reduce_scatter | solution.py:308
  641.9 22.0 %reduce-scatter.30.cloned.1.call-start = ((), (), s32[]{:S(2)}) async-start(), calls=%async_computation.25 | async-start | bytes 884736 | tf_op jit(solution)/shard_map/reduce_scatter | solution.py:308
  657.5 38.4 %reduce-scatter.38.cloned.1.call-start = ((), (), s32[]{:S(2)}) async-start(), calls=%async_computation.29 | async-start | bytes 884736 | tf_op jit(solution)/shard_map/reduce_scatter | solution.py:337
  686.6 42.3 %reduce-scatter.32.cloned.1.call-start = ((), (), s32[]{:S(2)}) async-start(), calls=%async_computation.26 | async-start | bytes 884736 | tf_op jit(solution)/shard_map/reduce_scatter | solution.py:337
  719.5 52.3 %reduce-scatter.40.cloned.1.call-start = ((), (), s32[]{:S(2)}) async-start(), calls=%async_computation.30 | async-start | bytes 655360 | tf_op jit(solution)/shard_map/reduce_scatter | solution.py:230
  742.4 45.0 %reduce-scatter.42.cloned.1.call-start = ((), (), s32[]{:S(2)}) async-start(), calls=%async_computation.31 | async-start | bytes 655360 | tf_op jit(solution)/shard_map/reduce_scatter | solution.py:233
  749.6 60.0 %reduce-scatter.34.cloned.1.call-start = ((), (), s32[]{:S(2)}) async-start(), calls=%async_computation.27 | async-start | bytes 655360 | tf_op jit(solution)/shard_map/reduce_scatter | solution.py:230
  755.0 77.3 %reduce-scatter.36.cloned.1.call-start = ((), (), s32[]{:S(2)}) async-start(), calls=%async_computation.28 | async-start | bytes 655360 | tf_op jit(solution)/shard_map/reduce_scatter | solution.py:233
  760.3 95.1 %all-reduce.39.cloned.1.call-start = ((), (), s32[]{:S(2)}) async-start(), calls=%async_computation.39 | async-start | bytes 3407872 | tf_op jit(solution)/shard_map/psum | solution.py:371
  770.4 61.9 %copy-start.96 = (f32[256]{0:T(256)S(1)}, f32[256]{0:T(256)}, u32[]{:S(2)}) copy-start(f32[256]{0:T(256)} %copy-done.95) | copy-start | bytes 3076
  832.3 165.1 %reduce-scatter.44.cloned.1.call-start = ((), (), s32[]{:S(2)}) async-start(), calls=%async_computation.32 | async-start | bytes 2506752 | tf_op jit(solution)/shard_map/reduce_scatter | solution.py:189
  835.1 287.4 %reduce-scatter.50.cloned.1.call-start = ((), (), s32[]{:S(2)}) async-start(), calls=%async_computation.35 | async-start | bytes 2506752 | tf_op jit(solution)/shard_map/reduce_scatter | solution.py:194
  838.6 19.8 copy-start.38
  838.6 19.8 copy-start.114
  838.6 19.8 copy-start.116
  838.6 19.8 copy-start.127
  838.7 20.0 copy-start.139
  838.7 20.0 copy-start.141
  838.7 412.7 %reduce-scatter.46.cloned.1.call-start = ((), (), s32[]{:S(2)}) async-start(), calls=%async_computation.33 | async-start | bytes 1253376 | tf_op jit(solution)/shard_map/reduce_scatter | solution.py:190
  860.9 519.1 %reduce-scatter.48.cloned.1.call-start = ((), (), s32[]{:S(2)}) async-start(), calls=%async_computation.34 | async-start | bytes 1253376 | tf_op jit(solution)/shard_map/reduce_scatter | solution.py:191
  863.3 775.4 %reduce-scatter.52.cloned.1.call-start = ((), (), s32[]{:S(2)}) async-start(), calls=%async_computation.36 | async-start | bytes 16920576
  875.2 1022.8 %reduce-scatter.54.cloned.1.call-start = ((), (), s32[]{:S(2)}) async-start(), calls=%async_computation.37 | async-start | bytes 16920576
  887.2 1270.2 %reduce-scatter.56.cloned.1.call-start = ((), (), s32[]{:S(2)}) async-start(), calls=%async_computation.38 | async-start | bytes 16920576
  909.8 83.8 %copy-start.17 = (f32[1,128,1152]{2,1,0:T(8,128)S(1)}, f32[1,128,1152]{2,1,0:T(8,128)}, u32[]{:S(2)}) copy-start(f32[1,128,1152]{2,1,0:T(8,128)} %get-tuple-element.406) | copy-start | bytes 1769476
  909.8 83.8 %copy-start.147 = (f32[128]{0:T(128)S(1)}, f32[128]{0:T(128)}, u32[]{:S(2)}) copy-start(f32[128]{0:T(128)} %dynamic-slice.34) | copy-start | bytes 1540
  912.2 82.9 %copy-start.21 = (f32[1,128,1152]{2,1,0:T(8,128)S(1)}, f32[1,128,1152]{2,1,0:T(8,128)}, u32[]{:S(2)}) copy-start(f32[1,128,1152]{2,1,0:T(8,128)} %copy-done.20) | copy-start | bytes 1769476
  912.2 82.9 %copy-start.35 = (f32[1,256,1152]{2,1,0:T(8,128)S(1)}, f32[1,256,1152]{2,1,0:T(8,128)}, u32[]{:S(2)}) copy-start(f32[1,256,1152]{2,1,0:T(8,128)} %get-tuple-element.418) | copy-start | bytes 3538948
  912.2 82.9 %copy-start.146 = (f32[128]{0:T(128)S(1)}, f32[128]{0:T(128)}, u32[]{:S(2)}) copy-start(f32[128]{0:T(128)} %dynamic-slice.32) | copy-start | bytes 1540
  (141 other events, 512.9 us)
Sparse Core Ops, SparseCore 0:
  10.8 58.9 all-gather.11
  72.6 55.9 all-gather.13
  282.5 7.6 reduce-scatter.27
  292.9 9.1 reduce-scatter.23
  304.7 110.1 all-gather.15
  417.5 107.1 all-gather.17
  527.5 107.1 all-gather.19
  642.0 6.2 reduce-scatter.25
  657.7 6.2 reduce-scatter.29
  686.7 9.1 reduce-scatter.37
  719.7 9.1 reduce-scatter.31
  742.5 22.7 reduce-scatter.39
  767.6 19.7 reduce-scatter.41
  789.6 19.9 reduce-scatter.33
  812.3 19.9 reduce-scatter.35
  836.0 19.2 all-reduce.38
  861.5 128.8 reduce-scatter.43
  995.7 126.7 reduce-scatter.49
  1128.5 122.8 reduce-scatter.45
  1257.2 122.6 reduce-scatter.47
  1387.3 251.2 reduce-scatter.51
  1646.0 251.9 reduce-scatter.53
  1905.4 251.9 reduce-scatter.55
where the time goes:
time: 2170 us; the launch traced here: 2160 us
  waiting for transfers between devices  1570 us (72%)
  blocking collectives  333 us (15%)
  matrix products  145 us (7%)
  other arithmetic  59.6 us (3%)
  local copies, waits for them, and re-layouts  37.4 us (2%)
    unnamed x26, waiting for transfers between devices  781 us
    unnamed x3, blocking collectives  163 us
    reduce_scatter x1, waiting for transfers between devices, reduce_grads(): lax.psum_scatter(grad_key, ('fsdp', 'ctx'), scatter_dimension=0, tiled=True)  129 us
    reduce_scatter x1, waiting for transfers between devices, reduce_grads(): lax.psum_scatter(grad_value, ('fsdp', 'ctx'), scatter_dimension=0, tiled=...  129 us
    reduce_scatter x1, waiting for transfers between devices, reduce_grads(): lax.psum_scatter(grad_out, ('fsdp', 'ctx'), scatter_dimension=1, tiled=True)  125 us
    all_gather x1, waiting for transfers between devices, gather_first(): lax.all_gather(gate_proj, ('fsdp', 'ctx'), axis=0, tiled=True)  103 us
    all_gather x1, waiting for transfers between devices, gather_first(): lax.all_gather(up_proj, ('fsdp', 'ctx'), axis=0, tiled=True)  102 us
    all_gather x1, waiting for transfers between devices, gather_first(): lax.all_gather(down_proj, ('fsdp', 'ctx'), axis=1, tiled=True)  101 us
  transfers between devices with their start and end apart: 23, of which 17 were waited for; matrix products, arithmetic and copies ran while one was open for 8% of the time, Pallas kernels for 0%

commit v1 on v0

v1 whole, which is shorter than its diff:
```python
import jax
import jax.numpy as jnp
from jax import lax
from jax.sharding import PartitionSpec as P

HEAD_DIM = 256
WINDOW = 512

EPSILON = 1e-06
ROPE_BASE = 10000.0
SCORE_SCALE = 0.0625
MASKED = -1e30

F32 = jnp.float32
BF16 = jnp.bfloat16
GROUPS = ((0, 1),)


def dot(spec, left, right):
    return jnp.einsum(spec, left, right, preferred_element_type=F32)


def normed(values, gain):
    return values * lax.rsqrt(jnp.mean(values * values, axis=-1, keepdims=True) + EPSILON) * gain


def turned(values, cosines, sines):
    middle = values.shape[-1] // 2
    first_half = values[..., :middle]
    second_half = values[..., middle:]
    return jnp.concatenate(
        [first_half * cosines - second_half * sines, second_half * cosines + first_half * sines],
        axis=-1,
    )


def rotations(offsets, depth):
    middle = depth // 2
    inverse = ROPE_BASE ** (-2.0 * jnp.arange(middle, dtype=F32) / depth)
    angle_grid = offsets[..., None] * inverse
    return (jnp.cos(angle_grid), jnp.sin(angle_grid))


def rope_normed(values, gain, cosines, sines):
    return turned(normed(values, gain), cosines, sines)


def feed_inner(gate_act, up_act):
    return jax.nn.gelu(gate_act, approximate=True) * up_act


def swap(value):
    return lax.ppermute(value, "tp", [(0, 1), (1, 0)])


def cross(value, axis, step):
    if step == 0:
        return value
    return lax.ppermute(value, axis, [(i, i ^ step) for i in range(lax.axis_size(axis))])


def shift(value, step):
    count = lax.axis_size("ctx")
    pairs = [(i, i + step) for i in range(count) if 0 <= i + step < count]
    return lax.ppermute(value, "ctx", pairs)


def gather_axis(value, axis):
    count, mine = lax.axis_size(axis), lax.axis_index(axis)
    whole = jnp.zeros((count,) + value.shape, value.dtype)
    for step in range(count):
        whole = lax.dynamic_update_index_in_dim(whole, cross(value, axis, step), mine ^ step, 0)
    return whole


def scatter_axis(value, axis):
    count, mine = lax.axis_size(axis), lax.axis_index(axis)
    total = lax.dynamic_index_in_dim(value, mine, 0, keepdims=False).astype(F32)
    for step in range(1, count):
        piece = lax.dynamic_index_in_dim(value, mine ^ step, 0, keepdims=False)
        total = total + cross(piece.astype(BF16), axis, step).astype(F32)
    return total


def trade_axis(value, axis):
    count, mine = lax.axis_size(axis), lax.axis_index(axis)
    whole = value
    for step in range(1, count):
        piece = lax.dynamic_index_in_dim(value, mine ^ step, 0, keepdims=False)
        whole = lax.dynamic_update_index_in_dim(whole, cross(piece, axis, step), mine ^ step, 0)
    return whole


def gather_rows(value):
    return jnp.swapaxes(gather_axis(gather_axis(value, "ctx"), "fsdp"), 0, 0)


def scatter_rows(value):
    return scatter_axis(scatter_axis(value, "fsdp").astype(BF16), "ctx")


def spread(rows):
    mine = [cross(rows, "fsdp", step) for step in range(lax.axis_size("fsdp"))]
    return jnp.concatenate(mine + [swap(piece) for piece in mine], axis=0)


def collect(part):
    count = lax.axis_size("fsdp")
    half = part.shape[0] // 2
    own = part[:half].astype(F32) + swap(part[half:]).astype(F32)
    size = half // count
    total = own[:size]
    for step in range(1, count):
        piece = own[step * size : (step + 1) * size].astype(BF16)
        total = total + cross(piece, "fsdp", step).astype(F32)
    return total


def local(
    tokens,
    segments,
    cotangent,
    norm_input,
    query_weight,
    key_weight,
    value_weight,
    norm_query,
    norm_key,
    out_weight,
    norm_attention,
    norm_feed,
    gate_weight,
    up_weight,
    down_weight,
    norm_feed_out,
):
    micros, seqs, block_len, width = tokens.shape
    planes = lax.axis_size("fsdp")
    depths = lax.axis_size("ctx")
    ctx_place = lax.axis_index("ctx")
    tp_place = lax.axis_index("tp")
    first_core = tp_place == 0
    half_len = block_len // lax.axis_size("tp")
    back_blocks = -(-WINDOW // block_len)
    rows_in = norm_input.shape[0]
    heads_half = query_weight.shape[1] // HEAD_DIM
    q_cols = query_weight.shape[1]
    units = gate_weight.shape[1] // planes

    gains_packed = jnp.concatenate(
        [norm_input, norm_attention, norm_feed, norm_feed_out, norm_query, norm_key]
    )[None]
    small = norm_query.shape[0]
    gains_all = gather_rows(gains_packed).reshape(planes * depths, -1).astype(F32)
    cuts = [0, rows_in, 2 * rows_in, 3 * rows_in, 4 * rows_in, 4 * rows_in + small]
    ends = cuts[1:] + [4 * rows_in + 2 * small]
    gain_input, gain_attention, gain_feed, gain_feed_out, gain_query, gain_key = (
        gains_all[:, lo:hi].reshape(-1) for lo, hi in zip(cuts, ends)
    )

    kv_shard = jnp.where(first_core, key_weight, value_weight)
    kv_own = gather_rows(kv_shard).reshape(width, HEAD_DIM)
    q_own = gather_rows(query_weight).reshape(width, q_cols)
    out_own = gather_rows(out_weight.T).reshape(width, q_cols)
    kv_cat = jnp.concatenate([kv_own, swap(kv_own)], axis=1)
    q_cat = jnp.concatenate([q_own, swap(q_own)], axis=1)
    out_cat = jnp.concatenate([out_own, swap(out_own)], axis=1)

    def plane_weight(shard):
        parts = jnp.swapaxes(shard.reshape(rows_in, planes, units), 0, 1)
        traded = trade_axis(parts, "fsdp")
        return lax.all_gather(traded, "ctx", axis=1, tiled=True).reshape(width, units)

    gate_w = plane_weight(gate_weight)
    up_w = plane_weight(up_weight)
    down_w = plane_weight(down_weight.T)

    segments_all = lax.all_gather(segments, "ctx", axis=2, tiled=True)
    half_at = tp_place * half_len
    seg_half = lax.dynamic_slice_in_dim(segments, half_at, half_len, 2)
    starts = jnp.sum(
        (segments_all[:, :, None, :] < seg_half[:, :, :, None]).astype(jnp.int32), axis=-1
    )
    token_place = ctx_place * block_len + half_at + jnp.arange(half_len, dtype=jnp.int32)
    cosines, sines = rotations((token_place - starts).astype(F32), HEAD_DIM)
    within = jnp.arange(half_len, dtype=jnp.int32)
    key_place = jnp.concatenate(
        [
            (ctx_place - back) * block_len + side * half_len + within
            for side in (tp_place, 1 - tp_place)
            for back in range(back_blocks + 1)
        ]
    )

    x_halves = lax.dynamic_slice_in_dim(tokens, half_at, half_len, 2)
    dy_halves = lax.dynamic_slice_in_dim(cotangent, half_at, half_len, 2)

    saved = []
    outputs = []
    for group in GROUPS:
        lo, hi = group[0], group[-1] + 1
        batch = (hi - lo) * seqs

        def pick(value):
            return value[lo:hi].reshape((batch,) + value.shape[2:])

        x = pick(x_halves).astype(F32)
        cos, sin, begin = pick(cosines), pick(sines), pick(starts)
        cos_heads, sin_heads = cos[:, :, None, :], sin[:, :, None, :]
        h1 = normed(x, gain_input).astype(BF16)
        kv = dot("bld,de->ble", h1, kv_cat)
        kv_left, kv_right = kv[..., :HEAD_DIM], kv[..., HEAD_DIM:]
        key_full = jnp.where(first_core, kv_left, kv_right)
        value_full = jnp.where(first_core, kv_right, kv_left)
        key_rot = rope_normed(key_full, gain_key, cos, sin).astype(BF16)
        pair = jnp.concatenate([key_rot, value_full.astype(BF16)], axis=-1)
        mine = jnp.concatenate(
            [pair] + [shift(pair, back) for back in range(1, back_blocks + 1)], axis=1
        )
        seen = jnp.concatenate([mine, swap(mine)], axis=1)
        keys, values = seen[..., :HEAD_DIM], seen[..., HEAD_DIM:]
        query_full = dot("bld,de->ble", h1, q_cat).reshape(
            batch, half_len, 2 * heads_half, HEAD_DIM
        )
        query_rot = rope_normed(query_full, gain_query, cos_heads, sin_heads).astype(BF16)
        allowed = (
            (key_place[None, None, :] <= token_place[None, :, None])
            & (token_place[None, :, None] - key_place[None, None, :] < WINDOW)
            & (key_place[None, None, :] >= begin[:, :, None])
        )
        raw = dot("blhe,bke->bhlk", query_rot, keys)
        scores = jnp.where(allowed[:, None], raw * SCORE_SCALE, MASKED)
        row_max = jnp.max(scores, axis=-1, keepdims=True)
        lifted = jnp.exp(scores - row_max)
        prob = lifted / jnp.sum(lifted, axis=-1, keepdims=True)
        prob_low = prob.astype(BF16)
        mixed = dot("bhlk,bke->blhe", prob_low, values).astype(BF16)
        mixed = mixed.reshape(batch, half_len, 2 * q_cols)
        attention = dot("ble,de->bld", mixed, out_cat)
        middle = x + normed(attention, gain_attention)
        h2 = normed(middle, gain_feed).astype(BF16).reshape(batch * half_len, width)
        h2_all = spread(h2)
        gate_act = dot("td,du->tu", h2_all, gate_w)
        up_act = dot("td,du->tu", h2_all, up_w)
        hidden = feed_inner(gate_act, up_act).astype(BF16)
        feed = collect(dot("tu,du->td", hidden, down_w).astype(BF16))
        feed = feed.reshape(batch, half_len, width)
        layer_out = (middle + normed(feed, gain_feed_out)).astype(BF16)
        outputs.append(layer_out.reshape(hi - lo, seqs, half_len, width))
        saved.append(
            (x, cos, sin, h1, key_full, query_full, query_rot, keys, values, prob, prob_low)
            + (mixed, attention, middle, h2_all, gate_act, up_act, hidden, feed)
        )

    input_grads = []
    grads = None
    for group, kept in zip(GROUPS, saved):
        lo, hi = group[0], group[-1] + 1
        batch = (hi - lo) * seqs
        (x, cos, sin, h1, key_full, query_full, query_rot, keys, values, prob, prob_low) = kept[:11]
        (mixed, attention, middle, h2_all, gate_act, up_act, hidden, feed) = kept[11:]
        cos_heads, sin_heads = cos[:, :, None, :], sin[:, :, None, :]
        dy = dy_halves[lo:hi].reshape(batch, half_len, width).astype(F32)
        d_feed, d_gain_feed_out = jax.vjp(normed, feed, gain_feed_out)[1](dy)
        d_feed_all = spread(d_feed.astype(BF16).reshape(batch * half_len, width))
        grad_down = dot("td,tu->du", d_feed_all, hidden)
        d_hidden = dot("td,du->tu", d_feed_all, down_w)
        d_gate, d_up = jax.vjp(feed_inner, gate_act, up_act)[1](d_hidden)
        d_gate, d_up = d_gate.astype(BF16), d_up.astype(BF16)
        d_h2 = collect(
            (dot("tu,du->td", d_gate, gate_w) + dot("tu,du->td", d_up, up_w)).astype(BF16)
        ).reshape(batch, half_len, width)
        grad_gate = dot("td,tu->du", h2_all, d_gate)
        grad_up = dot("td,tu->du", h2_all, d_up)
        d_mid_norm, d_gain_feed = jax.vjp(normed, middle, gain_feed)[1](d_h2)
        d_middle = dy + d_mid_norm
        d_attention, d_gain_attention = jax.vjp(normed, attention, gain_attention)[1](d_middle)
        d_attention = d_attention.astype(BF16)
        grad_out = dot("bld,ble->de", d_attention, mixed)
        d_mixed = dot("bld,de->ble", d_attention, out_cat).astype(BF16)
        d_mixed = d_mixed.reshape(batch, half_len, 2 * heads_half, HEAD_DIM)
        d_prob = dot("blhe,bke->bhlk", d_mixed, values)
        row_delta = jnp.sum(prob * d_prob, axis=-1, keepdims=True)
        d_raw = (prob * (d_prob - row_delta) * SCORE_SCALE).astype(BF16)
        d_query_rot = dot("bhlk,bke->blhe", d_raw, keys)
        d_keys = dot("bhlk,blhe->bke", d_raw, query_rot)
        d_values = dot("bhlk,blhe->bke", prob_low, d_mixed)
        d_pair = jnp.concatenate([d_keys, d_values], axis=-1)
        side = (back_blocks + 1) * half_len
        d_mine = d_pair[:, :side] + swap(d_pair[:, side:].astype(BF16)).astype(F32)
        d_kv = d_mine[:, :half_len]
        for back in range(1, back_blocks + 1):
            piece = d_mine[:, back * half_len : (back + 1) * half_len].astype(BF16)
            d_kv = d_kv + shift(piece, -back).astype(F32)

        def rotate_query(value, gain):
            return rope_normed(value, gain, cos_heads, sin_heads)

        def rotate_key(value, gain):
            return rope_normed(value, gain, cos, sin)

        d_query, d_gain_query = jax.vjp(rotate_query, query_full, gain_query)[1](d_query_rot)
        d_query = d_query.astype(BF16).reshape(batch, half_len, 2 * q_cols)
        d_key, d_gain_key = jax.vjp(rotate_key, key_full, gain_key)[1](d_kv[..., :HEAD_DIM])
        d_key = d_key.astype(BF16)
        d_value = d_kv[..., HEAD_DIM:].astype(BF16)
        d_kv_low = jnp.concatenate(
            [jnp.where(first_core, d_key, d_value), jnp.where(first_core, d_value, d_key)], axis=-1
        )
        grad_query = dot("bld,ble->de", h1, d_query)
        grad_kv = dot("bld,ble->de", h1, d_kv_low)
        d_h1 = dot("ble,de->bld", d_query, q_cat) + dot("ble,de->bld", d_kv_low, kv_cat)
        d_input_norm, d_gain_input = jax.vjp(normed, x, gain_input)[1](d_h1)
        input_grads.append((d_middle + d_input_norm).reshape(hi - lo, seqs, half_len, width))
        gain_grads = (d_gain_input, d_gain_attention, d_gain_feed, d_gain_feed_out)
        gain_grads = gain_grads + (d_gain_query, d_gain_key)
        now = (grad_down, grad_gate, grad_up, grad_out, grad_query, grad_kv) + gain_grads
        grads = now if grads is None else tuple(a + b for a, b in zip(grads, now))

    grad_down, grad_gate, grad_up, grad_out, grad_query, grad_kv = grads[:6]
    gain_grads = grads[6:]

    def plane_grad(grad):
        shaped = jnp.swapaxes(grad.astype(BF16).reshape(planes, depths, rows_in, units), 0, 1)
        part = lax.psum_scatter(
            shaped.reshape(depths * planes, rows_in, units), "ctx", scatter_dimension=0, tiled=True
        )
        return jnp.swapaxes(trade_axis(part, "fsdp"), 0, 1).reshape(rows_in, planes * units)

    out_down = plane_grad(grad_down).astype(F32).T
    out_gate = plane_grad(grad_gate).astype(F32)
    out_up = plane_grad(grad_up).astype(F32)

    def core_grad(grad):
        half = grad.shape[1] // 2
        own = grad[:, :half] + swap(grad[:, half:].astype(BF16)).astype(F32)
        return scatter_rows(own.astype(BF16).reshape(planes, depths, rows_in, half))

    out_out = core_grad(grad_out).T
    out_query = core_grad(grad_query)
    out_kv = core_grad(grad_kv)
    kv_other = swap(out_kv)
    out_key = jnp.where(first_core, out_kv, kv_other)
    out_value = jnp.where(first_core, kv_other, out_kv)

    gains_sum = jnp.concatenate(
        [grad.reshape(planes, depths, 1, -1) for grad in gain_grads], axis=-1
    )
    gains_sum = gains_sum + swap(gains_sum)
    gains_out = scatter_axis(scatter_axis(gains_sum, "fsdp"), "ctx")[0]
    pieces = [gains_out[lo:hi] for lo, hi in zip(cuts, ends)]

    return (
        jnp.concatenate(outputs, axis=0),
        jnp.concatenate(input_grads, axis=0),
        pieces[0],
        out_query,
        out_key,
        out_value,
        pieces[4],
        pieces[5],
        out_out,
        pieces[1],
        pieces[2],
        out_gate,
        out_up,
        out_down,
        pieces[3],
    )


def solution(mesh):
    both = ("fsdp", "ctx")
    return jax.shard_map(
        local,
        mesh=mesh,
        in_specs=(
            P(None, "fsdp", "ctx", None),
            P(None, "fsdp", "ctx"),
            P(None, "fsdp", "ctx", None),
            P(both),
            P(both, "tp"),
            P(both, None),
            P(both, None),
            P(both),
            P(both),
            P("tp", both),
            P(both),
            P(both),
            P(both, "tp"),
            P(both, "tp"),
            P("tp", both),
            P(both),
        ),
        out_specs=(
            P(None, "fsdp", ("ctx", "tp"), None),
            P(None, "fsdp", ("ctx", "tp"), None),
            P(both),
            P(both, "tp"),
            P(both, None),
            P(both, None),
            P(both),
            P(both),
            P("tp", both),
            P(both),
            P(both),
            P(both, "tp"),
            P(both, "tp"),
            P("tp", both),
            P(both),
        ),
        check_vma=False,
    )
```

time: 2170 us -> 667 us (0.31)
  waiting for transfers between devices: 1570 us -> 179 us
  blocking collectives: 333 us -> 7.9 us
  local copies, waits for them, and re-layouts: 37.4 us -> 167 us
  starting transfers between devices: 1.78 us -> 117 us
  matrix products: 145 us -> 116 us
    unnamed x26 -> x6, waiting for transfers between devices: 781 us -> 0.1 us
    reduce_scatter x14 -> x3, waiting for transfers between devices: 464 us -> 18 us  [plane_grad(): lax.psum_scatter(shaped.reshape(depths * planes, rows_in, units), 'ctx',...]
    all_gather x5 -> x3, waiting for transfers between devices: 306 us -> 16.2 us  [plane_weight(): lax.all_gather(traded, 'ctx', axis=1, tiled=True).reshape(width, units)]
    unnamed x3 -> x0, blocking collectives: 163 us -> none
    all_gather x12 -> x1, blocking collectives: 167 us -> 7.9 us  [local(): segments_all = lax.all_gather(segments, 'ctx', axis=2, tiled=True)]
    ppermute x0 -> x102, waiting for transfers between devices: none -> 144 us  [the longest x78 117 us: cross(): lax.ppermute(value, axis, [(i, i ^ step) for i in range(lax.axis_size(axi...]
    ppermute x0 -> x102, starting transfers between devices: none -> 116 us  [the longest x78 103 us: cross(): lax.ppermute(value, axis, [(i, i ^ step) for i in range(lax.axis_size(axi...]
    dynamic_update_slice x0 -> x46, local copies, waits for them, and re-layouts: none -> 50.3 us  [the longest x15 33.3 us: trade_axis(): lax.dynamic_update_index_in_dim(whole, cross(piece, axis, step), mine ^ s...]
  transfers between devices with their start and end apart: 23 -> 108, of which waited for: 17 -> 32; matrix products, arithmetic and copies ran while one was open for 8% -> 40% of each run, Pallas kernels for 0% -> 0%
where the time goes in v1:
time: 667 us; the launch traced here: 657 us
  waiting for transfers between devices  179 us (27%)
  local copies, waits for them, and re-layouts  167 us (25%)
  starting transfers between devices  117 us (18%)
  matrix products  116 us (17%)
  other arithmetic  54.2 us (8%)
  between operations  16.5 us (2%)
  blocking collectives  7.9 us (1%)
    ppermute x78, waiting for transfers between devices, cross(): lax.ppermute(value, axis, [(i, i ^ step) for i in range(lax.axis_size(axi...  117 us
    dot_general x24, matrix products, dot(): return jnp.einsum(spec, left, right, preferred_element_type=F32)  116 us
    ppermute x78, starting transfers between devices, cross(): lax.ppermute(value, axis, [(i, i ^ step) for i in range(lax.axis_size(axi...  103 us
    dynamic_update_slice x15, local copies, waits for them, and re-layouts, trade_axis(): lax.dynamic_update_index_in_dim(whole, cross(piece, axis, step), mine ^ s...  33.3 us
    unnamed x267, local copies, waits for them, and re-layouts  31.9 us
    ppermute x4, waiting for transfers between devices, shift(): return lax.ppermute(value, 'ctx', pairs)  19.8 us
    reduce_scatter x3, waiting for transfers between devices, plane_grad(): lax.psum_scatter(shaped.reshape(depths * planes, rows_in, units), 'ctx',...  18 us
    dynamic_update_slice x31, local copies, waits for them, and re-layouts, gather_axis(): lax.dynamic_update_index_in_dim(whole, cross(value, axis, step), mine ^ s...  17 us
  transfers between devices with their start and end apart: 108, of which 32 were waited for; matrix products, arithmetic and copies ran while one was open for 40% of the time, Pallas kernels for 0%

profile of v1, /device:TPU:0, one launch (start us, length us, event | category | flops | bytes accessed | tf_op | source)
XLA Modules:
  0.0 657.1 jit_solution(1506110889447572648)
XLA Ops:
  7.2 4.1 concatenate.47
  20.0 3.5 collective-permute-start.7
  24.0 7.9 %all_gather.12 = s32[2,1,1024]{2,1,0:T(1,128)S(1)} all-gather(s32[2,1,256]{2,1,0:T(1,128)} %param.17), channel_id=1, replica_groups=mesh['fsdp'=4,'ctx'=4,'tp'=2] {'ctx'}, dimensions={2}, use_global_device_ids=true | all-gather | bytes 10240 | tf_op jit(solution)/shard_map/all_gather | solution.py:178
  53.4 3.9 collective-permute-done.5
  63.5 3.4 dynamic_update_slice.189
  66.8 3.4 dynamic_update_slice.190
  70.2 3.4 dynamic_update_slice.191
  77.3 4.0 collective-permute-start.18
  85.6 3.9 collective-permute-start.25
  104.9 3.3 dynamic_update_slice.192
  108.2 3.4 dynamic_update_slice.193
  111.6 5.0 dynamic_update_slice.194
  133.5 4.4 collective-permute-start.14
  142.0 8.1 %collective-permute-done.14 = bf16[2,128,512]{2,1,0:T(8,128)(2,1)S(1)} collective-permute-done((bf16[2,128,512]{2,1,0:T(8,128)(2,1)S(1)}, bf16[2,128,512]{2,1,0:T(8,128)(2,1)S(1)}, u32[]{:S(2)}, u32[]{:S(2)}) %collective-permute-start.14) | collective-permute-done | bytes 262176 | tf_op jit(solution)/shard_map/ppermute | solution.py:65
  150.1 11.0 %collective-permute-done.13 = bf16[2,128,512]{2,1,0:T(8,128)(2,1)S(1)} collective-permute-done((bf16[2,128,512]{2,1,0:T(8,128)(2,1)S(1)}, bf16[2,128,512]{2,1,0:T(8,128)(2,1)S(1)}, u32[]{:S(2)}, u32[]{:S(2)}) %collective-permute-start.13) | collective-permute-done | bytes 262176 | tf_op jit(solution)/shard_map/ppermute | solution.py:65
  187.5 11.3 %collective-permute-done.43 = bf16[72,864]{1,0:T(8,128)(2,1)S(1)} collective-permute-done((bf16[72,864]{1,0:T(8,128)(2,1)S(1)}, bf16[72,864]{1,0:T(8,128)(2,1)S(1)}, u32[]{:S(2)}, u32[]{:S(2)}) %collective-permute-start.43) | collective-permute-done | bytes 124448 | tf_op jit(solution)/shard_map/ppermute | solution.py:59
  199.2 3.5 collective-permute-done.45
  202.9 3.4 dynamic_update_slice.195
  206.3 3.4 dynamic_update_slice.196
  209.7 3.4 dynamic_update_slice.197
  219.6 10.4 %collective-permute-done.32 = bf16[256,1152]{1,0:T(8,128)(2,1)S(1)} collective-permute-done((bf16[256,1152]{1,0:T(8,128)(2,1)S(1)}, bf16[256,1152]{1,0:T(8,128)(2,1)S(1)}, u32[]{:S(2)}, u32[]{:S(2)}) %collective-permute-start.32) | collective-permute-done | bytes 589856 | tf_op jit(solution)/shard_map/ppermute | solution.py:59
  238.9 7.6 %fusion.166 = f32[2048,864]{0,1:T(8,128)S(1)} fusion(bf16[2048,1152]{1,0:T(8,128)(2,1)} %constant_dynamic-update-slice_fusion.1, bf16[1152,864]{1,0:T(8,128)(2,1)S(1)} %bitcast.508), kind=kOutput, calls=%fused_computation.395 | convolution fusion | flops 4076863488 | bytes 13787136 | tf_op jit(solution)/shard_map/td,du->tu/dot_general | solution.py:20
  249.5 11.1 %multiply_convert_fusion.1 = (bf16[2048,864]{0,1:T(8,128)(2,1)}, f32[2048,864]{0,1:T(8,128)}) fusion(f32[2048,864]{0,1:T(8,128)S(1)} %fusion.166, bf16[2048,1152]{1,0:T(8,128)(2,1)} %constant_dynamic-update-slice_fusion.1, bf16[1152,864]{1,0:T(8,128)(2,1)S(1)} %bitcast.510), kind=kOutput, calls=%fused_computation.14 | convolution fusion | flops 4094558208 | bytes 24403968 | tf_op jit(solution)/shard_map/td,du->tu/dot_general | solution.py:20
  260.5 16.1 %all-gather.8.cloned.1.call-done = bf16[4,288,864]{2,0,1:T(4,128)(2,1)} async-done(((bf16[4,72,864]{2,0,1:T(4,128)(2,1)}), bf16[4,288,864]{2,0,1:T(4,128)(2,1)}) %all-gather.8.cloned.1.call-update) | async-done | bytes 1990672 | tf_op jit(solution)/shard_map/all_gather | solution.py:172
  279.3 6.3 convolution_convert_fusion
  285.8 4.5 collective-permute-done.46
  299.2 12.5 %collective-permute-done.49 = bf16[256,1152]{1,0:T(8,128)(2,1)S(1)} collective-permute-done((bf16[256,1152]{1,0:T(8,128)(2,1)}, bf16[256,1152]{1,0:T(8,128)(2,1)S(1)}, u32[]{:S(2)}, u32[]{:S(2)}) %collective-permute-start.49) | collective-permute-done | bytes 589856 | tf_op jit(solution)/shard_map/ppermute | solution.py:59
  311.7 11.8 %collective-permute-done.48 = bf16[256,1152]{1,0:T(8,128)(2,1)S(1)} collective-permute-done((bf16[256,1152]{1,0:T(8,128)(2,1)}, bf16[256,1152]{1,0:T(8,128)(2,1)S(1)}, u32[]{:S(2)}, u32[]{:S(2)}) %collective-permute-start.48) | collective-permute-done | bytes 589856 | tf_op jit(solution)/shard_map/ppermute | solution.py:59
  331.2 12.7 %collective-permute-done.50 = bf16[256,1152]{1,0:T(8,128)(2,1)S(1)} collective-permute-done((bf16[256,1152]{1,0:T(8,128)(2,1)S(1)}, bf16[256,1152]{1,0:T(8,128)(2,1)S(1)}, u32[]{:S(2)}, u32[]{:S(2)}) %collective-permute-start.50) | collective-permute-done | bytes 589856 | tf_op jit(solution)/shard_map/ppermute | solution.py:59
  344.0 12.8 %collective-permute-done.51 = bf16[256,1152]{1,0:T(8,128)(2,1)S(1)} collective-permute-done((bf16[256,1152]{1,0:T(8,128)(2,1)S(1)}, bf16[256,1152]{1,0:T(8,128)(2,1)S(1)}, u32[]{:S(2)}, u32[]{:S(2)}) %collective-permute-start.51) | collective-permute-done | bytes 589856 | tf_op jit(solution)/shard_map/ppermute | solution.py:59
  359.7 16.1 %multiply_convert_fusion = (bf16[2048,864]{0,1:T(8,128)(2,1)}, bf16[2048,864]{0,1:T(8,128)(2,1)S(1)}) fusion(f32[2048,864]{0,1:T(8,128)} %copy-done.111, f32[2048,864]{0,1:T(8,128)} %get-tuple-element.207, bf16[2048,1152]{1,0:T(8,128)(2,1)S(1)} %constant_dynamic-update-slice_fusion.9, bf16[1152,864]{1,0:T(8,128)(2,1)S(1)} %bitcast.513), kind=kOutput, calls=%fused_computation.13 | convolution fusion | flops 4119330816 | bytes 27942912 | tf_op jit(solution)/shard_map/td,du->tu/dot_general | solution.py:20
  377.6 8.4 %convolution_convert_fusion.3 = bf16[1152,864]{0,1:T(8,128)(2,1)} fusion(bf16[2048,864]{0,1:T(8,128)(2,1)S(1)} %get-tuple-element.115, bf16[2048,1152]{1,0:T(8,128)(2,1)} %constant_dynamic-update-slice_fusion.1), kind=kOutput, calls=%fused_computation.22 | convolution fusion | flops 4077858816 | bytes 10248192 | tf_op jit(solution)/shard_map/td,tu->du/dot_general | solution.py:20
  385.9 4.1 copy.216
  393.3 8.4 %fusion.167 = f32[2048,1152]{1,0:T(8,128)S(1)} fusion(bf16[2048,864]{0,1:T(8,128)(2,1)} %copy-done.114, bf16[1152,864]{1,0:T(8,128)(2,1)} %bitcast.509), kind=kOutput, calls=%fused_computation.396 | convolution fusion | flops 4076863488 | bytes 14966784 | tf_op jit(solution)/shard_map/tu,du->td/dot_general | solution.py:20
  401.7 5.8 add_convert_fusion
  410.6 8.2 %convolution_convert_fusion.2 = bf16[1152,864]{0,1:T(8,128)(2,1)} fusion(bf16[2048,864]{0,1:T(8,128)(2,1)S(1)} %copy-done.115, bf16[2048,1152]{1,0:T(8,128)(2,1)} %constant_dynamic-update-slice_fusion.1), kind=kOutput, calls=%fused_computation.21 | convolution fusion | flops 4077858816 | bytes 10248192 | tf_op jit(solution)/shard_map/td,tu->du/dot_general | solution.py:20
  418.9 4.1 copy.219
  426.8 5.1 fusion.154
  436.3 8.4 %convolution_convert_fusion.1 = bf16[1152,864]{0,1:T(8,128)(2,1)} fusion(bf16[2048,864]{0,1:T(8,128)(2,1)S(1)} %copy-done.113, bf16[2048,1152]{1,0:T(8,128)(2,1)} %copy-done.79), kind=kOutput, calls=%fused_computation.20 | convolution fusion | flops 4077858816 | bytes 10248192 | tf_op jit(solution)/shard_map/td,tu->du/dot_general | solution.py:20
  444.7 4.1 copy.222
  451.9 10.3 %collective-permute-done.59 = bf16[256,1152]{1,0:T(8,128)(2,1)} collective-permute-done((bf16[256,1152]{1,0:T(8,128)(2,1)S(1)}, bf16[256,1152]{1,0:T(8,128)(2,1)}, u32[]{:S(2)}, u32[]{:S(2)}) %collective-permute-start.59) | collective-permute-done | bytes 589856 | tf_op jit(solution)/shard_map/ppermute | solution.py:59
  468.2 3.5 fusion.35
  473.8 3.3 fusion.61
  477.2 5.8 convolution_bitcast_fusion.4
  487.5 6.6 fusion.34
  516.2 18.0 %reduce-scatter.8.cloned.1.call-done = bf16[4,72,864]{2,1,0:T(8,128)(2,1)} async-done(((bf16[16,72,864]{2,1,0:T(8,128)(2,1)}), bf16[4,72,864]{2,1,0:T(8,128)(2,1)}) %reduce-scatter.8.cloned.1.call-update) | async-done | bytes 497680 | tf_op jit(solution)/shard_map/reduce_scatter | solution.py:325
  562.5 5.2 collective-permute-start.69
  597.9 8.6 %collective-permute-done.100 = bf16[72,864]{1,0:T(8,128)(2,1)S(1)} collective-permute-done((bf16[72,864]{1,0:T(8,128)(2,1)S(1)}, bf16[72,864]{1,0:T(8,128)(2,1)S(1)}, u32[]{:S(2)}, u32[]{:S(2)}) %collective-permute-start.100) | collective-permute-done | bytes 124448 | tf_op jit(solution)/shard_map/ppermute | solution.py:59
  (678 shorter events, 303.4 us)
Async XLA Ops:
  7.2 227.2 %all-gather.4.cloned.1.call-start = ((), (), s32[]{:S(2)}) async-start(), calls=%async_computation.3 | async-start | bytes 2580480 | tf_op jit(solution)/shard_map/all_gather | solution.py:172
  11.3 30.8 %collective-permute-start = (bf16[1,320]{1,0:T(2,128)(2,1)S(1)}, bf16[1,320]{1,0:T(2,128)(2,1)S(1)}, u32[]{:S(2)}, u32[]{:S(2)}) collective-permute-start(bf16[1,320]{1,0:T(2,128)(2,1)S(1)} %broadcast_in_dim.231), channel_id=1, source_target_pairs={{0,2},{2,0},{4,6},{6,4},{1,3},{3,1},{5,7},{7,5},{8,10},{10,8},{12,... | collective-permute-start | bytes 1928 | tf_op jit(solution)/shard_map/ppermute | solution.py:59
  14.4 29.5 %collective-permute-start.1 = (bf16[1,320]{1,0:T(2,128)(2,1)S(1)}, bf16[1,320]{1,0:T(2,128)(2,1)S(1)}, u32[]{:S(2)}, u32[]{:S(2)}) collective-permute-start(bf16[1,320]{1,0:T(2,128)(2,1)S(1)} %broadcast_in_dim.231), channel_id=1, source_target_pairs={{0,4},{2,6},{4,0},{6,2},{1,5},{3,7},{5,1},{7,3},{8,12},{10,14},{12... | collective-permute-start | bytes 1928 | tf_op jit(solution)/shard_map/ppermute | solution.py:59
  17.0 28.5 %collective-permute-start.2 = (bf16[1,320]{1,0:T(2,128)(2,1)S(1)}, bf16[1,320]{1,0:T(2,128)(2,1)S(1)}, u32[]{:S(2)}, u32[]{:S(2)}) collective-permute-start(bf16[1,320]{1,0:T(2,128)(2,1)S(1)} %broadcast_in_dim.231), channel_id=1, source_target_pairs={{0,6},{2,4},{4,2},{6,0},{1,7},{3,5},{5,3},{7,1},{8,14},{10,12},{12... | collective-permute-start | bytes 1928 | tf_op jit(solution)/shard_map/ppermute | solution.py:59
  19.1 58.3 %collective-permute-start.6 = (bf16[72,256]{1,0:T(8,128)(2,1)}, bf16[72,256]{1,0:T(8,128)(2,1)}, u32[]{:S(2)}, u32[]{:S(2)}) collective-permute-start(bf16[72,256]{1,0:T(8,128)(2,1)} %get-tuple-element.113), channel_id=1, source_target_pairs={{0,2},{2,0},{4,6},{6,4},{1,3},{3,1},{5,7},{7,5},{8,10},{10,8},{12,... | collective-permute-start | bytes 110600 | tf_op jit(solution)/shard_map/ppermute | solution.py:59
  20.0 62.8 %collective-permute-start.7 = (bf16[72,256]{1,0:T(8,128)(2,1)}, bf16[72,256]{1,0:T(8,128)(2,1)S(1)}, u32[]{:S(2)}, u32[]{:S(2)}) collective-permute-start(bf16[72,256]{1,0:T(8,128)(2,1)} %get-tuple-element.113), channel_id=1, source_target_pairs={{0,4},{2,6},{4,0},{6,2},{1,5},{3,7},{5,1},{7,3},{8,12},{10,14},{12... | collective-permute-start | bytes 110600 | tf_op jit(solution)/shard_map/ppermute | solution.py:59
  57.9 25.5 %collective-permute-start.8 = (bf16[72,256]{1,0:T(8,128)(2,1)}, bf16[72,256]{1,0:T(8,128)(2,1)S(1)}, u32[]{:S(2)}, u32[]{:S(2)}) collective-permute-start(bf16[72,256]{1,0:T(8,128)(2,1)} %get-tuple-element.113), channel_id=1, source_target_pairs={{0,6},{2,4},{4,2},{6,0},{1,7},{3,5},{5,3},{7,1},{8,14},{10,12},{12... | collective-permute-start | bytes 110600 | tf_op jit(solution)/shard_map/ppermute | solution.py:59
  60.0 25.6 %collective-permute-start.16 = (bf16[72,512]{1,0:T(8,128)(2,1)S(1)}, bf16[72,512]{1,0:T(8,128)(2,1)S(1)}, u32[]{:S(2)}, u32[]{:S(2)}) collective-permute-start(bf16[72,512]{1,0:T(8,128)(2,1)S(1)} %copy-done.77), channel_id=1, source_target_pairs={{0,2},{2,0},{4,6},{6,4},{1,3},{3,1},{5,7},{7,5},{8,10},{10,8},{12,... | collective-permute-start | bytes 221192 | tf_op jit(solution)/shard_map/ppermute | solution.py:59
  63.2 26.3 %collective-permute-start.17 = (bf16[72,512]{1,0:T(8,128)(2,1)S(1)}, bf16[72,512]{1,0:T(8,128)(2,1)S(1)}, u32[]{:S(2)}, u32[]{:S(2)}) collective-permute-start(bf16[72,512]{1,0:T(8,128)(2,1)S(1)} %copy-done.77), channel_id=1, source_target_pairs={{0,4},{2,6},{4,0},{6,2},{1,5},{3,7},{5,1},{7,3},{8,12},{10,14},{12... | collective-permute-start | bytes 221192 | tf_op jit(solution)/shard_map/ppermute | solution.py:59
  74.4 161.9 %all-gather.6.cloned.1.call-start = ((), (), s32[]{:S(2)}) async-start(), calls=%async_computation.4 | async-start | bytes 2580480 | tf_op jit(solution)/shard_map/all_gather | solution.py:172
  93.9 23.7 %collective-permute-start.9 = (bf16[4,72,256]{2,1,0:T(8,128)(2,1)}, bf16[4,72,256]{2,1,0:T(8,128)(2,1)}, u32[]{:S(2)}, u32[]{:S(2)}) collective-permute-start(bf16[4,72,256]{2,1,0:T(8,128)(2,1)} %bitcast_dynamic-update-slice_fusion.29), channel_id=1, source_target_pairs={{0,8},{8,0},{16,24},{24,16},{1,9},{9,1},{17,25},{25,17},{2,10},{10... | collective-permute-start | bytes 442376 | tf_op jit(solution)/shard_map/ppermute | solution.py:59
  95.3 25.7 %collective-permute-start.10 = (bf16[4,72,256]{2,1,0:T(8,128)(2,1)}, bf16[4,72,256]{2,1,0:T(8,128)(2,1)}, u32[]{:S(2)}, u32[]{:S(2)}) collective-permute-start(bf16[4,72,256]{2,1,0:T(8,128)(2,1)} %bitcast_dynamic-update-slice_fusion.29), channel_id=1, source_target_pairs={{0,16},{8,24},{16,0},{24,8},{1,17},{9,25},{17,1},{25,9},{2,18},{10... | collective-permute-start | bytes 442376 | tf_op jit(solution)/shard_map/ppermute | solution.py:59
  99.9 23.4 %collective-permute-start.11 = (bf16[4,72,256]{2,1,0:T(8,128)(2,1)}, bf16[4,72,256]{2,1,0:T(8,128)(2,1)}, u32[]{:S(2)}, u32[]{:S(2)}) collective-permute-start(bf16[4,72,256]{2,1,0:T(8,128)(2,1)} %bitcast_dynamic-update-slice_fusion.29), channel_id=1, source_target_pairs={{0,24},{8,16},{16,8},{24,0},{1,25},{9,17},{17,9},{25,1},{2,26},{10... | collective-permute-start | bytes 442376 | tf_op jit(solution)/shard_map/ppermute | solution.py:59
  101.9 24.1 %collective-permute-start.19 = (bf16[4,72,512]{2,1,0:T(8,128)(2,1)S(1)}, bf16[4,72,512]{2,1,0:T(8,128)(2,1)}, u32[]{:S(2)}, u32[]{:S(2)}) collective-permute-start(bf16[4,72,512]{2,1,0:T(8,128)(2,1)S(1)} %bitcast_dynamic-update-slice_fusion.25), channel_id=1, source_target_pairs={{0,8},{8,0},{16,24},{24,16},{1,9},{9,1},{17,25},{25,17},{2,10},{10... | collective-permute-start | bytes 884744 | tf_op jit(solution)/shard_map/ppermute | solution.py:59
  102.9 25.8 %collective-permute-start.20 = (bf16[4,72,512]{2,1,0:T(8,128)(2,1)S(1)}, bf16[4,72,512]{2,1,0:T(8,128)(2,1)}, u32[]{:S(2)}, u32[]{:S(2)}) collective-permute-start(bf16[4,72,512]{2,1,0:T(8,128)(2,1)S(1)} %bitcast_dynamic-update-slice_fusion.25), channel_id=1, source_target_pairs={{0,16},{8,24},{16,0},{24,8},{1,17},{9,25},{17,1},{25,9},{2,18},{10... | collective-permute-start | bytes 884744 | tf_op jit(solution)/shard_map/ppermute | solution.py:59
  117.4 159.3 %all-gather.8.cloned.1.call-start = ((), (), s32[]{:S(2)}) async-start(), calls=%async_computation.5 | async-start | bytes 2580480 | tf_op jit(solution)/shard_map/all_gather | solution.py:172
  123.3 17.2 %collective-permute-start.27 = (bf16[4,72,512]{2,1,0:T(8,128)(2,1)}, bf16[4,72,512]{2,1,0:T(8,128)(2,1)S(1)}, u32[]{:S(2)}, u32[]{:S(2)}) collective-permute-start(bf16[4,72,512]{2,1,0:T(8,128)(2,1)} %bitcast_dynamic-update-slice_fusion.22), channel_id=1, source_target_pairs={{0,16},{8,24},{16,0},{24,8},{1,17},{9,25},{17,1},{25,9},{2,18},{10... | collective-permute-start | bytes 884744 | tf_op jit(solution)/shard_map/ppermute | solution.py:59
  129.8 32.3 %collective-permute-start.22 = (bf16[1152,512]{1,0:T(8,128)(2,1)S(1)}, bf16[1152,512]{1,0:T(8,128)(2,1)S(1)}, u32[]{:S(2)}, u32[]{:S(2)}) collective-permute-start(bf16[1152,512]{1,0:T(8,128)(2,1)S(1)} %bitcast.490), channel_id=1, source_target_pairs={{0,1},{1,0},{2,3},{3,2},{4,5},{5,4},{6,7},{7,6},{8,9},{9,8},{10,11... | collective-permute-start | bytes 3538952 | tf_op jit(solution)/shard_map/ppermute | solution.py:53
  133.5 16.6 %collective-permute-start.14 = (bf16[2,128,512]{2,1,0:T(8,128)(2,1)S(1)}, bf16[2,128,512]{2,1,0:T(8,128)(2,1)S(1)}, u32[]{:S(2)}, u32[]{:S(2)}) collective-permute-start(bf16[2,128,512]{2,1,0:T(8,128)(2,1)S(1)} %pad_maximum_fusion.8), channel_id=1, source_target_pairs={{0,4},{2,6},{1,5},{3,7},{8,12},{10,14},{9,13},{11,15},{16,20},{18,... | collective-permute-start | bytes 786440 | tf_op jit(solution)/shard_map/ppermute | solution.py:65
  137.9 23.2 %collective-permute-start.13 = (bf16[2,128,512]{2,1,0:T(8,128)(2,1)S(1)}, bf16[2,128,512]{2,1,0:T(8,128)(2,1)S(1)}, u32[]{:S(2)}, u32[]{:S(2)}) collective-permute-start(bf16[2,128,512]{2,1,0:T(8,128)(2,1)S(1)} %pad_maximum_fusion.8), channel_id=1, source_target_pairs={{0,2},{2,4},{4,6},{1,3},{3,5},{5,7},{8,10},{10,12},{12,14},{9,11},... | collective-permute-start | bytes 786440 | tf_op jit(solution)/shard_map/ppermute | solution.py:65
  142.0 34.1 %collective-permute-start.29 = (bf16[1152,512]{1,0:T(8,128)(2,1)}, bf16[1152,512]{1,0:T(8,128)(2,1)}, u32[]{:S(2)}, u32[]{:S(2)}) collective-permute-start(bf16[1152,512]{1,0:T(8,128)(2,1)} %bitcast.50), channel_id=1, source_target_pairs={{0,1},{1,0},{2,3},{3,2},{4,5},{5,4},{6,7},{7,6},{8,9},{9,8},{10,11... | collective-permute-start | bytes 3538952 | tf_op jit(solution)/shard_map/ppermute | solution.py:53
  179.9 35.2 %collective-permute-start.30 = (bf16[256,1152]{1,0:T(8,128)(2,1)S(1)}, bf16[256,1152]{1,0:T(8,128)(2,1)}, u32[]{:S(2)}, u32[]{:S(2)}) collective-permute-start(bf16[256,1152]{1,0:T(8,128)(2,1)S(1)} %bitcast.496), channel_id=1, source_target_pairs={{0,8},{8,0},{16,24},{24,16},{1,9},{9,1},{17,25},{25,17},{2,10},{10... | collective-permute-start | bytes 1769480 | tf_op jit(solution)/shard_map/ppermute | solution.py:59
  181.8 17.0 %collective-permute-start.43 = (bf16[72,864]{1,0:T(8,128)(2,1)S(1)}, bf16[72,864]{1,0:T(8,128)(2,1)S(1)}, u32[]{:S(2)}, u32[]{:S(2)}) collective-permute-start(bf16[72,864]{1,0:T(8,128)(2,1)S(1)} %bitcast.533), channel_id=1, source_target_pairs={{0,8},{8,0},{16,24},{24,16},{1,9},{9,1},{17,25},{25,17},{2,10},{10... | collective-permute-start | bytes 373256 | tf_op jit(solution)/shard_map/ppermute | solution.py:59
  185.4 17.3 %collective-permute-start.45 = (bf16[72,864]{1,0:T(8,128)(2,1)S(1)}, bf16[72,864]{1,0:T(8,128)(2,1)S(1)}, u32[]{:S(2)}, u32[]{:S(2)}) collective-permute-start(bf16[72,864]{1,0:T(8,128)(2,1)S(1)} %bitcast.537), channel_id=1, source_target_pairs={{0,24},{8,16},{16,8},{24,0},{1,25},{9,17},{17,9},{25,1},{2,26},{10... | collective-permute-start | bytes 373256 | tf_op jit(solution)/shard_map/ppermute | solution.py:59
  185.5 32.1 %collective-permute-start.31 = (bf16[256,1152]{1,0:T(8,128)(2,1)S(1)}, bf16[256,1152]{1,0:T(8,128)(2,1)}, u32[]{:S(2)}, u32[]{:S(2)}) collective-permute-start(bf16[256,1152]{1,0:T(8,128)(2,1)S(1)} %bitcast.497), channel_id=1, source_target_pairs={{0,16},{8,24},{16,0},{24,8},{1,17},{9,25},{17,1},{25,9},{2,18},{10... | collective-permute-start | bytes 1769480 | tf_op jit(solution)/shard_map/ppermute | solution.py:59
  213.9 299.2 %reduce-scatter.4.cloned.1.call-start = ((), (), s32[]{:S(2)}) async-start(), calls=%async_computation.6 | async-start | bytes 2580480 | tf_op jit(solution)/shard_map/reduce_scatter | solution.py:325
  215.2 16.6 %collective-permute-start.34 = (bf16[256,1152]{1,0:T(8,128)(2,1)}, bf16[256,1152]{1,0:T(8,128)(2,1)S(1)}, u32[]{:S(2)}, u32[]{:S(2)}) collective-permute-start(bf16[256,1152]{1,0:T(8,128)(2,1)} %collective-permute-done.30), channel_id=1, source_target_pairs={{0,1},{1,0},{2,3},{3,2},{4,5},{5,4},{6,7},{7,6},{8,9},{9,8},{10,11... | collective-permute-start | bytes 1769480 | tf_op jit(solution)/shard_map/ppermute | solution.py:53
  294.4 17.3 %collective-permute-start.49 = (bf16[256,1152]{1,0:T(8,128)(2,1)}, bf16[256,1152]{1,0:T(8,128)(2,1)S(1)}, u32[]{:S(2)}, u32[]{:S(2)}) collective-permute-start(bf16[256,1152]{1,0:T(8,128)(2,1)} %get-tuple-element.124), channel_id=1, source_target_pairs={{0,24},{8,16},{16,8},{24,0},{1,25},{9,17},{17,9},{25,1},{2,26},{10... | collective-permute-start | bytes 1769480 | tf_op jit(solution)/shard_map/ppermute | solution.py:59
  296.8 26.7 %collective-permute-start.48 = (bf16[256,1152]{1,0:T(8,128)(2,1)}, bf16[256,1152]{1,0:T(8,128)(2,1)S(1)}, u32[]{:S(2)}, u32[]{:S(2)}) collective-permute-start(bf16[256,1152]{1,0:T(8,128)(2,1)} %get-tuple-element.125), channel_id=1, source_target_pairs={{0,16},{8,24},{16,0},{24,8},{1,17},{9,25},{17,1},{25,9},{2,18},{10... | collective-permute-start | bytes 1769480 | tf_op jit(solution)/shard_map/ppermute | solution.py:59
  297.3 26.2 %collective-permute-start.47 = (bf16[256,1152]{1,0:T(8,128)(2,1)S(1)}, bf16[256,1152]{1,0:T(8,128)(2,1)S(1)}, u32[]{:S(2)}, u32[]{:S(2)}) collective-permute-start(bf16[256,1152]{1,0:T(8,128)(2,1)S(1)} %get-tuple-element.123), channel_id=1, source_target_pairs={{0,8},{8,0},{16,24},{24,16},{1,9},{9,1},{17,25},{25,17},{2,10},{10... | collective-permute-start | bytes 1769480 | tf_op jit(solution)/shard_map/ppermute | solution.py:59
  327.6 16.3 %collective-permute-start.50 = (bf16[256,1152]{1,0:T(8,128)(2,1)S(1)}, bf16[256,1152]{1,0:T(8,128)(2,1)S(1)}, u32[]{:S(2)}, u32[]{:S(2)}) collective-permute-start(bf16[256,1152]{1,0:T(8,128)(2,1)S(1)} %get-tuple-element.209), channel_id=1, source_target_pairs={{0,8},{8,0},{16,24},{24,16},{1,9},{9,1},{17,25},{25,17},{2,10},{10... | collective-permute-start | bytes 1769480 | tf_op jit(solution)/shard_map/ppermute | solution.py:59
  329.2 27.6 %collective-permute-start.51 = (bf16[256,1152]{1,0:T(8,128)(2,1)S(1)}, bf16[256,1152]{1,0:T(8,128)(2,1)S(1)}, u32[]{:S(2)}, u32[]{:S(2)}) collective-permute-start(bf16[256,1152]{1,0:T(8,128)(2,1)S(1)} %get-tuple-element.209), channel_id=1, source_target_pairs={{0,16},{8,24},{16,0},{24,8},{1,17},{9,25},{17,1},{25,9},{2,18},{10... | collective-permute-start | bytes 1769480 | tf_op jit(solution)/shard_map/ppermute | solution.py:59
  329.9 26.9 %collective-permute-start.52 = (bf16[256,1152]{1,0:T(8,128)(2,1)S(1)}, bf16[256,1152]{1,0:T(8,128)(2,1)S(1)}, u32[]{:S(2)}, u32[]{:S(2)}) collective-permute-start(bf16[256,1152]{1,0:T(8,128)(2,1)S(1)} %get-tuple-element.209), channel_id=1, source_target_pairs={{0,24},{8,16},{16,8},{24,0},{1,25},{9,17},{17,9},{25,1},{2,26},{10... | collective-permute-start | bytes 1769480 | tf_op jit(solution)/shard_map/ppermute | solution.py:59
  331.2 26.3 %collective-permute-start.53 = (bf16[256,1152]{1,0:T(8,128)(2,1)S(1)}, bf16[256,1152]{1,0:T(8,128)(2,1)S(1)}, u32[]{:S(2)}, u32[]{:S(2)}) collective-permute-start(bf16[256,1152]{1,0:T(8,128)(2,1)S(1)} %get-tuple-element.209), channel_id=1, source_target_pairs={{0,1},{1,0},{2,3},{3,2},{4,5},{5,4},{6,7},{7,6},{8,9},{9,8},{10,11... | collective-permute-start | bytes 1769480 | tf_op jit(solution)/shard_map/ppermute | solution.py:53
  393.1 121.5 %reduce-scatter.6.cloned.1.call-start = ((), (), s32[]{:S(2)}) async-start(), calls=%async_computation.7 | async-start | bytes 2580480 | tf_op jit(solution)/shard_map/reduce_scatter | solution.py:325
  426.0 108.2 %reduce-scatter.8.cloned.1.call-start = ((), (), s32[]{:S(2)}) async-start(), calls=%async_computation.8 | async-start | bytes 2580480 | tf_op jit(solution)/shard_map/reduce_scatter | solution.py:325
  432.8 19.1 %collective-permute-start.60 = (bf16[256,1152]{1,0:T(8,128)(2,1)}, bf16[256,1152]{1,0:T(8,128)(2,1)}, u32[]{:S(2)}, u32[]{:S(2)}) collective-permute-start(bf16[256,1152]{1,0:T(8,128)(2,1)} %get-tuple-element.121), channel_id=1, source_target_pairs={{0,24},{8,16},{16,8},{24,0},{1,25},{9,17},{17,9},{25,1},{2,26},{10... | collective-permute-start | bytes 1769480 | tf_op jit(solution)/shard_map/ppermute | solution.py:59
  434.2 28.1 %collective-permute-start.59 = (bf16[256,1152]{1,0:T(8,128)(2,1)S(1)}, bf16[256,1152]{1,0:T(8,128)(2,1)}, u32[]{:S(2)}, u32[]{:S(2)}) collective-permute-start(bf16[256,1152]{1,0:T(8,128)(2,1)S(1)} %get-tuple-element.122), channel_id=1, source_target_pairs={{0,16},{8,24},{16,0},{24,8},{1,17},{9,25},{17,1},{25,9},{2,18},{10... | collective-permute-start | bytes 1769480 | tf_op jit(solution)/shard_map/ppermute | solution.py:59
  434.7 27.5 %collective-permute-start.58 = (bf16[256,1152]{1,0:T(8,128)(2,1)S(1)}, bf16[256,1152]{1,0:T(8,128)(2,1)}, u32[]{:S(2)}, u32[]{:S(2)}) collective-permute-start(bf16[256,1152]{1,0:T(8,128)(2,1)S(1)} %get-tuple-element.120), channel_id=1, source_target_pairs={{0,8},{8,0},{16,24},{24,16},{1,9},{9,1},{17,25},{25,17},{2,10},{10... | collective-permute-start | bytes 1769480 | tf_op jit(solution)/shard_map/ppermute | solution.py:59
  487.5 18.6 %collective-permute-start.61 = (bf16[2,384,512]{2,1,0:T(8,128)(2,1)}, bf16[2,384,512]{2,1,0:T(8,128)(2,1)}, u32[]{:S(2)}, u32[]{:S(2)}) collective-permute-start(bf16[2,384,512]{2,1,0:T(8,128)(2,1)} %fusion.18), channel_id=1, source_target_pairs={{0,1},{1,0},{2,3},{3,2},{4,5},{5,4},{6,7},{7,6},{8,9},{9,8},{10,11... | collective-permute-start | bytes 2359304 | tf_op jit(solution)/shard_map/ppermute | solution.py:53
  501.5 83.7 %collective-permute-start.71 = (bf16[1152,512]{1,0:T(8,128)(2,1)}, bf16[1152,512]{1,0:T(8,128)(2,1)}, u32[]{:S(2)}, u32[]{:S(2)}) collective-permute-start(bf16[1152,512]{1,0:T(8,128)(2,1)} %slice.329), channel_id=1, source_target_pairs={{0,1},{1,0},{2,3},{3,2},{4,5},{5,4},{6,7},{7,6},{8,9},{9,8},{10,11... | collective-permute-start | bytes 3538952 | tf_op jit(solution)/shard_map/ppermute | solution.py:53
  506.1 82.5 %collective-permute-start.86 = (bf16[1152,512]{1,0:T(8,128)(2,1)}, bf16[1152,512]{1,0:T(8,128)(2,1)}, u32[]{:S(2)}, u32[]{:S(2)}) collective-permute-start(bf16[1152,512]{1,0:T(8,128)(2,1)} %slice.328), channel_id=1, source_target_pairs={{0,1},{1,0},{2,3},{3,2},{4,5},{5,4},{6,7},{7,6},{8,9},{9,8},{10,11... | collective-permute-start | bytes 3538952 | tf_op jit(solution)/shard_map/ppermute | solution.py:53
  510.1 26.5 %collective-permute-start.63 = (bf16[2,128,512]{2,1,0:T(8,128)(2,1)}, bf16[2,128,512]{2,1,0:T(8,128)(2,1)S(1)}, u32[]{:S(2)}, u32[]{:S(2)}) collective-permute-start(bf16[2,128,512]{2,1,0:T(8,128)(2,1)} %get-tuple-element.139), channel_id=1, source_target_pairs={{4,0},{6,2},{5,1},{7,3},{12,8},{14,10},{13,9},{15,11},{20,16},{22,... | collective-permute-start | bytes 786440 | tf_op jit(solution)/shard_map/ppermute | solution.py:65
  511.3 25.2 %collective-permute-start.62 = (bf16[2,128,512]{2,1,0:T(8,128)(2,1)S(1)}, bf16[2,128,512]{2,1,0:T(8,128)(2,1)S(1)}, u32[]{:S(2)}, u32[]{:S(2)}) collective-permute-start(bf16[2,128,512]{2,1,0:T(8,128)(2,1)S(1)} %get-tuple-element.138), channel_id=1, source_target_pairs={{2,0},{4,2},{6,4},{3,1},{5,3},{7,5},{10,8},{12,10},{14,12},{11,9},... | collective-permute-start | bytes 786440 | tf_op jit(solution)/shard_map/ppermute | solution.py:65
  578.2 46.1 %collective-permute-start.78 = (bf16[1152,256]{1,0:T(8,128)(2,1)}, bf16[1152,256]{1,0:T(8,128)(2,1)}, u32[]{:S(2)}, u32[]{:S(2)}) collective-permute-start(bf16[1152,256]{1,0:T(8,128)(2,1)} %slice.330), channel_id=1, source_target_pairs={{0,1},{1,0},{2,3},{3,2},{4,5},{5,4},{6,7},{7,6},{8,9},{9,8},{10,11... | collective-permute-start | bytes 1769480 | tf_op jit(solution)/shard_map/ppermute | solution.py:53
  595.7 23.5 %collective-permute-start.74 = (bf16[4,72,512]{2,1,0:T(8,128)(2,1)}, bf16[4,72,512]{2,1,0:T(8,128)(2,1)}, u32[]{:S(2)}, u32[]{:S(2)}) collective-permute-start(bf16[4,72,512]{2,1,0:T(8,128)(2,1)} %get-tuple-element.134), channel_id=1, source_target_pairs={{0,24},{8,16},{16,8},{24,0},{1,25},{9,17},{17,9},{25,1},{2,26},{10... | collective-permute-start | bytes 884744 | tf_op jit(solution)/shard_map/ppermute | solution.py:59
  596.5 23.6 %collective-permute-start.73 = (bf16[4,72,512]{2,1,0:T(8,128)(2,1)}, bf16[4,72,512]{2,1,0:T(8,128)(2,1)}, u32[]{:S(2)}, u32[]{:S(2)}) collective-permute-start(bf16[4,72,512]{2,1,0:T(8,128)(2,1)} %get-tuple-element.135), channel_id=1, source_target_pairs={{0,16},{8,24},{16,0},{24,8},{1,17},{9,25},{17,1},{25,9},{2,18},{10... | collective-permute-start | bytes 884744 | tf_op jit(solution)/shard_map/ppermute | solution.py:59
  608.5 19.1 %collective-permute-start.89 = (bf16[4,72,512]{2,1,0:T(8,128)(2,1)}, bf16[4,72,512]{2,1,0:T(8,128)(2,1)}, u32[]{:S(2)}, u32[]{:S(2)}) collective-permute-start(bf16[4,72,512]{2,1,0:T(8,128)(2,1)} %get-tuple-element.131), channel_id=1, source_target_pairs={{0,24},{8,16},{16,8},{24,0},{1,25},{9,17},{17,9},{25,1},{2,26},{10... | collective-permute-start | bytes 884744 | tf_op jit(solution)/shard_map/ppermute | solution.py:59
  (182 other events, 1346.3 us)
Sparse Core Ops, SparseCore 0:
  74.5 48.2 all-gather.3
  124.4 51.7 all-gather.5
  214.0 62.6 all-gather.7
  393.2 43.6 reduce-scatter.3
  439.2 42.4 reduce-scatter.5
  483.9 50.2 reduce-scatter.7

commit v2 on v1

v2 whole, which is shorter than its diff:
```python
import jax
import jax.numpy as jnp
from jax import lax
from jax.sharding import PartitionSpec as P

HEAD_DIM = 256
WINDOW = 512

EPSILON = 1e-06
ROPE_BASE = 10000.0
SCORE_SCALE = 0.0625
MASKED = -1e30

SEGMENT_NUMBERS = 10

F32 = jnp.float32
BF16 = jnp.bfloat16
GROUPS = ((0, 1),)


def dot(spec, left, right):
    return jnp.einsum(spec, left, right, preferred_element_type=F32)


def normed(values, gain):
    return values * lax.rsqrt(jnp.mean(values * values, axis=-1, keepdims=True) + EPSILON) * gain


def turned(values, cosines, sines):
    middle = values.shape[-1] // 2
    first_half = values[..., :middle]
    second_half = values[..., middle:]
    return jnp.concatenate(
        [first_half * cosines - second_half * sines, second_half * cosines + first_half * sines],
        axis=-1,
    )


def rotations(offsets, depth):
    middle = depth // 2
    inverse = ROPE_BASE ** (-2.0 * jnp.arange(middle, dtype=F32) / depth)
    angle_grid = offsets[..., None] * inverse
    return (jnp.cos(angle_grid), jnp.sin(angle_grid))


def rope_normed(values, gain, cosines, sines):
    return turned(normed(values, gain), cosines, sines)


def feed_inner(gate_act, up_act):
    return jax.nn.gelu(gate_act, approximate=True) * up_act


def swap(value):
    return lax.ppermute(value, "tp", [(0, 1), (1, 0)])


BOTH = ("fsdp", "ctx")


def cross(value, mask):
    count = lax.axis_size("fsdp") * lax.axis_size("ctx")
    return lax.ppermute(value, BOTH, [(i, i ^ mask) for i in range(count)])


def shift(value, step):
    count = lax.axis_size("ctx")
    pairs = [(i, i + step) for i in range(count) if 0 <= i + step < count]
    return lax.ppermute(value, "ctx", pairs)


def together(*values):
    return lax.optimization_barrier(values)


def placed(own, other, bit, dim):
    first = jnp.where(bit == 0, own, other)
    second = jnp.where(bit == 0, other, own)
    return jnp.concatenate([first, second], axis=dim)


def parted(value, bit, dim):
    zero = lax.index_in_dim(value, 0, axis=dim, keepdims=False)
    one = lax.index_in_dim(value, 1, axis=dim, keepdims=False)
    return jnp.where(bit == 0, zero, one), jnp.where(bit == 0, one, zero)


def copies_to(value, axis):
    count = lax.axis_size(axis)
    return lax.all_to_all(jnp.broadcast_to(value[None], (count,) + value.shape), axis, 0, 0)


def gather_rows(value):
    return copies_to(copies_to(value, "ctx"), "fsdp")


def sum_of(parts, axis):
    return jnp.sum(lax.all_to_all(parts.astype(BF16), axis, 0, 0).astype(F32), axis=0)


def scatter_rows(value):
    return sum_of(sum_of(value, "fsdp"), "ctx")


def near_groups():
    planes, depths = lax.axis_size("fsdp"), lax.axis_size("ctx")
    return [
        [(f + x) * depths + c + z for x in (0, 1) for z in (0, 1)]
        for f in range(0, planes, 2)
        for c in range(0, depths, 2)
    ]


def trade(value):
    return lax.all_to_all(value, BOTH, 0, 0, axis_index_groups=near_groups())


def trade_apart(value):
    depths = lax.axis_size("ctx")
    x_bit, z_bit = lax.axis_index("fsdp") & 1, lax.axis_index("ctx") & 1
    low, high = parted(value.reshape((2, 2) + value.shape[1:]), x_bit, 0)
    (p0, p1), (p2, p3) = parted(low, z_bit, 0), parted(high, z_bit, 0)
    p1, p2, p3 = cross(p1, 1), cross(p2, depths), cross(p3, depths | 1)
    low = placed(p0[None], p1[None], z_bit, 0)
    high = placed(p2[None], p3[None], z_bit, 0)
    return placed(low[None], high[None], x_bit, 0).reshape(value.shape)


def far_bits():
    planes, depths = lax.axis_size("fsdp"), lax.axis_size("ctx")
    f_place, c_place = lax.axis_index("fsdp"), lax.axis_index("ctx")
    f_count, c_count = (planes - 1).bit_length(), (depths - 1).bit_length()
    c_bits = [(1 << k, (c_place >> k) & 1) for k in range(c_count - 1, 0, -1)]
    f_bits = [(depths << k, (f_place >> k) & 1) for k in range(f_count - 1, 0, -1)]
    return c_bits, f_bits


def gather_depth(value):
    c_bits, _ = far_bits()
    for mask, bit in c_bits[::-1]:
        value = placed(value, cross(value, mask), bit, 1)
    return value


def gather_plane(value):
    _, f_bits = far_bits()
    for mask, bit in f_bits[::-1]:
        value = placed(value, cross(value, mask), bit, 0)
    return value


def scatter_plane(value):
    _, f_bits = far_bits()
    for mask, bit in f_bits:
        halves = value.reshape((2, value.shape[0] // 2) + value.shape[1:])
        mine, other = parted(halves, bit, 0)
        value = (mine.astype(F32) + cross(other, mask).astype(F32)).astype(BF16)
    return value


def scatter_depth(value):
    c_bits, _ = far_bits()
    for mask, bit in c_bits:
        halves = value.reshape((2, 2, value.shape[1] // 2) + value.shape[2:])
        mine, other = parted(halves, bit, 1)
        value = (mine.astype(F32) + cross(other, mask).astype(F32)).astype(BF16)
    return value


def spread_start(rows):
    mine = trade(jnp.broadcast_to(rows[None], (4,) + rows.shape))
    return mine.reshape((-1,) + rows.shape[1:])


def spread(rows):
    mine = spread_start(rows)
    return jnp.concatenate([mine, swap(mine)], axis=0)


def collect_start(part):
    half = part.shape[0] // 2
    own = part[:half].astype(F32) + swap(part[half:]).astype(F32)
    return own.astype(BF16).reshape(4, half // 4, part.shape[1])


def collect(part):
    return jnp.sum(trade(collect_start(part)).astype(F32), axis=0)


def local(
    tokens,
    segments,
    cotangent,
    norm_input,
    query_weight,
    key_weight,
    value_weight,
    norm_query,
    norm_key,
    out_weight,
    norm_attention,
    norm_feed,
    gate_weight,
    up_weight,
    down_weight,
    norm_feed_out,
):
    micros, seqs, block_len, width = tokens.shape
    planes = lax.axis_size("fsdp")
    depths = lax.axis_size("ctx")
    chunks = planes * depths
    ctx_place = lax.axis_index("ctx")
    tp_place = lax.axis_index("tp")
    first_core = tp_place == 0
    half_len = block_len // lax.axis_size("tp")
    back_blocks = -(-WINDOW // block_len)
    rows_in = norm_input.shape[0]
    small = norm_query.shape[0]
    heads_half = query_weight.shape[1] // HEAD_DIM
    q_cols = query_weight.shape[1]
    units = -(-gate_weight.shape[1] // (4 * 128)) * 128
    spare = 4 * units - gate_weight.shape[1]
    numbers = jnp.arange(SEGMENT_NUMBERS, dtype=jnp.int32)
    counts = jnp.sum((segments[..., None] == numbers).astype(F32), axis=2).astype(BF16)
    kv_shard = jnp.where(first_core, key_weight, value_weight)
    gain_row = jnp.concatenate(
        [norm_input, norm_attention, norm_feed, norm_feed_out, norm_query, norm_key]
    )
    first_cols = q_cols + HEAD_DIM
    gain_row = jnp.pad(gain_row, (0, first_cols - gain_row.shape[0]))
    count_row = counts.reshape(-1)
    count_row = jnp.pad(count_row, (0, 7 * first_cols - count_row.shape[0]))
    first_pack = jnp.concatenate([query_weight, kv_shard], axis=1)
    rows_more = jnp.concatenate([gain_row, count_row]).reshape(8, first_cols)
    first_pack = jnp.concatenate([first_pack, rows_more], axis=0)
    first_pack = jnp.broadcast_to(first_pack[None], (depths,) + first_pack.shape)
    first_pack, gate_weight, up_weight, down_weight, out_weight = together(
        first_pack, gate_weight, up_weight, down_weight, out_weight
    )
    first_pack = lax.all_to_all(first_pack, "ctx", 0, 0)

    feed_parts = jnp.stack([gate_weight, up_weight, down_weight.T], axis=0)
    feed_parts = jnp.pad(feed_parts, ((0, 0), (0, 0), (0, spare)))
    feed_parts = feed_parts.reshape(3, rows_in, 4, units).transpose(2, 0, 1, 3)
    feed_parts = trade_apart(feed_parts)
    first_pack, feed_parts = together(first_pack, feed_parts)
    counts_all = first_pack[:, rows_in + 1, : counts.size].astype(F32)
    counts_all = jnp.sum(counts_all, axis=0).reshape(counts.shape)

    feed_parts = feed_parts.reshape(2, 2, 3, rows_in, units)
    gate_near, up_near, down_near = (feed_parts[:, :, which] for which in range(3))
    gate_deep = gather_depth(gate_near)
    first_pack = copies_to(first_pack, "fsdp")
    first_pack, gate_deep, up_near, down_near, out_pack = together(
        first_pack, gate_deep, up_near, down_near, out_weight.T
    )

    first_pack = first_pack.reshape(chunks, rows_in + 8, first_cols)
    gains_all = first_pack[:, rows_in].astype(F32)
    first_own = first_pack[:, :rows_in].reshape(width, first_cols)
    first_other = swap(first_own)
    cuts = [0, rows_in, 2 * rows_in, 3 * rows_in, 4 * rows_in, 4 * rows_in + small]
    ends = cuts[1:] + [4 * rows_in + 2 * small]
    gain_input, gain_attention, gain_feed, gain_feed_out, gain_query, gain_key = (
        gains_all[:, lo:hi].reshape(-1) for lo, hi in zip(cuts, ends)
    )
    out_pack = copies_to(out_pack, "ctx")
    up_deep = gather_depth(up_near)
    gate_w = gather_plane(gate_deep).reshape(width, units)

    half_at = tp_place * half_len
    seg_half = lax.dynamic_slice_in_dim(segments, half_at, half_len, 2)
    earlier = numbers < seg_half[..., None]
    starts = jnp.sum(jnp.where(earlier, counts_all[:, :, None, :], 0.0), axis=-1)
    starts = starts.astype(jnp.int32)
    token_place = ctx_place * block_len + half_at + jnp.arange(half_len, dtype=jnp.int32)
    cosines, sines = rotations((token_place - starts).astype(F32), HEAD_DIM)
    within = jnp.arange(half_len, dtype=jnp.int32)
    key_place = jnp.concatenate(
        [
            (ctx_place - back) * block_len + side * half_len + within
            for side in (tp_place, 1 - tp_place)
            for back in range(back_blocks + 1)
        ]
    )

    x_halves = lax.dynamic_slice_in_dim(tokens, half_at, half_len, 2)
    dy_halves = lax.dynamic_slice_in_dim(cotangent, half_at, half_len, 2)

    saved = []
    outputs = []
    for group in GROUPS:
        lo, hi = group[0], group[-1] + 1
        batch = (hi - lo) * seqs

        def pick(value):
            return value[lo:hi].reshape((batch,) + value.shape[2:])

        x = pick(x_halves).astype(F32)
        cos, sin, begin = pick(cosines), pick(sines), pick(starts)
        cos_heads, sin_heads = cos[:, :, None, :], sin[:, :, None, :]
        h1 = normed(x, gain_input).astype(BF16)
        left = dot("bld,de->ble", h1, first_own)
        right = dot("bld,de->ble", h1, first_other)
        kv_left, kv_right = left[..., q_cols:], right[..., q_cols:]
        key_full = jnp.where(first_core, kv_left, kv_right)
        value_full = jnp.where(first_core, kv_right, kv_left)
        key_rot = rope_normed(key_full, gain_key, cos, sin).astype(BF16)
        pair = jnp.concatenate([key_rot, value_full.astype(BF16)], axis=-1)
        pair, left, right, up_deep, gate_w, out_pack = together(
            pair, left, right, up_deep, gate_w, out_pack
        )
        up_w = gather_plane(up_deep).reshape(width, units)
        out_own = copies_to(out_pack, "fsdp").reshape(width, q_cols)
        mine = jnp.concatenate(
            [pair] + [shift(pair, back) for back in range(1, back_blocks + 1)], axis=1
        )
        seen = jnp.concatenate([mine, swap(mine)], axis=1)
        keys, values = seen[..., :HEAD_DIM], seen[..., HEAD_DIM:]
        query_full = jnp.concatenate([left[..., :q_cols], right[..., :q_cols]], axis=-1)
        query_full = query_full.reshape(batch, half_len, 2 * heads_half, HEAD_DIM)
        query_rot = rope_normed(query_full, gain_query, cos_heads, sin_heads).astype(BF16)
        query_rot, keys, values, up_w, out_own, down_near = together(
            query_rot, keys, values, up_w, out_own, down_near
        )
        out_other = swap(out_own)
        down_deep = gather_depth(down_near)
        allowed = (
            (key_place[None, None, :] <= token_place[None, :, None])
            & (token_place[None, :, None] - key_place[None, None, :] < WINDOW)
            & (key_place[None, None, :] >= begin[:, :, None])
        )
        raw = dot("blhe,bke->bhlk", query_rot, keys)
        scores = jnp.where(allowed[:, None], raw * SCORE_SCALE, MASKED)
        row_max = jnp.max(scores, axis=-1, keepdims=True)
        lifted = jnp.exp(scores - row_max)
        prob = lifted / jnp.sum(lifted, axis=-1, keepdims=True)
        prob_low = prob.astype(BF16)
        mixed = dot("bhlk,bke->blhe", prob_low, values).astype(BF16)
        mixed = mixed.reshape(batch, half_len, 2 * q_cols)
        attention = dot("ble,de->bld", mixed[..., :q_cols], out_own)
        attention = attention + dot("ble,de->bld", mixed[..., q_cols:], out_other)
        middle = x + normed(attention, gain_attention)
        h2 = normed(middle, gain_feed).astype(BF16).reshape(batch * half_len, width)
        h2, down_deep = together(h2, down_deep)
        down_w = gather_plane(down_deep).reshape(width, units)
        h2_mine, down_w = together(spread_start(h2), down_w)
        h2_all = jnp.concatenate([h2_mine, swap(h2_mine)], axis=0)
        gate_act = dot("td,du->tu", h2_all, gate_w)
        up_act = dot("td,du->tu", h2_all, up_w)
        hidden = feed_inner(gate_act, up_act).astype(BF16)
        feed = collect(dot("tu,du->td", hidden, down_w).astype(BF16))
        feed = feed.reshape(batch, half_len, width)
        layer_out = (middle + normed(feed, gain_feed_out)).astype(BF16)
        outputs.append(layer_out.reshape(hi - lo, seqs, half_len, width))
        saved.append(
            (x, cos, sin, h1, key_full, query_full, query_rot, keys, values, prob, prob_low)
            + (mixed, attention, middle, h2_all, gate_act, up_act, hidden, feed)
        )

    input_grads = []
    grads = None
    for group, kept in zip(GROUPS, saved):
        lo, hi = group[0], group[-1] + 1
        batch = (hi - lo) * seqs
        (x, cos, sin, h1, key_full, query_full, query_rot, keys, values, prob, prob_low) = kept[:11]
        (mixed, attention, middle, h2_all, gate_act, up_act, hidden, feed) = kept[11:]
        cos_heads, sin_heads = cos[:, :, None, :], sin[:, :, None, :]
        dy = dy_halves[lo:hi].reshape(batch, half_len, width).astype(F32)
        d_feed, d_gain_feed_out = jax.vjp(normed, feed, gain_feed_out)[1](dy)
        d_feed_all = spread(d_feed.astype(BF16).reshape(batch * half_len, width))
        grad_down = dot("td,tu->du", d_feed_all, hidden).astype(BF16)
        d_feed_all, grad_down = together(d_feed_all, grad_down)
        down_plane = scatter_plane(grad_down.reshape(planes, depths, rows_in, units))
        d_hidden = dot("td,du->tu", d_feed_all, down_w)
        d_gate, d_up = jax.vjp(feed_inner, gate_act, up_act)[1](d_hidden)
        d_gate, d_up = d_gate.astype(BF16), d_up.astype(BF16)
        d_h2_part = dot("tu,du->td", d_gate, gate_w) + dot("tu,du->td", d_up, up_w)
        d_h2_part = d_h2_part.astype(BF16)
        d_h2_part, down_plane, d_gate, d_up = together(d_h2_part, down_plane, d_gate, d_up)
        d_h2_part = collect_start(d_h2_part)
        grad_gate = dot("td,tu->du", h2_all, d_gate).astype(BF16)
        d_h2_part, grad_gate, d_up = together(d_h2_part, grad_gate, d_up)
        d_h2_parts = trade(d_h2_part)
        gate_plane = scatter_plane(grad_gate.reshape(planes, depths, rows_in, units))
        grad_up = dot("td,tu->du", h2_all, d_up).astype(BF16)
        d_h2_parts, gate_plane, grad_up, down_plane = together(
            d_h2_parts, gate_plane, grad_up, down_plane
        )
        up_plane = scatter_plane(grad_up.reshape(planes, depths, rows_in, units))
        down_near = scatter_depth(down_plane)
        d_h2 = jnp.sum(d_h2_parts.astype(F32), axis=0).reshape(batch, half_len, width)
        d_mid_norm, d_gain_feed = jax.vjp(normed, middle, gain_feed)[1](d_h2)
        d_middle = dy + d_mid_norm
        d_attention, d_gain_attention = jax.vjp(normed, attention, gain_attention)[1](d_middle)
        d_attention = d_attention.astype(BF16)
        d_mixed = jnp.concatenate(
            [dot("bld,de->ble", d_attention, half) for half in (out_own, out_other)], axis=-1
        ).astype(BF16)
        d_mixed = d_mixed.reshape(batch, half_len, 2 * heads_half, HEAD_DIM)
        d_prob = dot("blhe,bke->bhlk", d_mixed, values)
        row_delta = jnp.sum(prob * d_prob, axis=-1, keepdims=True)
        d_raw = (prob * (d_prob - row_delta) * SCORE_SCALE).astype(BF16)
        d_raw, prob_low, up_plane, down_near, gate_plane = together(
            d_raw, prob_low, up_plane, down_near, gate_plane
        )
        gate_near = scatter_depth(gate_plane)
        d_query_rot = dot("bhlk,bke->blhe", d_raw, keys)
        d_keys = dot("bhlk,blhe->bke", d_raw, query_rot)
        d_values = dot("bhlk,blhe->bke", prob_low, d_mixed)
        d_pair = jnp.concatenate([d_keys, d_values], axis=-1)
        out_right = dot("bld,ble->de", d_attention, mixed[..., q_cols:]).astype(BF16)
        d_pair, gate_near, up_plane, out_right = together(d_pair, gate_near, up_plane, out_right)
        out_sum = dot("bld,ble->de", d_attention, mixed[..., :q_cols])
        out_sum = (out_sum + swap(out_right).astype(F32)).astype(BF16)
        out_sum = sum_of(out_sum.reshape(planes, depths, rows_in, q_cols), "fsdp")
        side = (back_blocks + 1) * half_len
        d_mine = d_pair[:, :side] + swap(d_pair[:, side:].astype(BF16)).astype(F32)
        d_kv = d_mine[:, :half_len]
        for back in range(1, back_blocks + 1):
            piece = d_mine[:, back * half_len : (back + 1) * half_len].astype(BF16)
            d_kv = d_kv + shift(piece, -back).astype(F32)
        d_kv, out_sum, up_plane = together(d_kv, out_sum, up_plane)
        out_sum = sum_of(out_sum, "ctx")
        up_near = scatter_depth(up_plane)

        def rotate_query(value, gain):
            return rope_normed(value, gain, cos_heads, sin_heads)

        def rotate_key(value, gain):
            return rope_normed(value, gain, cos, sin)

        d_query, d_gain_query = jax.vjp(rotate_query, query_full, gain_query)[1](d_query_rot)
        d_query = d_query.astype(BF16).reshape(batch, half_len, 2 * q_cols)
        d_key, d_gain_key = jax.vjp(rotate_key, key_full, gain_key)[1](d_kv[..., :HEAD_DIM])
        d_key = d_key.astype(BF16)
        d_value = d_kv[..., HEAD_DIM:].astype(BF16)
        d_left = jnp.concatenate(
            [d_query[..., :q_cols], jnp.where(first_core, d_key, d_value)], axis=-1
        )
        d_right = jnp.concatenate(
            [d_query[..., q_cols:], jnp.where(first_core, d_value, d_key)], axis=-1
        )
        first_left = dot("bld,ble->de", h1, d_left)
        first_right = dot("bld,ble->de", h1, d_right)
        d_h1 = dot("ble,de->bld", d_left, first_own) + dot("ble,de->bld", d_right, first_other)
        d_input_norm, d_gain_input = jax.vjp(normed, x, gain_input)[1](d_h1)
        d_x = d_middle + d_input_norm
        input_grads.append(d_x.reshape(hi - lo, seqs, half_len, width))
        gain_grads = (d_gain_input, d_gain_attention, d_gain_feed, d_gain_feed_out)
        gain_grads = gain_grads + (d_gain_query, d_gain_key)
        now = (down_near, gate_near, up_near, out_sum, first_left, first_right)
        now = now + gain_grads
        grads = now if grads is None else tuple(a + b for a, b in zip(grads, now))

    down_near, gate_near, up_near, out_sum, first_left, first_right = grads[:6]
    gain_grads = grads[6:]

    gain_sums = jnp.concatenate([grad.reshape(chunks, -1) for grad in gain_grads], axis=-1)
    gain_sums = jnp.pad(gain_sums, ((0, 0), (0, first_cols - gain_sums.shape[1])))
    gain_sums = jnp.pad(gain_sums[:, None], ((0, 0), (0, 7), (0, 0)))
    first_left, first_right = (
        jnp.concatenate([grad.reshape(chunks, rows_in, first_cols), gain_sums], axis=1)
        for grad in (first_left, first_right)
    )
    last = (first_left + swap(first_right.astype(BF16)).astype(F32)).astype(BF16)
    last = sum_of(last.reshape((planes, depths) + last.shape[1:]), "fsdp")
    last, gate_near, up_near, down_near = together(last, gate_near, up_near, down_near)
    last = sum_of(last, "ctx")
    feed_grads = jnp.stack([gate_near, up_near, down_near], axis=2)
    feed_grads = trade_apart(feed_grads.reshape(4, 3, rows_in, units))
    feed_grads = feed_grads.astype(F32).transpose(1, 2, 0, 3)
    feed_grads = feed_grads.reshape(3, rows_in, 4 * units)[:, :, : 4 * units - spare]
    out_gate, out_up, out_down = feed_grads[0], feed_grads[1], feed_grads[2].T
    out_out = out_sum.T
    out_query = last[:rows_in, :q_cols]
    out_kv = last[:rows_in, q_cols:]
    gains_out = last[rows_in]
    kv_other = swap(out_kv)
    out_key = jnp.where(first_core, out_kv, kv_other)
    out_value = jnp.where(first_core, kv_other, out_kv)
    pieces = [gains_out[lo:hi] for lo, hi in zip(cuts, ends)]

    return (
        jnp.concatenate(outputs, axis=0),
        jnp.concatenate(input_grads, axis=0),
        pieces[0],
        out_query,
        out_key,
        out_value,
        pieces[4],
        pieces[5],
        out_out,
        pieces[1],
        pieces[2],
        out_gate,
        out_up,
        out_down,
        pieces[3],
    )


def solution(mesh):
    both = ("fsdp", "ctx")
    return jax.shard_map(
        local,
        mesh=mesh,
        in_specs=(
            P(None, "fsdp", "ctx", None),
            P(None, "fsdp", "ctx"),
            P(None, "fsdp", "ctx", None),
            P(both),
            P(both, "tp"),
            P(both, None),
            P(both, None),
            P(both),
            P(both),
            P("tp", both),
            P(both),
            P(both),
            P(both, "tp"),
            P(both, "tp"),
            P("tp", both),
            P(both),
        ),
        out_specs=(
            P(None, "fsdp", ("ctx", "tp"), None),
            P(None, "fsdp", ("ctx", "tp"), None),
            P(both),
            P(both, "tp"),
            P(both, None),
            P(both, None),
            P(both),
            P(both),
            P("tp", both),
            P(both),
            P(both),
            P(both, "tp"),
            P(both, "tp"),
            P("tp", both),
            P(both),
        ),
        check_vma=False,
    )
```

time: 667 us -> 610 us (0.915)
  local copies, waits for them, and re-layouts: 167 us -> 51.1 us
  waiting for transfers between devices: 179 us -> 268 us
  starting transfers between devices: 117 us -> 71.2 us
  other arithmetic: 54.2 us -> 83.5 us
  matrix products: 116 us -> 92.1 us
  blocking collectives: 7.9 us -> 31.1 us
  between operations: 16.5 us -> 2.81 us
    ppermute x78 -> x18, starting transfers between devices: 103 us -> 15.5 us  [cross(): return lax.ppermute(value, BOTH, [(i, i ^ mask) for i in range(count)])]
    ppermute x78 -> x18, waiting for transfers between devices: 117 us -> 204 us  [cross(): return lax.ppermute(value, BOTH, [(i, i ^ mask) for i in range(count)])]
    dynamic_update_slice x46 -> x0, local copies, waits for them, and re-layouts: 50.3 us -> none  [the longest x15 33.3 us: trade_axis(): lax.dynamic_update_index_in_dim(whole, cross(piece, axis, step), mine ^ s...]
    all_to_all x0 -> x11, starting transfers between devices: none -> 46.7 us  [the longest x4 15.7 us: sum_of(): lax.all_to_all(parts.astype(BF16), axis, 0, 0).astype(F32)]
    all_to_all x0 -> x11, waiting for transfers between devices: none -> 32.3 us  [the longest x3 27.8 us: trade(): return lax.all_to_all(value, BOTH, 0, 0, axis_index_groups=near_groups())]
    all_to_all x0 -> x1, blocking collectives: none -> 31.1 us  [trade(): return lax.all_to_all(value, BOTH, 0, 0, axis_index_groups=near_groups())]
    dot_general x24 -> x27, matrix products: 116 us -> 92.1 us  [dot(): return jnp.einsum(spec, left, right, preferred_element_type=F32)]
    select_n x0 -> x20, other arithmetic: none -> 18.1 us  [the longest x11 11 us: parted(): return (jnp.where(bit == 0, zero, one), jnp.where(bit == 0, one, zero))]
  transfers between devices with their start and end apart: 108 -> 44, of which waited for: 32 -> 26; matrix products, arithmetic and copies ran while one was open for 40% -> 21% of each run, Pallas kernels for 0% -> 0%
where the time goes in v2:
time: 610 us; the launch traced here: 600 us
  waiting for transfers between devices  268 us (44%)
  matrix products  92.1 us (15%)
  other arithmetic  83.5 us (14%)
  starting transfers between devices  71.2 us (12%)
  local copies, waits for them, and re-layouts  51.1 us (8%)
  blocking collectives  31.1 us (5%)
    ppermute x18, waiting for transfers between devices, cross(): return lax.ppermute(value, BOTH, [(i, i ^ mask) for i in range(count)])  204 us
    dot_general x27, matrix products, dot(): return jnp.einsum(spec, left, right, preferred_element_type=F32)  92.1 us
    all_to_all x1, blocking collectives, trade(): return lax.all_to_all(value, BOTH, 0, 0, axis_index_groups=near_groups())  31.1 us
    all_to_all x3, waiting for transfers between devices, trade(): return lax.all_to_all(value, BOTH, 0, 0, axis_index_groups=near_groups())  27.8 us
    ppermute x11, waiting for transfers between devices, swap(): return lax.ppermute(value, 'tp', [(0, 1), (1, 0)])  17.1 us
    unnamed x231, local copies, waits for them, and re-layouts  16.5 us
    all_to_all x4, starting transfers between devices, sum_of(): lax.all_to_all(parts.astype(BF16), axis, 0, 0).astype(F32)  15.7 us
    ppermute x18, starting transfers between devices, cross(): return lax.ppermute(value, BOTH, [(i, i ^ mask) for i in range(count)])  15.5 us
  transfers between devices with their start and end apart: 44, of which 26 were waited for; matrix products, arithmetic and copies ran while one was open for 21% of the time, Pallas kernels for 0%

profile of v2, /device:TPU:0, one launch (start us, length us, event | category | flops | bytes accessed | tf_op | source)
XLA Modules:
  0.0 599.9 jit_solution(3217132202980289514)
XLA Ops:
  1.6 4.1 concatenate.178
  11.9 3.6 broadcast_select_fusion.3
  15.6 3.1 collective-permute-start
  20.5 5.3 all-to-all-start
  28.6 2.9 collective-permute-done.1
  31.5 12.1 %collective-permute-done.2 = bf16[3,72,896]{2,1,0:T(8,128)(2,1)} collective-permute-done((bf16[3,72,896]{2,1,0:T(8,128)(2,1)S(1)}, bf16[3,72,896]{2,1,0:T(8,128)(2,1)}, u32[]{:S(2)}, u32[]{:S(2)}) %collective-permute-start.2) | collective-permute-done | bytes 387104 | tf_op jit(solution)/shard_map/ppermute | solution.py:63
  45.2 2.4 broadcast_in_dim.49
  47.6 3.6 all-to-all-start.1
  57.9 19.1 %collective-permute-done.3 = bf16[2,2,72,896]{3,2,1,0:T(8,128)(2,1)} collective-permute-done((bf16[2,2,72,896]{3,2,1,0:T(8,128)(2,1)}, bf16[2,2,72,896]{3,2,1,0:T(8,128)(2,1)}, u32[]{:S(2)}, u32[]{:S(2)}) %collective-permute-start.3) | collective-permute-done | bytes 516128 | tf_op jit(solution)/shard_map/ppermute | solution.py:63
  84.0 5.2 all-to-all-start.2
  90.0 2.4 fusion.66
  92.5 15.9 %collective-permute-done.5 = bf16[2,2,72,896]{3,2,1,0:T(8,128)(2,1)S(1)} collective-permute-done((bf16[2,2,72,896]{3,2,1,0:T(8,128)(2,1)}, bf16[2,2,72,896]{3,2,1,0:T(8,128)(2,1)S(1)}, u32[]{:S(2)}, u32[]{:S(2)}) %collective-permute-start.5) | collective-permute-done | bytes 516128 | tf_op jit(solution)/shard_map/ppermute | solution.py:63
  118.5 3.0 collective-permute-start.8
  127.7 3.8 all-to-all-start.3
  136.1 20.3 %collective-permute-done.10 = bf16[2,4,72,896]{3,2,1,0:T(8,128)(2,1)} collective-permute-done((bf16[2,4,72,896]{3,2,1,0:T(8,128)(2,1)}, bf16[2,4,72,896]{3,2,1,0:T(8,128)(2,1)}, u32[]{:S(2)}, u32[]{:S(2)}) %collective-permute-start.10) | collective-permute-done | bytes 1032224 | tf_op jit(solution)/shard_map/ppermute | solution.py:63
  166.6 18.0 %collective-permute-done.12 = bf16[2,2,72,896]{3,2,1,0:T(8,128)(2,1)S(1)} collective-permute-done((bf16[2,2,72,896]{3,2,1,0:T(8,128)(2,1)}, bf16[2,2,72,896]{3,2,1,0:T(8,128)(2,1)S(1)}, u32[]{:S(2)}, u32[]{:S(2)}) %collective-permute-start.12) | collective-permute-done | bytes 516128 | tf_op jit(solution)/shard_map/ppermute | solution.py:63
  190.5 3.8 all-to-all-start.4
  194.8 24.6 %collective-permute-done.13 = bf16[2,4,72,896]{3,2,1,0:T(8,128)(2,1)S(1)} collective-permute-done((bf16[2,4,72,896]{3,2,1,0:T(8,128)(2,1)}, bf16[2,4,72,896]{3,2,1,0:T(8,128)(2,1)S(1)}, u32[]{:S(2)}, u32[]{:S(2)}) %collective-permute-start.13) | collective-permute-done | bytes 1032224 | tf_op jit(solution)/shard_map/ppermute | solution.py:63
  222.6 4.3 collective-permute-done.14
  227.4 5.5 fusion.133
  232.9 8.3 %multiply_convert_fusion.1 = (bf16[2048,896]{1,0:T(8,128)(2,1)S(1)}, f32[2048,896]{1,0:T(8,128)}) fusion(f32[2048,896]{1,0:T(8,128)S(1)} %fusion.133, bf16[2048,1152]{1,0:T(8,128)(2,1)S(1)} %constant_dynamic-update-slice_fusion.5, bf16[1152,896]{1,0:T(8,128)(2,1)S(1)} %bitcast.435), kind=kOutput, calls=%fused_computation.14 | convolution fusion | flops 4246208512 | bytes 25133056 | tf_op jit(solution)/shard_map/td,du->tu/dot_general | solution.py:22
  241.2 5.7 convolution_convert_fusion
  247.4 4.4 collective-permute-done.15
  253.8 4.6 all-to-all-start.5
  259.1 27.6 %all-to-all-done.5 = bf16[4,256,1152]{2,1,0:T(8,128)(2,1)} async-done(((bf16[4,256,1152]{2,1,0:T(8,128)(2,1)}), bf16[4,256,1152]{2,1,0:T(8,128)(2,1)}, u32[]{:S(2)}, u32[]{:S(2)}) %all-to-all-start.5) | async-done | bytes 2359328 | tf_op jit(solution)/shard_map/all_to_all | solution.py:115
  290.6 31.1 %all_to_all.60 = bf16[4,256,1152]{2,1,0:T(8,128)(2,1)S(1)} all-to-all(bf16[4,256,1152]{2,1,0:T(8,128)(2,1)S(1)} %broadcast_in_dim.63), channel_id=1, replica_groups={{0,2,8,10},{4,6,12,14},{16,18,24,26},{20,22,28,30},{1,3,9,11},{5,7,13,1..., dimensions={0} | all-to-all | bytes 4718592 | tf_op jit(solution)/shard_map/all_to_all | solution.py:115
  321.8 4.5 collective-permute-done.16
  326.3 5.2 convolution_convert_fusion.3
  333.4 14.0 %multiply_convert_fusion = (bf16[2048,896]{1,0:T(8,128)(2,1)S(1)}, bf16[2048,896]{1,0:T(8,128)(2,1)}) fusion(f32[2048,896]{1,0:T(8,128)} %copy-done.104, f32[2048,896]{1,0:T(8,128)} %get-tuple-element.390, bf16[2048,1152]{1,0:T(8,128)(2,1)S(1)} %pad_maximum_fusion, bf16[1152,896]{1,0:T(8,128)(2,1)S(1)} %bitcast.438), kind=kOutput, calls=%fused_computation.13 | convolution fusion | flops 4271898624 | bytes 28803072 | tf_op jit(solution)/shard_map/td,du->tu/dot_general | solution.py:22
  347.5 10.8 %fusion.134 = f32[2048,1152]{1,0:T(8,128)} fusion(bf16[2048,896]{1,0:T(8,128)(2,1)} %get-tuple-element.103, bf16[1152,896]{1,0:T(8,128)(2,1)S(1)} %bitcast.434), kind=kOutput, calls=%fused_computation.352 | convolution fusion | flops 4227858432 | bytes 15171584 | tf_op jit(solution)/shard_map/tu,du->td/dot_general | solution.py:22
  358.3 8.5 %add_convert_fusion = bf16[2048,1152]{1,0:T(8,128)(2,1)S(1)} fusion(f32[2048,1152]{1,0:T(8,128)} %fusion.134, bf16[2048,896]{1,0:T(8,128)(2,1)S(1)} %get-tuple-element.107, bf16[1152,896]{1,0:T(8,128)(2,1)S(1)} %bitcast.436), kind=kOutput, calls=%fused_computation.4 | convolution fusion | flops 4232577024 | bytes 19890176 | tf_op jit(solution)/shard_map/tu,du->td/dot_general | solution.py:22
  370.2 6.3 %convolution_convert_fusion.2 = bf16[1152,896]{1,0:T(8,128)(2,1)} fusion(bf16[2048,1152]{1,0:T(8,128)(2,1)S(1)} %bitcast.443, bf16[2048,896]{1,0:T(8,128)(2,1)S(1)} %copy-done.103), kind=kOutput, calls=%fused_computation.25 | convolution fusion | flops 4228890624 | bytes 10452992 | tf_op jit(solution)/shard_map/td,tu->du/dot_general | solution.py:22
  378.5 4.6 all-to-all-start.7
  386.5 8.7 %convolution_convert_fusion.1 = bf16[1152,896]{1,0:T(8,128)(2,1)} fusion(bf16[2048,1152]{1,0:T(8,128)(2,1)} %copy-done.51, bf16[2048,896]{1,0:T(8,128)(2,1)S(1)} %copy-done.102), kind=kOutput, calls=%fused_computation.24 | convolution fusion | flops 4228890624 | bytes 10452992 | tf_op jit(solution)/shard_map/td,tu->du/dot_general | solution.py:22
  395.2 15.5 %collective-permute-done.19 = bf16[2,4,72,896]{3,2,1,0:T(8,128)(2,1)S(1)} collective-permute-done((bf16[2,4,72,896]{3,2,1,0:T(8,128)(2,1)S(1)}, bf16[2,4,72,896]{3,2,1,0:T(8,128)(2,1)S(1)}, u32[]{:S(2)}, u32[]{:S(2)}) %collective-permute-start.19) | collective-permute-done | bytes 1032224 | tf_op jit(solution)/shard_map/ppermute | solution.py:63
  428.5 15.9 %collective-permute-done.21 = bf16[2,2,72,896]{3,2,1,0:T(8,128)(2,1)} collective-permute-done((bf16[2,2,72,896]{3,2,1,0:T(8,128)(2,1)}, bf16[2,2,72,896]{3,2,1,0:T(8,128)(2,1)}, u32[]{:S(2)}, u32[]{:S(2)}) %collective-permute-start.21) | collective-permute-done | bytes 516128 | tf_op jit(solution)/shard_map/ppermute | solution.py:63
  451.2 21.1 %collective-permute-done.22 = bf16[2,2,72,896]{3,2,1,0:T(8,128)(2,1)S(1)} collective-permute-done((bf16[2,2,72,896]{3,2,1,0:T(8,128)(2,1)S(1)}, bf16[2,2,72,896]{3,2,1,0:T(8,128)(2,1)S(1)}, u32[]{:S(2)}, u32[]{:S(2)}) %collective-permute-start.22) | collective-permute-done | bytes 516128 | tf_op jit(solution)/shard_map/ppermute | solution.py:63
  480.4 4.3 all-to-all-start.8
  492.7 5.6 collective-permute-done.24
  498.3 8.7 %collective-permute-done.25 = bf16[2,128,512]{2,1,0:T(8,128)(2,1)} collective-permute-done((bf16[2,128,512]{2,1,0:T(8,128)(2,1)}, bf16[2,128,512]{2,1,0:T(8,128)(2,1)}, u32[]{:S(2)}, u32[]{:S(2)}) %collective-permute-start.25) | collective-permute-done | bytes 262176 | tf_op jit(solution)/shard_map/ppermute | solution.py:69
  514.4 3.0 fusion.38
  527.4 2.6 collective-permute-done.27
  531.8 3.9 all-to-all-start.9
  535.8 21.0 %collective-permute-done.28 = bf16[2,2,72,896]{3,2,1,0:T(8,128)(2,1)S(1)} collective-permute-done((bf16[2,2,72,896]{3,2,1,0:T(8,128)(2,1)S(1)}, bf16[2,2,72,896]{3,2,1,0:T(8,128)(2,1)S(1)}, u32[]{:S(2)}, u32[]{:S(2)}) %collective-permute-start.28) | collective-permute-done | bytes 516128 | tf_op jit(solution)/shard_map/ppermute | solution.py:63
  559.4 4.1 all-to-all-start.11
  573.8 3.5 all-to-all-start.10
  577.3 2.5 collective-permute-done.30
  579.9 14.3 %collective-permute-done.32 = bf16[3,72,896]{2,1,0:T(8,128)(2,1)S(1)} collective-permute-done((bf16[3,72,896]{2,1,0:T(8,128)(2,1)S(1)}, bf16[3,72,896]{2,1,0:T(8,128)(2,1)S(1)}, u32[]{:S(2)}, u32[]{:S(2)}) %collective-permute-start.32) | collective-permute-done | bytes 387104 | tf_op jit(solution)/shard_map/ppermute | solution.py:63
  (476 shorter events, 163.6 us)
Async XLA Ops:
  15.6 12.9 %collective-permute-start = (bf16[3,72,896]{2,1,0:T(8,128)(2,1)S(1)}, bf16[3,72,896]{2,1,0:T(8,128)(2,1)S(1)}, u32[]{:S(2)}, u32[]{:S(2)}) collective-permute-start(bf16[3,72,896]{2,1,0:T(8,128)(2,1)S(1)} %bitcast.451), channel_id=1, source_target_pairs={{0,2},{2,0},{4,6},{6,4},{8,10},{10,8},{12,14},{14,12},{16,18},{18,... | collective-permute-start | bytes 1161224 | tf_op jit(solution)/shard_map/ppermute | solution.py:63
  18.8 12.7 %collective-permute-start.1 = (bf16[3,72,896]{2,1,0:T(8,128)(2,1)S(1)}, bf16[3,72,896]{2,1,0:T(8,128)(2,1)}, u32[]{:S(2)}, u32[]{:S(2)}) collective-permute-start(bf16[3,72,896]{2,1,0:T(8,128)(2,1)S(1)} %bitcast.449), channel_id=1, source_target_pairs={{0,8},{2,10},{4,12},{6,14},{8,0},{10,2},{12,4},{14,6},{16,24},{18,... | collective-permute-start | bytes 1161224 | tf_op jit(solution)/shard_map/ppermute | solution.py:63
  20.4 23.2 %collective-permute-start.2 = (bf16[3,72,896]{2,1,0:T(8,128)(2,1)S(1)}, bf16[3,72,896]{2,1,0:T(8,128)(2,1)}, u32[]{:S(2)}, u32[]{:S(2)}) collective-permute-start(bf16[3,72,896]{2,1,0:T(8,128)(2,1)S(1)} %bitcast.450), channel_id=1, source_target_pairs={{0,10},{2,8},{4,14},{6,12},{8,2},{10,0},{12,6},{14,4},{16,26},{18,... | collective-permute-start | bytes 1161224 | tf_op jit(solution)/shard_map/ppermute | solution.py:63
  20.5 24.7 %all-to-all-start = ((bf16[4,80,768]{2,1,0:T(8,128)(2,1)}), bf16[4,80,768]{2,1,0:T(8,128)(2,1)}, u32[]{:S(2)}, u32[]{:S(2)}) async-start(bf16[4,80,768]{2,1,0:T(8,128)(2,1)} %broadcast_in_dim.48), calls=%async_computation | async-start | bytes 983040 | tf_op jit(solution)/shard_map/all_to_all | solution.py:240
  47.6 30.6 %all-to-all-start.1 = ((bf16[4,4,80,768]{3,2,1,0:T(8,128)(2,1)}), bf16[4,4,80,768]{3,2,1,0:T(8,128)(2,1)S(1)}, u32[]{:S(2)}, u32[]{:S(2)}) async-start(bf16[4,4,80,768]{3,2,1,0:T(8,128)(2,1)} %broadcast_in_dim.49), calls=%async_computation.1 | async-start | bytes 3932160 | tf_op jit(solution)/shard_map/all_to_all | solution.py:90
  52.9 24.1 %collective-permute-start.3 = (bf16[2,2,72,896]{3,2,1,0:T(8,128)(2,1)}, bf16[2,2,72,896]{3,2,1,0:T(8,128)(2,1)}, u32[]{:S(2)}, u32[]{:S(2)}) collective-permute-start(bf16[2,2,72,896]{3,2,1,0:T(8,128)(2,1)} %get-tuple-element.325), channel_id=1, source_target_pairs={{0,4},{2,6},{4,0},{6,2},{8,12},{10,14},{12,8},{14,10},{16,20},{18,... | collective-permute-start | bytes 1548296 | tf_op jit(solution)/shard_map/ppermute | solution.py:63
  78.3 31.3 %collective-permute-start.6 = (bf16[2,4,72,896]{3,2,1,0:T(8,128)(2,1)S(1)}, bf16[2,4,72,896]{3,2,1,0:T(8,128)(2,1)}, u32[]{:S(2)}, u32[]{:S(2)}) collective-permute-start(bf16[2,4,72,896]{3,2,1,0:T(8,128)(2,1)S(1)} %pad_maximum_fusion.10), channel_id=1, source_target_pairs={{0,16},{2,18},{4,20},{6,22},{8,24},{10,26},{12,28},{14,30},{16,0},... | collective-permute-start | bytes 3096584 | tf_op jit(solution)/shard_map/ppermute | solution.py:63
  80.0 28.4 %collective-permute-start.5 = (bf16[2,2,72,896]{3,2,1,0:T(8,128)(2,1)}, bf16[2,2,72,896]{3,2,1,0:T(8,128)(2,1)S(1)}, u32[]{:S(2)}, u32[]{:S(2)}) collective-permute-start(bf16[2,2,72,896]{3,2,1,0:T(8,128)(2,1)} %get-tuple-element.80), channel_id=1, source_target_pairs={{0,4},{2,6},{4,0},{6,2},{8,12},{10,14},{12,8},{14,10},{16,20},{18,... | collective-permute-start | bytes 1548296 | tf_op jit(solution)/shard_map/ppermute | solution.py:63
  81.4 31.1 %collective-permute-start.4 = (bf16[1152,768]{1,0:T(8,128)(2,1)}, bf16[1152,768]{1,0:T(8,128)(2,1)}, u32[]{:S(2)}, u32[]{:S(2)}) collective-permute-start(bf16[1152,768]{1,0:T(8,128)(2,1)} %bitcast.19), channel_id=1, source_target_pairs={{0,1},{1,0},{2,3},{3,2},{4,5},{5,4},{6,7},{7,6},{8,9},{9,8},{10,11... | collective-permute-start | bytes 5308424 | tf_op jit(solution)/shard_map/ppermute | solution.py:55
  82.2 30.3 %copy-start.65 = (f32[1152]{0:T(1024)}, f32[1152]{0:T(1024)S(1)}, u32[]{:S(2)}) copy-start(f32[1152]{0:T(1024)S(1)} %mul.616) | copy-start | bytes 13828
  82.4 32.6 %copy-start.78 = (f32[256]{0:T(256)}, f32[256]{0:T(256)S(1)}, u32[]{:S(2)}) copy-start(f32[256]{0:T(256)S(1)} %mul.626) | copy-start | bytes 3076
  84.0 32.4 %all-to-all-start.2 = ((bf16[4,72,512]{2,1,0:T(8,128)(2,1)}), bf16[4,72,512]{2,1,0:T(8,128)(2,1)S(1)}, u32[]{:S(2)}, u32[]{:S(2)}) async-start(bf16[4,72,512]{2,1,0:T(8,128)(2,1)} %broadcast_in_dim.57), calls=%async_computation.2 | async-start | bytes 589824 | tf_op jit(solution)/shard_map/all_to_all | solution.py:90
  116.5 16.3 %collective-permute-start.7 = (bf16[2,128,512]{2,1,0:T(8,128)(2,1)S(1)}, bf16[2,128,512]{2,1,0:T(8,128)(2,1)}, u32[]{:S(2)}, u32[]{:S(2)}) collective-permute-start(bf16[2,128,512]{2,1,0:T(8,128)(2,1)S(1)} %pad_maximum_fusion.21), channel_id=1, source_target_pairs={{0,2},{2,4},{4,6},{1,3},{3,5},{5,7},{8,10},{10,12},{12,14},{9,11},... | collective-permute-start | bytes 786440 | tf_op jit(solution)/shard_map/ppermute | solution.py:69
  118.5 14.3 %collective-permute-start.8 = (bf16[2,128,512]{2,1,0:T(8,128)(2,1)S(1)}, bf16[2,128,512]{2,1,0:T(8,128)(2,1)}, u32[]{:S(2)}, u32[]{:S(2)}) collective-permute-start(bf16[2,128,512]{2,1,0:T(8,128)(2,1)S(1)} %pad_maximum_fusion.21), channel_id=1, source_target_pairs={{0,4},{2,6},{1,5},{3,7},{8,12},{10,14},{9,13},{11,15},{16,20},{18,... | collective-permute-start | bytes 786440 | tf_op jit(solution)/shard_map/ppermute | solution.py:69
  124.0 32.4 %collective-permute-start.10 = (bf16[2,4,72,896]{3,2,1,0:T(8,128)(2,1)}, bf16[2,4,72,896]{3,2,1,0:T(8,128)(2,1)}, u32[]{:S(2)}, u32[]{:S(2)}) collective-permute-start(bf16[2,4,72,896]{3,2,1,0:T(8,128)(2,1)} %pad_maximum_fusion.11), channel_id=1, source_target_pairs={{0,16},{2,18},{4,20},{6,22},{8,24},{10,26},{12,28},{14,30},{16,0},... | collective-permute-start | bytes 3096584 | tf_op jit(solution)/shard_map/ppermute | solution.py:63
  127.7 33.2 %all-to-all-start.3 = ((bf16[4,4,72,512]{3,2,1,0:T(8,128)(2,1)}), bf16[4,4,72,512]{3,2,1,0:T(8,128)(2,1)S(1)}, u32[]{:S(2)}, u32[]{:S(2)}) async-start(bf16[4,4,72,512]{3,2,1,0:T(8,128)(2,1)} %broadcast_in_dim.58), calls=%async_computation.3 | async-start | bytes 2359296 | tf_op jit(solution)/shard_map/all_to_all | solution.py:90
  134.0 25.6 %collective-permute-start.9 = (bf16[2,384,512]{2,1,0:T(8,128)(2,1)S(1)}, bf16[2,384,512]{2,1,0:T(8,128)(2,1)S(1)}, u32[]{:S(2)}, u32[]{:S(2)}) collective-permute-start(bf16[2,384,512]{2,1,0:T(8,128)(2,1)S(1)} %pad_maximum_fusion.13), channel_id=1, source_target_pairs={{0,1},{1,0},{2,3},{3,2},{4,5},{5,4},{6,7},{7,6},{8,9},{9,8},{10,11... | collective-permute-start | bytes 2359304 | tf_op jit(solution)/shard_map/ppermute | solution.py:55
  160.9 23.7 %collective-permute-start.12 = (bf16[2,2,72,896]{3,2,1,0:T(8,128)(2,1)}, bf16[2,2,72,896]{3,2,1,0:T(8,128)(2,1)S(1)}, u32[]{:S(2)}, u32[]{:S(2)}) collective-permute-start(bf16[2,2,72,896]{3,2,1,0:T(8,128)(2,1)} %get-tuple-element.93), channel_id=1, source_target_pairs={{0,4},{2,6},{4,0},{6,2},{8,12},{10,14},{12,8},{14,10},{16,20},{18,... | collective-permute-start | bytes 1548296 | tf_op jit(solution)/shard_map/ppermute | solution.py:63
  160.9 24.9 %collective-permute-start.11 = (bf16[1152,512]{1,0:T(8,128)(2,1)S(1)}, bf16[1152,512]{1,0:T(8,128)(2,1)S(1)}, u32[]{:S(2)}, u32[]{:S(2)}) collective-permute-start(bf16[1152,512]{1,0:T(8,128)(2,1)S(1)} %bitcast.411), channel_id=1, source_target_pairs={{0,1},{1,0},{2,3},{3,2},{4,5},{5,4},{6,7},{7,6},{8,9},{9,8},{10,11... | collective-permute-start | bytes 3538952 | tf_op jit(solution)/shard_map/ppermute | solution.py:55
  190.5 31.9 %all-to-all-start.4 = ((bf16[4,256,1152]{2,1,0:T(8,128)(2,1)}), bf16[4,256,1152]{2,1,0:T(8,128)(2,1)S(1)}, u32[]{:S(2)}, u32[]{:S(2)}) async-start(bf16[4,256,1152]{2,1,0:T(8,128)(2,1)} %broadcast_in_dim.61), calls=%async_computation.4 | async-start | bytes 4718592 | tf_op jit(solution)/shard_map/all_to_all | solution.py:115
  194.4 25.0 %collective-permute-start.13 = (bf16[2,4,72,896]{3,2,1,0:T(8,128)(2,1)}, bf16[2,4,72,896]{3,2,1,0:T(8,128)(2,1)S(1)}, u32[]{:S(2)}, u32[]{:S(2)}) collective-permute-start(bf16[2,4,72,896]{3,2,1,0:T(8,128)(2,1)} %pad_maximum_fusion.12), channel_id=1, source_target_pairs={{0,16},{2,18},{4,20},{6,22},{8,24},{10,26},{12,28},{14,30},{16,0},... | collective-permute-start | bytes 3096584 | tf_op jit(solution)/shard_map/ppermute | solution.py:63
  222.4 4.5 collective-permute-start.14
  247.2 4.6 collective-permute-start.15
  253.8 32.9 %all-to-all-start.5 = ((bf16[4,256,1152]{2,1,0:T(8,128)(2,1)}), bf16[4,256,1152]{2,1,0:T(8,128)(2,1)}, u32[]{:S(2)}, u32[]{:S(2)}) async-start(bf16[4,256,1152]{2,1,0:T(8,128)(2,1)} %bitcast.38), calls=%async_computation.5 | async-start | bytes 4718592 | tf_op jit(solution)/shard_map/all_to_all | solution.py:115
  259.1 29.9 %copy-start.32 = (bf16[2,1,256,1152]{3,2,1,0:T(8,128)(2,1)S(1)}, bf16[2,1,256,1152]{3,2,1,0:T(8,128)(2,1)}, u32[]{:S(2)}) copy-start(bf16[2,1,256,1152]{3,2,1,0:T(8,128)(2,1)} %param.18) | copy-start | bytes 3538948
  290.6 35.7 %copy-start.106 = (bf16[2048,896]{1,0:T(8,128)(2,1)S(1)}, bf16[2048,896]{1,0:T(8,128)(2,1)}, u32[]{:S(2)}) copy-start(bf16[2048,896]{1,0:T(8,128)(2,1)} %copy-done.105) | copy-start | bytes 11010052
  321.7 4.5 collective-permute-start.16
  332.1 34.8 %collective-permute-start.17 = (bf16[2,4,72,896]{3,2,1,0:T(8,128)(2,1)S(1)}, bf16[2,4,72,896]{3,2,1,0:T(8,128)(2,1)S(1)}, u32[]{:S(2)}, u32[]{:S(2)}) collective-permute-start(bf16[2,4,72,896]{3,2,1,0:T(8,128)(2,1)S(1)} %bitcast.444), channel_id=1, source_target_pairs={{0,16},{2,18},{4,20},{6,22},{8,24},{10,26},{12,28},{14,30},{16,0},... | collective-permute-start | bytes 3096584 | tf_op jit(solution)/shard_map/ppermute | solution.py:63
  368.3 8.2 %collective-permute-start.18 = (bf16[1024,1152]{1,0:T(8,128)(2,1)S(1)}, bf16[1024,1152]{1,0:T(8,128)(2,1)S(1)}, u32[]{:S(2)}, u32[]{:S(2)}) collective-permute-start(bf16[1024,1152]{1,0:T(8,128)(2,1)S(1)} %slice.298), channel_id=1, source_target_pairs={{0,1},{1,0},{2,3},{3,2},{4,5},{5,4},{6,7},{7,6},{8,9},{9,8},{10,11... | collective-permute-start | bytes 7077896 | tf_op jit(solution)/shard_map/ppermute | solution.py:55
  378.5 33.3 %all-to-all-start.7 = ((bf16[4,256,1152]{2,1,0:T(8,128)(2,1)}), bf16[4,256,1152]{2,1,0:T(8,128)(2,1)}, u32[]{:S(2)}, u32[]{:S(2)}) async-start(bf16[4,256,1152]{2,1,0:T(8,128)(2,1)} %bitcast.393), calls=%async_computation.7 | async-start | bytes 4718592 | tf_op jit(solution)/shard_map/all_to_all | solution.py:115
  385.7 24.9 %collective-permute-start.19 = (bf16[2,4,72,896]{3,2,1,0:T(8,128)(2,1)S(1)}, bf16[2,4,72,896]{3,2,1,0:T(8,128)(2,1)S(1)}, u32[]{:S(2)}, u32[]{:S(2)}) collective-permute-start(bf16[2,4,72,896]{3,2,1,0:T(8,128)(2,1)S(1)} %bitcast.445), channel_id=1, source_target_pairs={{0,16},{2,18},{4,20},{6,22},{8,24},{10,26},{12,28},{14,30},{16,0},... | collective-permute-start | bytes 3096584 | tf_op jit(solution)/shard_map/ppermute | solution.py:63
  419.1 25.3 %collective-permute-start.21 = (bf16[2,2,72,896]{3,2,1,0:T(8,128)(2,1)}, bf16[2,2,72,896]{3,2,1,0:T(8,128)(2,1)}, u32[]{:S(2)}, u32[]{:S(2)}) collective-permute-start(bf16[2,2,72,896]{3,2,1,0:T(8,128)(2,1)} %select_bitcast_fusion.2), channel_id=1, source_target_pairs={{0,4},{2,6},{4,0},{6,2},{8,12},{10,14},{12,8},{14,10},{16,20},{18,... | collective-permute-start | bytes 1548296 | tf_op jit(solution)/shard_map/ppermute | solution.py:63
  420.6 25.8 %collective-permute-start.20 = (bf16[2,4,72,896]{3,2,1,0:T(8,128)(2,1)}, bf16[2,4,72,896]{3,2,1,0:T(8,128)(2,1)}, u32[]{:S(2)}, u32[]{:S(2)}) collective-permute-start(bf16[2,4,72,896]{3,2,1,0:T(8,128)(2,1)} %bitcast.60), channel_id=1, source_target_pairs={{0,16},{2,18},{4,20},{6,22},{8,24},{10,26},{12,28},{14,30},{16,0},... | collective-permute-start | bytes 3096584 | tf_op jit(solution)/shard_map/ppermute | solution.py:63
  448.2 24.0 %collective-permute-start.22 = (bf16[2,2,72,896]{3,2,1,0:T(8,128)(2,1)S(1)}, bf16[2,2,72,896]{3,2,1,0:T(8,128)(2,1)S(1)}, u32[]{:S(2)}, u32[]{:S(2)}) collective-permute-start(bf16[2,2,72,896]{3,2,1,0:T(8,128)(2,1)S(1)} %select_bitcast_fusion.1), channel_id=1, source_target_pairs={{0,4},{2,6},{4,0},{6,2},{8,12},{10,14},{12,8},{14,10},{16,20},{18,... | collective-permute-start | bytes 1548296 | tf_op jit(solution)/shard_map/ppermute | solution.py:63
  473.2 5.7 collective-permute-start.26
  473.4 3.8 collective-permute-start.23
  480.4 27.8 %all-to-all-start.8 = ((bf16[4,4,72,512]{3,2,1,0:T(8,128)(2,1)}), bf16[4,4,72,512]{3,2,1,0:T(8,128)(2,1)}, u32[]{:S(2)}, u32[]{:S(2)}) async-start(bf16[4,4,72,512]{3,2,1,0:T(8,128)(2,1)} %bitcast.414), calls=%async_computation.8 | async-start | bytes 2359296 | tf_op jit(solution)/shard_map/all_to_all | solution.py:98
  486.6 11.7 %collective-permute-start.24 = (bf16[2,128,512]{2,1,0:T(8,128)(2,1)}, bf16[2,128,512]{2,1,0:T(8,128)(2,1)}, u32[]{:S(2)}, u32[]{:S(2)}) collective-permute-start(bf16[2,128,512]{2,1,0:T(8,128)(2,1)} %get-tuple-element.347), channel_id=1, source_target_pairs={{2,0},{4,2},{6,4},{3,1},{5,3},{7,5},{10,8},{12,10},{14,12},{11,9},... | collective-permute-start | bytes 786440 | tf_op jit(solution)/shard_map/ppermute | solution.py:69
  487.9 19.1 %collective-permute-start.25 = (bf16[2,128,512]{2,1,0:T(8,128)(2,1)}, bf16[2,128,512]{2,1,0:T(8,128)(2,1)}, u32[]{:S(2)}, u32[]{:S(2)}) collective-permute-start(bf16[2,128,512]{2,1,0:T(8,128)(2,1)} %get-tuple-element.348), channel_id=1, source_target_pairs={{4,0},{6,2},{5,1},{7,3},{12,8},{14,10},{13,9},{15,11},{20,16},{22,... | collective-permute-start | bytes 786440 | tf_op jit(solution)/shard_map/ppermute | solution.py:69
  526.0 4.0 collective-permute-start.27
  531.8 27.6 %all-to-all-start.9 = ((bf16[4,4,80,768]{3,2,1,0:T(8,128)(2,1)}), bf16[4,4,80,768]{3,2,1,0:T(8,128)(2,1)S(1)}, u32[]{:S(2)}, u32[]{:S(2)}) async-start(bf16[4,4,80,768]{3,2,1,0:T(8,128)(2,1)} %bitcast.405), calls=%async_computation.9 | async-start | bytes 3932160 | tf_op jit(solution)/shard_map/all_to_all | solution.py:98
  535.7 21.1 %collective-permute-start.28 = (bf16[2,2,72,896]{3,2,1,0:T(8,128)(2,1)S(1)}, bf16[2,2,72,896]{3,2,1,0:T(8,128)(2,1)S(1)}, u32[]{:S(2)}, u32[]{:S(2)}) collective-permute-start(bf16[2,2,72,896]{3,2,1,0:T(8,128)(2,1)S(1)} %select_bitcast_fusion), channel_id=1, source_target_pairs={{0,4},{2,6},{4,0},{6,2},{8,12},{10,14},{12,8},{14,10},{16,20},{18,... | collective-permute-start | bytes 1548296 | tf_op jit(solution)/shard_map/ppermute | solution.py:63
  559.4 12.7 %all-to-all-start.11 = ((bf16[4,72,512]{2,1,0:T(8,128)(2,1)}), bf16[4,72,512]{2,1,0:T(8,128)(2,1)}, u32[]{:S(2)}, u32[]{:S(2)}) async-start(bf16[4,72,512]{2,1,0:T(8,128)(2,1)} %convert_reduce_fusion.3), calls=%async_computation.11 | async-start | bytes 589824 | tf_op jit(solution)/shard_map/all_to_all | solution.py:98
  566.8 13.0 %collective-permute-start.30 = (bf16[3,72,896]{2,1,0:T(8,128)(2,1)}, bf16[3,72,896]{2,1,0:T(8,128)(2,1)S(1)}, u32[]{:S(2)}, u32[]{:S(2)}) collective-permute-start(bf16[3,72,896]{2,1,0:T(8,128)(2,1)} %select_bitcast_fusion.7), channel_id=1, source_target_pairs={{0,2},{2,0},{4,6},{6,4},{8,10},{10,8},{12,14},{14,12},{16,18},{18,... | collective-permute-start | bytes 1161224 | tf_op jit(solution)/shard_map/ppermute | solution.py:63
  568.8 11.0 %collective-permute-start.31 = (bf16[3,72,896]{2,1,0:T(8,128)(2,1)S(1)}, bf16[3,72,896]{2,1,0:T(8,128)(2,1)S(1)}, u32[]{:S(2)}, u32[]{:S(2)}) collective-permute-start(bf16[3,72,896]{2,1,0:T(8,128)(2,1)S(1)} %get-tuple-element.351), channel_id=1, source_target_pairs={{0,8},{2,10},{4,12},{6,14},{8,0},{10,2},{12,4},{14,6},{16,24},{18,... | collective-permute-start | bytes 1161224 | tf_op jit(solution)/shard_map/ppermute | solution.py:63
  570.3 23.8 %collective-permute-start.32 = (bf16[3,72,896]{2,1,0:T(8,128)(2,1)S(1)}, bf16[3,72,896]{2,1,0:T(8,128)(2,1)S(1)}, u32[]{:S(2)}, u32[]{:S(2)}) collective-permute-start(bf16[3,72,896]{2,1,0:T(8,128)(2,1)S(1)} %get-tuple-element.352), channel_id=1, source_target_pairs={{0,10},{2,8},{4,14},{6,12},{8,2},{10,0},{12,6},{14,4},{16,26},{18,... | collective-permute-start | bytes 1161224 | tf_op jit(solution)/shard_map/ppermute | solution.py:63
  573.8 23.2 %all-to-all-start.10 = ((bf16[4,80,768]{2,1,0:T(8,128)(2,1)}), bf16[4,80,768]{2,1,0:T(8,128)(2,1)S(1)}, u32[]{:S(2)}, u32[]{:S(2)}) async-start(bf16[4,80,768]{2,1,0:T(8,128)(2,1)} %convert_reduce_fusion.2), calls=%async_computation.10 | async-start | bytes 983040 | tf_op jit(solution)/shard_map/all_to_all | solution.py:98
  597.7 1.3 collective-permute-start.29
  (105 other events, 645.9 us)

commit v3 on v2

v3 whole, which is shorter than its diff:
```python
import jax
import jax.numpy as jnp
from jax import lax
from jax.experimental import pallas as pl
from jax.experimental.pallas import tpu as pltpu
from jax.sharding import PartitionSpec as P

HEAD_DIM = 256
WINDOW = 512

EPSILON = 1e-06
ROPE_BASE = 10000.0
SCORE_SCALE = 0.0625
MASKED = -1e30

SEGMENT_NUMBERS = 10

F32 = jnp.float32
BF16 = jnp.bfloat16


def dot(spec, left, right):
    return jnp.einsum(spec, left, right, preferred_element_type=F32)


def normed(values, gain):
    return values * lax.rsqrt(jnp.mean(values * values, axis=-1, keepdims=True) + EPSILON) * gain


def rotations(offsets, depth):
    middle = depth // 2
    inverse = ROPE_BASE ** (-2.0 * jnp.arange(middle, dtype=F32) / depth)
    angle_grid = offsets[..., None] * inverse
    return (jnp.cos(angle_grid), jnp.sin(angle_grid))


GELU_SCALE = 0.7978845608028654
GELU_CUBE = 0.044715


def feed_forward(rows, gate_w, up_w, down_w):
    z = dot("td,du->tu", rows, gate_w)
    up = dot("td,du->tu", rows, up_w)
    square = z * z
    t = jnp.tanh(GELU_SCALE * z * (1.0 + GELU_CUBE * square))
    half_one = 0.5 * (1.0 + t)
    gelu = z * half_one
    slope = half_one + 0.5 * z * (1.0 - t * t) * GELU_SCALE * (1.0 + 3.0 * GELU_CUBE * square)
    hidden = (gelu * up).astype(BF16)
    part = dot("tu,du->td", hidden, down_w).astype(BF16)
    return hidden, gelu.astype(BF16), (up * slope).astype(BF16), part


def contract(left, right, left_dim, right_dim):
    dims = (((left_dim,), (right_dim,)), ((), ()))
    return lax.dot_general(left, right, dims, preferred_element_type=F32)


def normed_back(values, gain, grad):
    scale = lax.rsqrt(jnp.mean(values * values, axis=-1, keepdims=True) + EPSILON)
    inner = gain * grad
    along = jnp.mean(values * inner, axis=-1, keepdims=True)
    d_values = scale * inner - values * (scale * scale * scale) * along
    return d_values, jnp.sum(grad * values * scale, axis=0, keepdims=True)


def turned(values, cosines, sines):
    middle = values.shape[-1] // 2
    first, second = values[:, :middle], values[:, middle:]
    return jnp.concatenate(
        [first * cosines - second * sines, second * cosines + first * sines], axis=-1
    )


def turned_back(values, cosines, sines):
    return turned(values, cosines, -sines)


def head(at):
    return slice(at * HEAD_DIM, (at + 1) * HEAD_DIM)


def project_kernel(core, x, own, other, gain_in, gain_q, gain_k, cosines, sines, *outs):
    h1, raw, query_rot, key_full, pair = outs
    cos, sin = cosines[...], sines[...]
    low = normed(x[...].astype(F32), gain_in[...]).astype(BF16)
    h1[...] = low
    q_cols = own.shape[1] - HEAD_DIM
    left, right = contract(low, own[...], 1, 0), contract(low, other[...], 1, 0)
    first = core[0] == 0
    key = jnp.where(first, left[:, q_cols:], right[:, q_cols:])
    value = jnp.where(first, right[:, q_cols:], left[:, q_cols:])
    key_full[...] = key
    pair[:, :HEAD_DIM] = turned(normed(key, gain_k[...]), cos, sin).astype(BF16)
    pair[:, HEAD_DIM:] = value.astype(BF16)
    raw[:, :q_cols] = left[:, :q_cols]
    raw[:, q_cols:] = right[:, :q_cols]
    for at in range(raw.shape[1] // HEAD_DIM):
        turn = turned(normed(raw[:, head(at)], gain_q[...]), cos, sin)
        query_rot[:, head(at)] = turn.astype(BF16)


def allowed_pairs(tokens_at, keys_at, starts):
    t, u, begin = tokens_at[...], keys_at[...], starts[...]
    return (u <= t) & (t - u < WINDOW) & (u >= begin)


def probabilities(query, keys, allowed):
    scores = jnp.where(allowed, contract(query, keys, 1, 1) * SCORE_SCALE, MASKED)
    lifted = jnp.exp(scores - jnp.max(scores, axis=-1, keepdims=True))
    return lifted / jnp.sum(lifted, axis=-1, keepdims=True)


def attend_kernel(tokens_at, keys_at, starts, query_rot, seen, x, own, other, gain_a, gain_f, *outs):
    mixed, attention, middle, h2 = outs
    allowed = allowed_pairs(tokens_at, keys_at, starts)
    keys, values = seen[0, :, :HEAD_DIM], seen[0, :, HEAD_DIM:]
    for at in range(query_rot.shape[1] // HEAD_DIM):
        prob = probabilities(query_rot[:, head(at)], keys, allowed).astype(BF16)
        mixed[:, head(at)] = contract(prob, values, 1, 0).astype(BF16)
    q_cols = own.shape[1]
    result = contract(mixed[:, :q_cols], own[...], 1, 1)
    result = result + contract(mixed[:, q_cols:], other[...], 1, 1)
    attention[...] = result
    mid = x[...].astype(F32) + normed(result, gain_a[...])
    middle[...] = mid
    h2[...] = normed(mid, gain_f[...]).astype(BF16)


def attend_back_kernel(tokens_at, keys_at, starts, query_rot, seen, own, other, *rest):
    gain_a, gain_f, gain_q, cosines, sines, parts, middle, attention, dy, raw = rest[:10]
    d_middle, d_attention, d_query, d_near, d_far, d_gains, d_gain_q, d_mixed = rest[10:]

    @pl.when(pl.program_id(0) == 0)
    def _():
        d_gains[...] = jnp.zeros_like(d_gains)
        d_gain_q[...] = jnp.zeros_like(d_gain_q)

    d_h2 = parts[0].astype(F32)
    for at in range(1, parts.shape[0]):
        d_h2 = d_h2 + parts[at].astype(F32)
    d_mid, d_gain_f = normed_back(middle[...], gain_f[...], d_h2)
    d_mid = d_mid + dy[...].astype(F32)
    d_middle[...] = d_mid
    d_att, d_gain_a = normed_back(attention[...], gain_a[...], d_mid)
    d_gains[0:1, :] += d_gain_f
    d_gains[1:2, :] += d_gain_a
    d_att = d_att.astype(BF16)
    d_attention[...] = d_att
    q_cols = own.shape[1]
    d_mixed[:, :q_cols] = contract(d_att, own[...], 1, 0).astype(BF16)
    d_mixed[:, q_cols:] = contract(d_att, other[...], 1, 0).astype(BF16)
    allowed = allowed_pairs(tokens_at, keys_at, starts)
    keys, values = seen[0, :, :HEAD_DIM], seen[0, :, HEAD_DIM:]
    d_keys = jnp.zeros(keys.shape, F32)
    d_values = jnp.zeros(keys.shape, F32)
    for at in range(query_rot.shape[1] // HEAD_DIM):
        query, d_mix = query_rot[:, head(at)], d_mixed[:, head(at)]
        prob = probabilities(query, keys, allowed)
        d_prob = contract(d_mix, values, 1, 1)
        delta = jnp.sum(prob * d_prob, axis=-1, keepdims=True)
        d_raw = (prob * (d_prob - delta) * SCORE_SCALE).astype(BF16)
        d_keys = d_keys + contract(d_raw, query, 0, 0)
        d_values = d_values + contract(prob.astype(BF16), d_mix, 0, 0)
        d_rot = turned_back(contract(d_raw, keys, 1, 0), cosines[...], sines[...])
        d_full, d_gain = normed_back(raw[:, head(at)], gain_q[...], d_rot)
        d_query[:, head(at)] = d_full.astype(BF16)
        d_gain_q[0:1, :] += d_gain
    side = keys.shape[0] // 2
    d_near[0, :, :HEAD_DIM] = d_keys[:side]
    d_near[0, :, HEAD_DIM:] = d_values[:side]
    d_far[0, :, :HEAD_DIM] = d_keys[side:].astype(BF16)
    d_far[0, :, HEAD_DIM:] = d_values[side:].astype(BF16)


def project_back_kernel(core, d_kv, key_full, d_query, h1, x, own, other, *rest):
    gain_in, gain_k, cosines, sines, d_middle = rest[:5]
    input_grad, kv_left, kv_right, d_gain_in, d_gain_k = rest[5:]
    d_rot = turned_back(d_kv[:, :HEAD_DIM], cosines[...], sines[...])
    d_key, d_gain = normed_back(key_full[...], gain_k[...], d_rot)
    d_gain_k[...] = jnp.broadcast_to(d_gain, d_gain_k.shape)
    d_key, d_value = d_key.astype(BF16).astype(F32), d_kv[:, HEAD_DIM:]
    first = core[0] == 0
    d_left = jnp.where(first, d_key, d_value).astype(BF16)
    d_right = jnp.where(first, d_value, d_key).astype(BF16)
    low = h1[...]
    kv_left[...] = contract(low, d_left, 0, 0)
    kv_right[...] = contract(low, d_right, 0, 0)
    q_cols = own.shape[1] - HEAD_DIM
    d_h1 = contract(d_query[:, :q_cols], own[:, :q_cols], 1, 1)
    d_h1 = d_h1 + contract(d_query[:, q_cols:], other[:, :q_cols], 1, 1)
    d_h1 = d_h1 + contract(d_left, own[:, q_cols:], 1, 1)
    d_h1 = d_h1 + contract(d_right, other[:, q_cols:], 1, 1)
    d_x, d_gain = normed_back(x[...].astype(F32), gain_in[...], d_h1)
    input_grad[...] = d_middle[...] + d_x
    d_gain_in[...] = jnp.broadcast_to(d_gain, d_gain_in.shape)


def feed_norm_kernel(gain, parts, middle, dy, layer_out, d_feed, d_gain):
    feed = parts[0].astype(F32)
    for at in range(1, parts.shape[0]):
        feed = feed + parts[at].astype(F32)
    layer_out[...] = (middle[...] + normed(feed, gain[...])).astype(BF16)
    d_values, d_row = normed_back(feed, gain[...], dy[...].astype(F32))
    d_feed[...] = d_values.astype(BF16)
    d_gain[...] = jnp.broadcast_to(d_row, d_gain.shape)


def run(kernel, outs, *values, grid=None, in_specs=None, out_specs=None, scratch=()):
    more = {}
    if grid is not None:
        more = dict(grid=grid, in_specs=in_specs, out_specs=out_specs)
    elif in_specs is not None:
        more = dict(in_specs=in_specs)
    return pl.pallas_call(
        kernel,
        out_shape=[jax.ShapeDtypeStruct(shape, dtype) for shape, dtype in outs],
        scratch_shapes=list(scratch),
        compiler_params=pltpu.CompilerParams(vmem_limit_bytes=48 * 1024 * 1024),
        cost_estimate=pl.CostEstimate(flops=1, bytes_accessed=1, transcendentals=0),
        **more,
    )(*values)


def in_vmem(count):
    return [pl.BlockSpec(memory_space=pltpu.VMEM)] * count


def rows_spec(rows, width):
    return pl.BlockSpec((rows, width), lambda i: (i, 0))


def same_spec(*shape):
    return pl.BlockSpec(shape, lambda i: (0,) * len(shape))


def swap(value):
    return lax.ppermute(value, "tp", [(0, 1), (1, 0)])


BOTH = ("fsdp", "ctx")


def cross(value, mask):
    count = lax.axis_size("fsdp") * lax.axis_size("ctx")
    return lax.ppermute(value, BOTH, [(i, i ^ mask) for i in range(count)])


def shift(value, step):
    count = lax.axis_size("ctx")
    pairs = [(i, i + step) for i in range(count) if 0 <= i + step < count]
    return lax.ppermute(value, "ctx", pairs)


def together(*values):
    return lax.optimization_barrier(values)


def placed(own, other, bit, dim):
    first = jnp.where(bit == 0, own, other)
    second = jnp.where(bit == 0, other, own)
    return jnp.concatenate([first, second], axis=dim)


def parted(value, bit, dim):
    zero = lax.index_in_dim(value, 0, axis=dim, keepdims=False)
    one = lax.index_in_dim(value, 1, axis=dim, keepdims=False)
    return jnp.where(bit == 0, zero, one), jnp.where(bit == 0, one, zero)


def copies_to(value, axis):
    count = lax.axis_size(axis)
    return lax.all_to_all(jnp.broadcast_to(value[None], (count,) + value.shape), axis, 0, 0)


def gather_rows(value):
    return copies_to(copies_to(value, "ctx"), "fsdp")


def sum_of(parts, axis):
    return jnp.sum(lax.all_to_all(parts.astype(BF16), axis, 0, 0).astype(F32), axis=0)


def scatter_rows(value):
    return sum_of(sum_of(value, "fsdp"), "ctx")


def near_groups():
    planes, depths = lax.axis_size("fsdp"), lax.axis_size("ctx")
    return [
        [(f + x) * depths + c + z for x in (0, 1) for z in (0, 1)]
        for f in range(0, planes, 2)
        for c in range(0, depths, 2)
    ]


def trade(value):
    return lax.all_to_all(value, BOTH, 0, 0, axis_index_groups=near_groups())


def trade_apart(value):
    depths = lax.axis_size("ctx")
    x_bit, z_bit = lax.axis_index("fsdp") & 1, lax.axis_index("ctx") & 1
    low, high = parted(value.reshape((2, 2) + value.shape[1:]), x_bit, 0)
    (p0, p1), (p2, p3) = parted(low, z_bit, 0), parted(high, z_bit, 0)
    p1, p2, p3 = cross(p1, 1), cross(p2, depths), cross(p3, depths | 1)
    low = placed(p0[None], p1[None], z_bit, 0)
    high = placed(p2[None], p3[None], z_bit, 0)
    return placed(low[None], high[None], x_bit, 0).reshape(value.shape)


def far_bits():
    planes, depths = lax.axis_size("fsdp"), lax.axis_size("ctx")
    f_place, c_place = lax.axis_index("fsdp"), lax.axis_index("ctx")
    f_count, c_count = (planes - 1).bit_length(), (depths - 1).bit_length()
    c_bits = [(1 << k, (c_place >> k) & 1) for k in range(c_count - 1, 0, -1)]
    f_bits = [(depths << k, (f_place >> k) & 1) for k in range(f_count - 1, 0, -1)]
    return c_bits, f_bits


def gather_depth(value):
    c_bits, _ = far_bits()
    for mask, bit in c_bits[::-1]:
        value = placed(value, cross(value, mask), bit, 1)
    return value


def gather_plane(value):
    _, f_bits = far_bits()
    for mask, bit in f_bits[::-1]:
        value = placed(value, cross(value, mask), bit, 0)
    return value


def scatter_plane(value):
    _, f_bits = far_bits()
    for mask, bit in f_bits:
        halves = value.reshape((2, value.shape[0] // 2) + value.shape[1:])
        mine, other = parted(halves, bit, 0)
        value = (mine.astype(F32) + cross(other, mask).astype(F32)).astype(BF16)
    return value


def scatter_depth(value):
    c_bits, _ = far_bits()
    for mask, bit in c_bits:
        halves = value.reshape((2, 2, value.shape[1] // 2) + value.shape[2:])
        mine, other = parted(halves, bit, 1)
        value = (mine.astype(F32) + cross(other, mask).astype(F32)).astype(BF16)
    return value


def spread_start(rows):
    mine = trade(jnp.broadcast_to(rows[None], (4,) + rows.shape))
    return mine.reshape((-1,) + rows.shape[1:])


def spread(rows):
    mine = spread_start(rows)
    return jnp.concatenate([mine, swap(mine)], axis=0)


def collect_start(part):
    half = part.shape[0] // 2
    own = part[:half].astype(F32) + swap(part[half:]).astype(F32)
    return own.astype(BF16).reshape(4, half // 4, part.shape[1])


def local(
    tokens,
    segments,
    cotangent,
    norm_input,
    query_weight,
    key_weight,
    value_weight,
    norm_query,
    norm_key,
    out_weight,
    norm_attention,
    norm_feed,
    gate_weight,
    up_weight,
    down_weight,
    norm_feed_out,
):
    micros, seqs, block_len, width = tokens.shape
    planes = lax.axis_size("fsdp")
    depths = lax.axis_size("ctx")
    chunks = planes * depths
    ctx_place = lax.axis_index("ctx")
    tp_place = lax.axis_index("tp")
    first_core = tp_place == 0
    half_len = block_len // lax.axis_size("tp")
    back_blocks = -(-WINDOW // block_len)
    rows_in = norm_input.shape[0]
    small = norm_query.shape[0]
    heads_half = query_weight.shape[1] // HEAD_DIM
    q_cols = query_weight.shape[1]
    units = -(-gate_weight.shape[1] // (4 * 128)) * 128
    spare = 4 * units - gate_weight.shape[1]
    numbers = jnp.arange(SEGMENT_NUMBERS, dtype=jnp.int32)
    counts = jnp.sum((segments[..., None] == numbers).astype(F32), axis=2).astype(BF16)
    kv_shard = jnp.where(first_core, key_weight, value_weight)
    gains = (norm_input, norm_attention, norm_feed, norm_feed_out, norm_query, norm_key)
    gain_sizes = [gain.shape[0] for gain in gains]
    first_cols = q_cols + HEAD_DIM

    def row(value):
        return jnp.pad(value[None], ((0, 0), (0, first_cols - value.shape[0])))

    more = [row(gain) for gain in gains] + [row(counts.reshape(-1))]
    more = more + [jnp.zeros((1, first_cols), BF16)]
    first_pack = jnp.concatenate([query_weight, kv_shard], axis=1)
    first_pack = jnp.concatenate([first_pack] + more, axis=0)
    first_pack = jnp.broadcast_to(first_pack[None], (depths,) + first_pack.shape)
    first_pack, gate_weight, up_weight, down_weight, out_weight = together(
        first_pack, gate_weight, up_weight, down_weight, out_weight
    )
    first_pack = lax.all_to_all(first_pack, "ctx", 0, 0)

    feed_parts = jnp.stack([gate_weight, up_weight, down_weight.T], axis=0)
    feed_parts = jnp.pad(feed_parts, ((0, 0), (0, 0), (0, spare)))
    feed_parts = feed_parts.reshape(3, rows_in, 4, units).transpose(2, 0, 1, 3)
    feed_parts = trade_apart(feed_parts)
    first_pack, feed_parts = together(first_pack, feed_parts)
    counts_all = first_pack[:, rows_in + len(gains), : counts.size].astype(F32)
    counts_all = jnp.sum(counts_all, axis=0).reshape(counts.shape)

    feed_parts = feed_parts.reshape(2, 2, 3, rows_in, units)
    gate_near, up_near, down_near = (feed_parts[:, :, which] for which in range(3))
    gate_deep = gather_depth(gate_near)
    first_pack = copies_to(first_pack, "fsdp")
    first_pack, gate_deep, up_near, down_near, out_pack = together(
        first_pack, gate_deep, up_near, down_near, out_weight.T
    )

    first_pack = first_pack.reshape(chunks, rows_in + 8, first_cols)
    first_own = first_pack[:, :rows_in].reshape(width, first_cols)
    first_other = swap(first_own)
    gain_input, gain_attention, gain_feed, gain_feed_out, gain_query, gain_key = (
        first_pack[:, rows_in + at, :size].astype(F32).reshape(-1)
        for at, size in enumerate(gain_sizes)
    )
    out_pack = copies_to(out_pack, "ctx")
    up_deep = gather_depth(up_near)
    gate_w = gather_plane(gate_deep).reshape(width, units)

    half_at = tp_place * half_len
    seg_half = lax.dynamic_slice_in_dim(segments, half_at, half_len, 2)
    earlier = numbers < seg_half[..., None]
    starts = jnp.sum(jnp.where(earlier, counts_all[:, :, None, :], 0.0), axis=-1)
    starts = starts.astype(jnp.int32)
    token_place = ctx_place * block_len + half_at + jnp.arange(half_len, dtype=jnp.int32)
    cosines, sines = rotations((token_place - starts).astype(F32), HEAD_DIM)
    within = jnp.arange(half_len, dtype=jnp.int32)
    key_place = jnp.concatenate(
        [
            (ctx_place - back) * block_len + side * half_len + within
            for side in (tp_place, 1 - tp_place)
            for back in range(back_blocks + 1)
        ]
    )

    batch = micros * seqs
    rows = batch * half_len
    x_low = lax.dynamic_slice_in_dim(tokens, half_at, half_len, 2).reshape(rows, width)
    dy_low = lax.dynamic_slice_in_dim(cotangent, half_at, half_len, 2).reshape(rows, width)
    cos, sin = cosines.reshape(rows, -1), sines.reshape(rows, -1)
    starts = starts.reshape(rows, 1)
    core = tp_place.reshape(1)
    gains_wide = [
        gain[None]
        for gain in (gain_input, gain_attention, gain_feed, gain_feed_out, gain_query, gain_key)
    ]
    g_in, g_att, g_feed, g_out, g_query, g_key = gains_wide
    smem = [pl.BlockSpec(memory_space=pltpu.SMEM)]
    wide, cols_all = (rows, width), 2 * q_cols

    h1, query_raw, query_rot, key_full, pair = run(
        project_kernel,
        [(wide, BF16), ((rows, cols_all), F32), ((rows, cols_all), BF16)]
        + [((rows, HEAD_DIM), F32), ((rows, 2 * HEAD_DIM), BF16)],
        core, x_low, first_own, first_other, g_in, g_query, g_key, cos, sin,
        in_specs=smem + in_vmem(8),
    )
    pair, up_deep, gate_w, out_pack, down_near = together(
        pair, up_deep, gate_w, out_pack, down_near
    )
    down_deep = gather_depth(down_near)
    up_w = gather_plane(up_deep).reshape(width, units)
    out_own = copies_to(out_pack, "fsdp").reshape(width, q_cols)
    pair = pair.reshape(batch, half_len, 2 * HEAD_DIM)
    mine = jnp.concatenate(
        [pair] + [shift(pair, back) for back in range(1, back_blocks + 1)], axis=1
    )
    seen = jnp.concatenate([mine, swap(mine)], axis=1)
    seen, up_w, out_own, down_deep = together(seen, up_w, out_own, down_deep)
    out_other = swap(out_own)
    down_w = gather_plane(down_deep).reshape(width, units)
    span = seen.shape[1]
    token_rows, key_cols = token_place[:, None], key_place[None]
    place_specs = [same_spec(half_len, 1), same_spec(1, span), rows_spec(half_len, 1)]
    seen_spec = pl.BlockSpec((1, span, 2 * HEAD_DIM), lambda i: (i, 0, 0))
    row_spec, col_spec = rows_spec(half_len, width), rows_spec(half_len, cols_all)
    out_specs = [same_spec(width, q_cols)] * 2
    mixed, attention, middle, h2 = run(
        attend_kernel,
        [((rows, cols_all), BF16), (wide, F32), (wide, F32), (wide, BF16)],
        token_rows, key_cols, starts, query_rot, seen, x_low, out_own, out_other, g_att, g_feed,
        grid=(batch,),
        in_specs=place_specs
        + [col_spec, seen_spec, row_spec]
        + out_specs
        + [same_spec(1, width)] * 2,
        out_specs=[col_spec] + [row_spec] * 3,
    )

    h2_mine, down_w = together(spread_start(h2), down_w)
    h2_all = jnp.concatenate([h2_mine, swap(h2_mine)], axis=0)
    hidden, by_up, by_gate, part = feed_forward(h2_all, gate_w, up_w, down_w)
    feed_parts = trade(collect_start(part))
    layer_out, d_feed, d_gain_out = run(
        feed_norm_kernel,
        [(wide, BF16), (wide, BF16), ((8, width), F32)],
        g_out, feed_parts, middle, dy_low,
    )
    d_feed_all = spread(d_feed)
    grad_down = dot("td,tu->du", d_feed_all, hidden).astype(BF16)
    d_feed_all, grad_down = together(d_feed_all, grad_down)
    down_plane = scatter_plane(grad_down.reshape(planes, depths, rows_in, units))
    d_hidden = dot("td,du->tu", d_feed_all, down_w)
    d_gate = (d_hidden * by_gate.astype(F32)).astype(BF16)
    d_up = (d_hidden * by_up.astype(F32)).astype(BF16)
    grad_gate = dot("td,tu->du", h2_all, d_gate).astype(BF16)
    d_gate, d_up, grad_gate, down_plane = together(d_gate, d_up, grad_gate, down_plane)
    gate_plane = scatter_plane(grad_gate.reshape(planes, depths, rows_in, units))
    down_near = scatter_depth(down_plane)
    grad_up = dot("td,tu->du", h2_all, d_up).astype(BF16)
    d_h2_part = dot("tu,du->td", d_gate, gate_w) + dot("tu,du->td", d_up, up_w)
    d_h2_part, grad_up, gate_plane, down_near = together(
        d_h2_part.astype(BF16), grad_up, gate_plane, down_near
    )
    d_h2_part = collect_start(d_h2_part)
    gate_near = scatter_depth(gate_plane)
    up_plane = scatter_plane(grad_up.reshape(planes, depths, rows_in, units))
    d_h2_parts = trade(d_h2_part)
    d_h2_parts, gate_near, up_plane = together(d_h2_parts, gate_near, up_plane)
    up_near = scatter_depth(up_plane)

    side = span // 2
    near_spec = pl.BlockSpec((1, side, 2 * HEAD_DIM), lambda i: (i, 0, 0))
    turn_spec = rows_spec(half_len, HEAD_DIM // 2)
    d_middle, d_attention, d_query, d_near, d_far, d_gains, d_gain_query = run(
        attend_back_kernel,
        [(wide, F32), (wide, BF16), ((rows, cols_all), BF16)]
        + [((batch, side, 2 * HEAD_DIM), F32), ((batch, side, 2 * HEAD_DIM), BF16)]
        + [((8, width), F32), ((8, HEAD_DIM), F32)],
        token_rows, key_cols, starts, query_rot, seen, out_own, out_other,
        g_att, g_feed, g_query, cos, sin, d_h2_parts, middle, attention, dy_low, query_raw,
        grid=(batch,),
        in_specs=place_specs
        + [col_spec, seen_spec]
        + out_specs
        + [same_spec(1, width)] * 2
        + [same_spec(1, HEAD_DIM), turn_spec, turn_spec]
        + [pl.BlockSpec((4, half_len, width), lambda i: (0, i, 0))]
        + [row_spec] * 3
        + [col_spec],
        out_specs=[row_spec, row_spec, col_spec, near_spec, near_spec]
        + [same_spec(8, width), same_spec(8, HEAD_DIM)],
        scratch=[pltpu.VMEM((half_len, cols_all), BF16)],
    )
    d_near, d_far, d_query, d_attention, up_near = together(
        d_near, d_far, d_query, d_attention, up_near
    )
    feed_grads = jnp.stack([gate_near, up_near, down_near], axis=2)
    feed_grads = trade_apart(feed_grads.reshape(4, 3, rows_in, units))
    d_mine = d_near + swap(d_far).astype(F32)
    both_left = jnp.concatenate(
        [dot("td,te->de", d_attention, mixed[:, :q_cols])]
        + [dot("td,te->de", h1, d_query[:, :q_cols])],
        axis=1,
    )
    both_right = jnp.concatenate(
        [dot("td,te->de", d_attention, mixed[:, q_cols:]).astype(BF16)]
        + [dot("td,te->de", h1, d_query[:, q_cols:]).astype(BF16)],
        axis=1,
    )
    both = (both_left + swap(both_right).astype(F32)).astype(BF16)
    both = sum_of(both.reshape(planes, depths, rows_in, cols_all), "fsdp")
    d_kv = d_mine[:, :half_len]
    for back in range(1, back_blocks + 1):
        piece = d_mine[:, back * half_len : (back + 1) * half_len].astype(BF16)
        d_kv = d_kv + shift(piece, -back).astype(F32)
    d_kv, both, feed_grads = together(d_kv, both, feed_grads)
    both = sum_of(both, "ctx")
    input_grad, kv_left, kv_right, d_gain_in, d_gain_key = run(
        project_back_kernel,
        [(wide, F32), ((width, HEAD_DIM), F32), ((width, HEAD_DIM), F32)]
        + [((8, width), F32), ((8, HEAD_DIM), F32)],
        core, d_kv.reshape(rows, 2 * HEAD_DIM), key_full, d_query, h1, x_low,
        first_own, first_other, g_in, g_key, cos, sin, d_middle,
        in_specs=smem + in_vmem(12),
    )
    kv_left, kv_right, both = together(kv_left, kv_right, both)
    gain_grads = (d_gain_in[0], d_gains[1], d_gains[0], d_gain_out[0])
    gain_grads = gain_grads + (d_gain_query[0], d_gain_key[0])

    gain_sums = [
        jnp.pad(grad.reshape(chunks, 1, -1), ((0, 0), (0, 0), (0, HEAD_DIM - size)))
        for grad, size in zip(gain_grads, gain_sizes)
    ]
    gain_sums = gain_sums + [jnp.zeros((chunks, 8 - len(gains), HEAD_DIM), F32)]
    kv_left, kv_right = (
        jnp.concatenate([grad.reshape(chunks, rows_in, HEAD_DIM)] + gain_sums, axis=1)
        for grad in (kv_left, kv_right)
    )
    last = (kv_left + swap(kv_right.astype(BF16)).astype(F32)).astype(BF16)
    out_out, out_query = both[:, :q_cols].T, both[:, q_cols:]
    last = sum_of(sum_of(last.reshape((planes, depths) + last.shape[1:]), "fsdp"), "ctx")
    feed_grads = feed_grads.astype(F32).transpose(1, 2, 0, 3)
    feed_grads = feed_grads.reshape(3, rows_in, 4 * units)[:, :, : 4 * units - spare]
    out_gate, out_up, out_down = feed_grads[0], feed_grads[1], feed_grads[2].T
    out_kv = last[:rows_in]
    kv_other = swap(out_kv)
    out_key = jnp.where(first_core, out_kv, kv_other)
    out_value = jnp.where(first_core, kv_other, out_kv)
    pieces = [last[rows_in + at, :size] for at, size in enumerate(gain_sizes)]

    return (
        layer_out.reshape(micros, seqs, half_len, width),
        input_grad.reshape(micros, seqs, half_len, width),
        pieces[0],
        out_query,
        out_key,
        out_value,
        pieces[4],
        pieces[5],
        out_out,
        pieces[1],
        pieces[2],
        out_gate,
        out_up,
        out_down,
        pieces[3],
    )


def solution(mesh):
    both = ("fsdp", "ctx")
    return jax.shard_map(
        local,
        mesh=mesh,
        in_specs=(
            P(None, "fsdp", "ctx", None),
            P(None, "fsdp", "ctx"),
            P(None, "fsdp", "ctx", None),
            P(both),
            P(both, "tp"),
            P(both, None),
            P(both, None),
            P(both),
            P(both),
            P("tp", both),
            P(both),
            P(both),
            P(both, "tp"),
            P(both, "tp"),
            P("tp", both),
            P(both),
        ),
        out_specs=(
            P(None, "fsdp", ("ctx", "tp"), None),
            P(None, "fsdp", ("ctx", "tp"), None),
            P(both),
            P(both, "tp"),
            P(both, None),
            P(both, None),
            P(both),
            P(both),
            P("tp", both),
            P(both),
            P(both),
            P(both, "tp"),
            P(both, "tp"),
            P("tp", both),
            P(both),
        ),
        check_vma=False,
    )
```

time: 610 us -> 580 us (0.951)
  waiting for transfers between devices: 268 us -> 228 us
  Pallas kernels: 0 us -> 31 us
  other arithmetic: 83.5 us -> 60.9 us
  matrix products: 92.1 us -> 70.5 us
  starting transfers between devices: 71.2 us -> 89.3 us
    ppermute x18, waiting for transfers between devices: 204 us -> 135 us  [cross(): return lax.ppermute(value, BOTH, [(i, i ^ mask) for i in range(count)])]
    pallas_call x0 -> x5, Pallas kernels: none -> 31 us  [run(): pl.pallas_call(kernel, out_shape=[jax.ShapeDtypeStruct(shape, dtype) for...]
    dot_general x27 -> x13, matrix products: 92.1 us -> 70.5 us  [dot(): return jnp.einsum(spec, left, right, preferred_element_type=F32)]
    all_to_all x4, waiting for transfers between devices: 3.37 us -> 19.8 us  [sum_of(): lax.all_to_all(parts.astype(BF16), axis, 0, 0).astype(F32)]
    ppermute x4, waiting for transfers between devices: 14.3 us -> 24.3 us  [shift(): return lax.ppermute(value, 'ctx', pairs)]
    reduce_sum x12 -> x0, other arithmetic: 8.9 us -> none  [the longest x5 3.42 us: normed(): values * lax.rsqrt(jnp.mean(values * values, axis=-1, keepdims=True) + EP...]
    ppermute x18, starting transfers between devices: 15.5 us -> 24.1 us  [cross(): return lax.ppermute(value, BOTH, [(i, i ^ mask) for i in range(count)])]
    all_to_all x3, starting transfers between devices: 13.1 us -> 21.5 us  [trade(): return lax.all_to_all(value, BOTH, 0, 0, axis_index_groups=near_groups())]
  transfers between devices with their start and end apart: 44 -> 44, of which waited for: 26 -> 30; matrix products, arithmetic and copies ran while one was open for 21% -> 18% of each run, Pallas kernels for 0% -> 4%
where the time goes in v3:
time: 580 us; the launch traced here: 569 us
  waiting for transfers between devices  228 us (39%)
  starting transfers between devices  89.3 us (15%)
  matrix products  70.5 us (12%)
  other arithmetic  60.9 us (10%)
  local copies, waits for them, and re-layouts  56 us (10%)
  Pallas kernels  31 us (5%)
  blocking collectives  30.7 us (5%)
    ppermute x18, waiting for transfers between devices, cross(): return lax.ppermute(value, BOTH, [(i, i ^ mask) for i in range(count)])  135 us
    dot_general x13, matrix products, dot(): return jnp.einsum(spec, left, right, preferred_element_type=F32)  70.5 us
    pallas_call x5, Pallas kernels, run(): pl.pallas_call(kernel, out_shape=[jax.ShapeDtypeStruct(shape, dtype) for...  31 us
    all_to_all x1, blocking collectives, trade(): return lax.all_to_all(value, BOTH, 0, 0, axis_index_groups=near_groups())  30.7 us
    all_to_all x3, waiting for transfers between devices, trade(): return lax.all_to_all(value, BOTH, 0, 0, axis_index_groups=near_groups())  27 us
    ppermute x4, waiting for transfers between devices, shift(): return lax.ppermute(value, 'ctx', pairs)  24.3 us
    ppermute x18, starting transfers between devices, cross(): return lax.ppermute(value, BOTH, [(i, i ^ mask) for i in range(count)])  24.1 us
    ppermute x11, waiting for transfers between devices, swap(): return lax.ppermute(value, 'tp', [(0, 1), (1, 0)])  22.3 us
  transfers between devices with their start and end apart: 44, of which 30 were waited for; matrix products, arithmetic and copies ran while one was open for 18% of the time, Pallas kernels for 4%

profile of v3, /device:TPU:0, one launch (start us, length us, event | category | flops | bytes accessed | tf_op | source)
XLA Modules:
  0.0 568.8 jit_solution(8670031577249523553)
XLA Ops:
  15.7 3.6 broadcast_select_fusion.3
  26.2 5.3 all-to-all-start
  38.0 10.3 %collective-permute-done.2 = bf16[3,72,896]{2,1,0:T(8,128)(2,1)} collective-permute-done((bf16[3,72,896]{2,1,0:T(8,128)(2,1)}, bf16[3,72,896]{2,1,0:T(8,128)(2,1)}, u32[]{:S(2)}, u32[]{:S(2)}) %collective-permute-start.2) | collective-permute-done | bytes 387104 | tf_op jit(solution)/shard_map/ppermute | solution.py:246
  51.9 4.4 all-to-all-start.1
  58.9 22.5 %collective-permute-done.3 = bf16[2,2,72,896]{3,2,1,0:T(8,128)(2,1)S(1)} collective-permute-done((bf16[2,2,72,896]{3,2,1,0:T(8,128)(2,1)}, bf16[2,2,72,896]{3,2,1,0:T(8,128)(2,1)S(1)}, u32[]{:S(2)}, u32[]{:S(2)}) %collective-permute-start.3) | collective-permute-done | bytes 516128 | tf_op jit(solution)/shard_map/ppermute | solution.py:246
  93.6 4.9 all-to-all-start.2
  98.5 20.6 %collective-permute-done.5 = bf16[2,2,72,896]{3,2,1,0:T(8,128)(2,1)} collective-permute-done((bf16[2,2,72,896]{3,2,1,0:T(8,128)(2,1)S(1)}, bf16[2,2,72,896]{3,2,1,0:T(8,128)(2,1)}, u32[]{:S(2)}, u32[]{:S(2)}) %collective-permute-start.5) | collective-permute-done | bytes 516128 | tf_op jit(solution)/shard_map/ppermute | solution.py:246
  130.1 3.2 collective-permute-start.7
  133.3 4.0 collective-permute-start.8
  139.4 3.8 all-to-all-start.3
  143.2 4.9 collective-permute-done.7
  148.2 3.7 collective-permute-done.8
  156.1 6.0 %collective-permute-done.10 = bf16[2,4,72,896]{3,2,1,0:T(8,128)(2,1)} collective-permute-done((bf16[2,4,72,896]{3,2,1,0:T(8,128)(2,1)}, bf16[2,4,72,896]{3,2,1,0:T(8,128)(2,1)}, u32[]{:S(2)}, u32[]{:S(2)}) %collective-permute-start.10) | collective-permute-done | bytes 1032224 | tf_op jit(solution)/shard_map/ppermute | solution.py:246
  169.4 7.8 %shard_map.272 = (bf16[256,1024]{1,0:T(8,128)(2,1)S(1)}, f32[256,1152]{1,0:T(8,128)S(1)}, f32[256,1152]{1,0:T(8,128)S(1)}, bf16[256,1152]{1,0:T(8,128)(2,1)S(1)}) custom-call(s32[128,1]{1,0:T(8,128)S(1)} %iota_add_fusion.tokens_at, s32[1,768]{1,0:T(1,128)S(1)} %broadcast_in_dim.55.keys_at, s32[256,1]{1,0:T(8,128)S(1)} %copy.279.starts, ...), custom_call_target="tpu_custom_call" | custom-call | flops 1 | bytes 1 | tf_op jit(solution)/shard_map/pallas_call | solution.py:215
  181.6 13.2 %all-to-all-start.4 = ((bf16[4,256,1152]{2,1,0:T(8,128)(2,1)}), bf16[4,256,1152]{2,1,0:T(8,128)(2,1)S(1)}, u32[]{:S(2)}, u32[]{:S(2)}) async-start(bf16[4,256,1152]{2,1,0:T(8,128)(2,1)} %broadcast_in_dim.114), calls=%async_computation.4 | async-start | bytes 4718592 | tf_op jit(solution)/shard_map/all_to_all | solution.py:298
  196.2 23.3 %collective-permute-done.13 = bf16[2,4,72,896]{3,2,1,0:T(8,128)(2,1)S(1)} collective-permute-done((bf16[2,4,72,896]{3,2,1,0:T(8,128)(2,1)}, bf16[2,4,72,896]{3,2,1,0:T(8,128)(2,1)S(1)}, u32[]{:S(2)}, u32[]{:S(2)}) %collective-permute-start.13) | collective-permute-done | bytes 1032224 | tf_op jit(solution)/shard_map/ppermute | solution.py:246
  223.0 4.3 collective-permute-done.14
  227.7 5.5 fusion.35
  233.2 8.4 %multiply_convert_fusion.3 = (bf16[2048,896]{1,0:T(8,128)(2,1)S(1)}, f32[2048,896]{1,0:T(8,128)}) fusion(f32[2048,896]{1,0:T(8,128)S(1)} %fusion.35, bf16[2048,1152]{1,0:T(8,128)(2,1)S(1)} %constant_dynamic-update-slice_fusion.1, bf16[1152,896]{1,0:T(8,128)(2,1)S(1)} %bitcast.273), kind=kOutput, calls=%fused_computation.5 | convolution fusion | flops 4246208512 | bytes 25133056 | tf_op jit(solution)/shard_map/td,du->tu/dot_general | solution.py:23
  241.6 5.7 %convolution_convert_fusion = bf16[2048,1152]{1,0:T(8,128)(2,1)S(1)} fusion(bf16[2048,896]{1,0:T(8,128)(2,1)S(1)} %get-tuple-element.379, bf16[1152,896]{1,0:T(8,128)(2,1)S(1)} %bitcast.275), kind=kOutput, calls=%fused_computation.1 | convolution fusion | flops 4230217728 | bytes 10452992 | tf_op jit(solution)/shard_map/tu,du->td/dot_general | solution.py:23
  247.8 4.4 collective-permute-done.15
  254.3 3.8 all-to-all-start.5
  260.6 25.7 %all-to-all-done.5.parts = bf16[4,256,1152]{2,1,0:T(8,128)(2,1)S(1)} async-done(((bf16[4,256,1152]{2,1,0:T(8,128)(2,1)}), bf16[4,256,1152]{2,1,0:T(8,128)(2,1)S(1)}, u32[]{:S(2)}, u32[]{:S(2)}) %all-to-all-start.5) | async-done | bytes 2359328 | tf_op jit(solution)/shard_map/all_to_all | solution.py:298
  290.1 30.7 %all_to_all.60 = bf16[4,256,1152]{2,1,0:T(8,128)(2,1)S(1)} all-to-all(bf16[4,256,1152]{2,1,0:T(8,128)(2,1)S(1)} %broadcast_in_dim.115), channel_id=1, replica_groups={{0,2,8,10},{4,6,12,14},{16,18,24,26},{20,22,28,30},{1,3,9,11},{5,7,13,1..., dimensions={0} | all-to-all | bytes 4718592 | tf_op jit(solution)/shard_map/all_to_all | solution.py:298
  320.8 4.5 collective-permute-done.16
  325.3 5.2 convolution_convert_fusion.3
  332.6 13.5 %multiply_convert_fusion = (bf16[2048,896]{1,0:T(8,128)(2,1)S(1)}, bf16[2048,896]{1,0:T(8,128)(2,1)}) fusion(f32[2048,896]{1,0:T(8,128)} %copy-done.65, f32[2048,896]{1,0:T(8,128)} %get-tuple-element.380, bf16[2048,1152]{1,0:T(8,128)(2,1)S(1)} %pad_maximum_fusion, bf16[1152,896]{1,0:T(8,128)(2,1)S(1)} %bitcast.276), kind=kOutput, calls=%fused_computation.2 | convolution fusion | flops 4275568640 | bytes 28803072 | tf_op jit(solution)/shard_map/td,du->tu/dot_general | solution.py:23
  346.2 7.2 %convolution_convert_fusion.2 = bf16[1152,896]{1,0:T(8,128)(2,1)S(1)} fusion(bf16[2048,1152]{1,0:T(8,128)(2,1)S(1)} %bitcast.281, bf16[2048,896]{1,0:T(8,128)(2,1)} %get-tuple-element.117), kind=kOutput, calls=%fused_computation.16 | convolution fusion | flops 4228890624 | bytes 10452992 | tf_op jit(solution)/shard_map/td,tu->du/dot_general | solution.py:23
  356.4 3.4 collective-permute-start.19
  361.6 7.9 %fusion.36 = f32[2048,1152]{1,0:T(8,128)} fusion(bf16[2048,896]{1,0:T(8,128)(2,1)S(1)} %copy-done.64, bf16[1152,896]{1,0:T(8,128)(2,1)S(1)} %bitcast.272), kind=kOutput, calls=%fused_computation.193 | convolution fusion | flops 4227858432 | bytes 15171584 | tf_op jit(solution)/shard_map/tu,du->td/dot_general | solution.py:23
  369.5 8.2 %add_convert_fusion = bf16[2048,1152]{1,0:T(8,128)(2,1)S(1)} fusion(f32[2048,1152]{1,0:T(8,128)} %fusion.36, bf16[2048,896]{1,0:T(8,128)(2,1)S(1)} %get-tuple-element.118, bf16[1152,896]{1,0:T(8,128)(2,1)S(1)} %bitcast.274), kind=kOutput, calls=%fused_computation | convolution fusion | flops 4232577024 | bytes 19890176 | tf_op jit(solution)/shard_map/tu,du->td/dot_general | solution.py:23
  377.7 6.7 %convolution_convert_fusion.1 = bf16[1152,896]{1,0:T(8,128)(2,1)} fusion(bf16[2048,1152]{1,0:T(8,128)(2,1)S(1)} %bitcast.281, bf16[2048,896]{1,0:T(8,128)(2,1)S(1)} %get-tuple-element.118), kind=kOutput, calls=%fused_computation.15 | convolution fusion | flops 4228890624 | bytes 10452992 | tf_op jit(solution)/shard_map/td,tu->du/dot_general | solution.py:23
  385.9 4.5 collective-permute-done.20
  392.5 4.5 all-to-all-start.7
  401.0 33.1 %collective-permute-done.21 = bf16[2,2,72,896]{3,2,1,0:T(8,128)(2,1)S(1)} collective-permute-done((bf16[2,2,72,896]{3,2,1,0:T(8,128)(2,1)S(1)}, bf16[2,2,72,896]{3,2,1,0:T(8,128)(2,1)S(1)}, u32[]{:S(2)}, u32[]{:S(2)}) %collective-permute-start.21) | collective-permute-done | bytes 516128 | tf_op jit(solution)/shard_map/ppermute | solution.py:246
  440.2 13.3 %shard_map.274 = (f32[256,1152]{1,0:T(8,128)S(1)}, bf16[256,1152]{1,0:T(8,128)(2,1)S(1)}, bf16[256,1024]{1,0:T(8,128)(2,1)S(1)}, f32[2,384,512]{2,1,0:T(8,128)},...) custom-call(s32[128,1]{1,0:T(8,128)S(1)} %copy-done.24, s32[1,768]{1,0:T(1,128)S(1)} %copy-done.32, ...), custom_call_target="tpu_custom_call" | custom-call | flops 1 | bytes 1 | tf_op jit(solution)/shard_map/pallas_call | solution.py:215
  453.5 8.0 %collective-permute-done.23 = bf16[2,2,72,896]{3,2,1,0:T(8,128)(2,1)S(1)} collective-permute-done((bf16[2,2,72,896]{3,2,1,0:T(8,128)(2,1)S(1)}, bf16[2,2,72,896]{3,2,1,0:T(8,128)(2,1)S(1)}, u32[]{:S(2)}, u32[]{:S(2)}) %collective-permute-start.23) | collective-permute-done | bytes 516128 | tf_op jit(solution)/shard_map/ppermute | solution.py:246
  472.9 4.3 copy.287
  477.1 4.5 all-to-all-start.8
  492.4 6.4 %collective-permute-done.25 = bf16[2,128,512]{2,1,0:T(8,128)(2,1)S(1)} collective-permute-done((bf16[2,128,512]{2,1,0:T(8,128)(2,1)S(1)}, bf16[2,128,512]{2,1,0:T(8,128)(2,1)S(1)}, u32[]{:S(2)}, u32[]{:S(2)}) %collective-permute-start.25) | collective-permute-done | bytes 262176 | tf_op jit(solution)/shard_map/ppermute | solution.py:252
  498.8 9.3 %collective-permute-done.26 = bf16[2,128,512]{2,1,0:T(8,128)(2,1)S(1)} collective-permute-done((bf16[2,128,512]{2,1,0:T(8,128)(2,1)S(1)}, bf16[2,128,512]{2,1,0:T(8,128)(2,1)S(1)}, u32[]{:S(2)}, u32[]{:S(2)}) %collective-permute-start.26) | collective-permute-done | bytes 262176 | tf_op jit(solution)/shard_map/ppermute | solution.py:252
  513.9 3.5 all-to-all-start.9
  518.6 5.3 shard_map.275
  526.3 7.5 %all-to-all-done.9 = bf16[4,72,1024]{2,1,0:T(8,128)(2,1)S(1)} async-done(((bf16[4,72,1024]{2,1,0:T(8,128)(2,1)}), bf16[4,72,1024]{2,1,0:T(8,128)(2,1)S(1)}, u32[]{:S(2)}, u32[]{:S(2)}) %all-to-all-start.9) | async-done | bytes 589856 | tf_op jit(solution)/shard_map/all_to_all | solution.py:281
  542.1 3.5 all-to-all-start.10
  547.8 7.7 %all-to-all-done.10 = bf16[4,4,80,256]{3,2,1,0:T(8,128)(2,1)S(1)} async-done(((bf16[4,4,80,256]{3,2,1,0:T(8,128)(2,1)}), bf16[4,4,80,256]{3,2,1,0:T(8,128)(2,1)S(1)}, u32[]{:S(2)}, u32[]{:S(2)}) %all-to-all-start.10) | async-done | bytes 655392 | tf_op jit(solution)/shard_map/all_to_all | solution.py:281
  556.4 3.3 all-to-all-start.11
  559.7 3.6 slice_bitcast_fusion
  (358 shorter events, 157.4 us)
Async XLA Ops:
  0.6 58.2 %copy-start = (bf16[2,1,256,1152]{3,2,1,0:T(8,128)(2,1)S(1)}, bf16[2,1,256,1152]{3,2,1,0:T(8,128)(2,1)}, u32[]{:S(2)}) copy-start(bf16[2,1,256,1152]{3,2,1,0:T(8,128)(2,1)} %param.16) | copy-start | bytes 3538948
  20.1 13.0 %collective-permute-start = (bf16[3,72,896]{2,1,0:T(8,128)(2,1)}, bf16[3,72,896]{2,1,0:T(8,128)(2,1)S(1)}, u32[]{:S(2)}, u32[]{:S(2)}) collective-permute-start(bf16[3,72,896]{2,1,0:T(8,128)(2,1)} %bitcast.229), channel_id=1, source_target_pairs={{0,2},{2,0},{4,6},{6,4},{8,10},{10,8},{12,14},{14,12},{16,18},{18,... | collective-permute-start | bytes 1161224 | tf_op jit(solution)/shard_map/ppermute | solution.py:246
  23.9 14.0 %collective-permute-start.1 = (bf16[3,72,896]{2,1,0:T(8,128)(2,1)}, bf16[3,72,896]{2,1,0:T(8,128)(2,1)}, u32[]{:S(2)}, u32[]{:S(2)}) collective-permute-start(bf16[3,72,896]{2,1,0:T(8,128)(2,1)} %bitcast.228), channel_id=1, source_target_pairs={{0,8},{2,10},{4,12},{6,14},{8,0},{10,2},{12,4},{14,6},{16,24},{18,... | collective-permute-start | bytes 1161224 | tf_op jit(solution)/shard_map/ppermute | solution.py:246
  26.2 22.1 %collective-permute-start.2 = (bf16[3,72,896]{2,1,0:T(8,128)(2,1)}, bf16[3,72,896]{2,1,0:T(8,128)(2,1)}, u32[]{:S(2)}, u32[]{:S(2)}) collective-permute-start(bf16[3,72,896]{2,1,0:T(8,128)(2,1)} %bitcast.227), channel_id=1, source_target_pairs={{0,10},{2,8},{4,14},{6,12},{8,2},{10,0},{12,6},{14,4},{16,26},{18,... | collective-permute-start | bytes 1161224 | tf_op jit(solution)/shard_map/ppermute | solution.py:246
  26.2 23.6 %all-to-all-start = ((bf16[4,80,768]{2,1,0:T(8,128)(2,1)}), bf16[4,80,768]{2,1,0:T(8,128)(2,1)S(1)}, u32[]{:S(2)}, u32[]{:S(2)}) async-start(bf16[4,80,768]{2,1,0:T(8,128)(2,1)} %broadcast_in_dim.53), calls=%async_computation | async-start | bytes 983040 | tf_op jit(solution)/shard_map/all_to_all | solution.py:420
  51.9 31.7 %all-to-all-start.1 = ((bf16[4,4,80,768]{3,1,2,0:T(4,128)(2,1)}), bf16[4,4,80,768]{3,1,2,0:T(4,128)(2,1)}, u32[]{:S(2)}, u32[]{:S(2)}) async-start(bf16[4,4,80,768]{3,1,2,0:T(4,128)(2,1)} %broadcast_in_dim.54), calls=%async_computation.1 | async-start | bytes 3932160 | tf_op jit(solution)/shard_map/all_to_all | solution.py:273
  57.5 23.9 %collective-permute-start.3 = (bf16[2,2,72,896]{3,2,1,0:T(8,128)(2,1)}, bf16[2,2,72,896]{3,2,1,0:T(8,128)(2,1)S(1)}, u32[]{:S(2)}, u32[]{:S(2)}) collective-permute-start(bf16[2,2,72,896]{3,2,1,0:T(8,128)(2,1)} %get-tuple-element.341), channel_id=1, source_target_pairs={{0,4},{2,6},{4,0},{6,2},{8,12},{10,14},{12,8},{14,10},{16,20},{18,... | collective-permute-start | bytes 1548296 | tf_op jit(solution)/shard_map/ppermute | solution.py:246
  86.7 37.5 %copy-start.2 = (bf16[16,72,768]{2,1,0:T(8,128)(2,1)}, bf16[16,72,768]{2,1,0:T(8,128)(2,1)S(1)}, u32[]{:S(2)}) copy-start(bf16[16,72,768]{2,1,0:T(8,128)(2,1)S(1)} %slice.284) | copy-start | bytes 5308420
  86.7 37.5 %collective-permute-start.4 = (bf16[1152,768]{1,0:T(8,128)(2,1)S(1)}, bf16[1152,768]{1,0:T(8,128)(2,1)}, u32[]{:S(2)}, u32[]{:S(2)}) collective-permute-start(bf16[1152,768]{1,0:T(8,128)(2,1)S(1)} %bitcast.231), channel_id=1, source_target_pairs={{0,1},{1,0},{2,3},{3,2},{4,5},{5,4},{6,7},{7,6},{8,9},{9,8},{10,11... | collective-permute-start | bytes 5308424 | tf_op jit(solution)/shard_map/ppermute | solution.py:238
  87.7 33.6 %collective-permute-start.6 = (bf16[2,4,72,896]{3,2,1,0:T(8,128)(2,1)}, bf16[2,4,72,896]{3,2,1,0:T(8,128)(2,1)}, u32[]{:S(2)}, u32[]{:S(2)}) collective-permute-start(bf16[2,4,72,896]{3,2,1,0:T(8,128)(2,1)} %pad_maximum_fusion.9), channel_id=1, source_target_pairs={{0,16},{2,18},{4,20},{6,22},{8,24},{10,26},{12,28},{14,30},{16,0},... | collective-permute-start | bytes 3096584 | tf_op jit(solution)/shard_map/ppermute | solution.py:246
  89.5 29.6 %collective-permute-start.5 = (bf16[2,2,72,896]{3,2,1,0:T(8,128)(2,1)S(1)}, bf16[2,2,72,896]{3,2,1,0:T(8,128)(2,1)}, u32[]{:S(2)}, u32[]{:S(2)}) collective-permute-start(bf16[2,2,72,896]{3,2,1,0:T(8,128)(2,1)S(1)} %get-tuple-element.96), channel_id=1, source_target_pairs={{0,4},{2,6},{4,0},{6,2},{8,12},{10,14},{12,8},{14,10},{16,20},{18,... | collective-permute-start | bytes 1548296 | tf_op jit(solution)/shard_map/ppermute | solution.py:246
  93.6 36.1 %all-to-all-start.2 = ((bf16[4,72,512]{2,1,0:T(8,128)(2,1)}), bf16[4,72,512]{2,1,0:T(8,128)(2,1)}, u32[]{:S(2)}, u32[]{:S(2)}) async-start(bf16[4,72,512]{2,1,0:T(8,128)(2,1)} %broadcast_in_dim.59), calls=%async_computation.2 | async-start | bytes 589824 | tf_op jit(solution)/shard_map/all_to_all | solution.py:273
  129.7 39.7 %copy-start.12 = (bf16[256,1024]{1,0:T(8,128)(2,1)}, bf16[256,1024]{1,0:T(8,128)(2,1)S(1)}, u32[]{:S(2)}) copy-start(bf16[256,1024]{1,0:T(8,128)(2,1)S(1)} %get-tuple-element.94.query_rot) | copy-start | bytes 1572868
  129.7 32.4 %collective-permute-start.10 = (bf16[2,4,72,896]{3,2,1,0:T(8,128)(2,1)}, bf16[2,4,72,896]{3,2,1,0:T(8,128)(2,1)}, u32[]{:S(2)}, u32[]{:S(2)}) collective-permute-start(bf16[2,4,72,896]{3,2,1,0:T(8,128)(2,1)} %pad_maximum_fusion.10), channel_id=1, source_target_pairs={{0,16},{2,18},{4,20},{6,22},{8,24},{10,26},{12,28},{14,30},{16,0},... | collective-permute-start | bytes 3096584 | tf_op jit(solution)/shard_map/ppermute | solution.py:246
  130.1 23.7 %collective-permute-start.11 = (bf16[2,2,72,896]{3,2,1,0:T(8,128)(2,1)}, bf16[2,2,72,896]{3,2,1,0:T(8,128)(2,1)}, u32[]{:S(2)}, u32[]{:S(2)}) collective-permute-start(bf16[2,2,72,896]{3,2,1,0:T(8,128)(2,1)} %get-tuple-element.103), channel_id=1, source_target_pairs={{0,4},{2,6},{4,0},{6,2},{8,12},{10,14},{12,8},{14,10},{16,20},{18,... | collective-permute-start | bytes 1548296 | tf_op jit(solution)/shard_map/ppermute | solution.py:246
  130.1 18.1 %collective-permute-start.7 = (bf16[2,128,512]{2,1,0:T(8,128)(2,1)S(1)}, bf16[2,128,512]{2,1,0:T(8,128)(2,1)S(1)}, u32[]{:S(2)}, u32[]{:S(2)}) collective-permute-start(bf16[2,128,512]{2,1,0:T(8,128)(2,1)S(1)} %bitcast.244), channel_id=1, source_target_pairs={{0,2},{2,4},{4,6},{1,3},{3,5},{5,7},{8,10},{10,12},{12,14},{9,11},... | collective-permute-start | bytes 786440 | tf_op jit(solution)/shard_map/ppermute | solution.py:252
  133.3 18.5 %collective-permute-start.8 = (bf16[2,128,512]{2,1,0:T(8,128)(2,1)S(1)}, bf16[2,128,512]{2,1,0:T(8,128)(2,1)S(1)}, u32[]{:S(2)}, u32[]{:S(2)}) collective-permute-start(bf16[2,128,512]{2,1,0:T(8,128)(2,1)S(1)} %bitcast.245), channel_id=1, source_target_pairs={{0,4},{2,6},{1,5},{3,7},{8,12},{10,14},{9,13},{11,15},{16,20},{18,... | collective-permute-start | bytes 786440 | tf_op jit(solution)/shard_map/ppermute | solution.py:252
  139.4 27.0 %all-to-all-start.3 = ((bf16[4,4,72,512]{3,2,1,0:T(8,128)(2,1)}), bf16[4,4,72,512]{3,2,1,0:T(8,128)(2,1)S(1)}, u32[]{:S(2)}, u32[]{:S(2)}) async-start(bf16[4,4,72,512]{3,2,1,0:T(8,128)(2,1)} %broadcast_in_dim.60), calls=%async_computation.3 | async-start | bytes 2359296 | tf_op jit(solution)/shard_map/all_to_all | solution.py:273
  151.9 13.2 %collective-permute-start.9 = (bf16[2,384,512]{2,1,0:T(8,128)(2,1)S(1)}, bf16[2,384,512]{2,1,0:T(8,128)(2,1)S(1)}, u32[]{:S(2)}, u32[]{:S(2)}) collective-permute-start(bf16[2,384,512]{2,1,0:T(8,128)(2,1)S(1)} %pad_maximum_fusion.12), channel_id=1, source_target_pairs={{0,1},{1,0},{2,3},{3,2},{4,5},{5,4},{6,7},{7,6},{8,9},{9,8},{10,11... | collective-permute-start | bytes 2359304 | tf_op jit(solution)/shard_map/ppermute | solution.py:238
  166.4 3.0 collective-permute-start.12
  181.6 41.2 %all-to-all-start.4 = ((bf16[4,256,1152]{2,1,0:T(8,128)(2,1)}), bf16[4,256,1152]{2,1,0:T(8,128)(2,1)S(1)}, u32[]{:S(2)}, u32[]{:S(2)}) async-start(bf16[4,256,1152]{2,1,0:T(8,128)(2,1)} %broadcast_in_dim.114), calls=%async_computation.4 | async-start | bytes 4718592 | tf_op jit(solution)/shard_map/all_to_all | solution.py:298
  194.8 24.8 %collective-permute-start.13 = (bf16[2,4,72,896]{3,2,1,0:T(8,128)(2,1)}, bf16[2,4,72,896]{3,2,1,0:T(8,128)(2,1)S(1)}, u32[]{:S(2)}, u32[]{:S(2)}) collective-permute-start(bf16[2,4,72,896]{3,2,1,0:T(8,128)(2,1)} %pad_maximum_fusion.11), channel_id=1, source_target_pairs={{0,16},{2,18},{4,20},{6,22},{8,24},{10,26},{12,28},{14,30},{16,0},... | collective-permute-start | bytes 3096584 | tf_op jit(solution)/shard_map/ppermute | solution.py:246
  222.8 4.5 collective-permute-start.14
  247.6 4.6 collective-permute-start.15
  254.3 32.0 %all-to-all-start.5 = ((bf16[4,256,1152]{2,1,0:T(8,128)(2,1)}), bf16[4,256,1152]{2,1,0:T(8,128)(2,1)S(1)}, u32[]{:S(2)}, u32[]{:S(2)}) async-start(bf16[4,256,1152]{2,1,0:T(8,128)(2,1)} %bitcast.249), calls=%async_computation.5 | async-start | bytes 4718592 | tf_op jit(solution)/shard_map/all_to_all | solution.py:298
  290.1 35.2 %copy-start.67 = (bf16[2048,896]{1,0:T(8,128)(2,1)S(1)}, bf16[2048,896]{1,0:T(8,128)(2,1)}, u32[]{:S(2)}) copy-start(bf16[2048,896]{1,0:T(8,128)(2,1)} %copy-done.66) | copy-start | bytes 11010052
  320.8 4.5 collective-permute-start.16
  331.1 24.9 %collective-permute-start.17 = (bf16[2,4,72,896]{3,2,1,0:T(8,128)(2,1)S(1)}, bf16[2,4,72,896]{3,2,1,0:T(8,128)(2,1)S(1)}, u32[]{:S(2)}, u32[]{:S(2)}) collective-permute-start(bf16[2,4,72,896]{3,2,1,0:T(8,128)(2,1)S(1)} %bitcast.284), channel_id=1, source_target_pairs={{0,16},{2,18},{4,20},{6,22},{8,24},{10,26},{12,28},{14,30},{16,0},... | collective-permute-start | bytes 3096584 | tf_op jit(solution)/shard_map/ppermute | solution.py:246
  356.4 28.0 %collective-permute-start.19 = (bf16[2,2,72,896]{3,2,1,0:T(8,128)(2,1)S(1)}, bf16[2,2,72,896]{3,2,1,0:T(8,128)(2,1)S(1)}, u32[]{:S(2)}, u32[]{:S(2)}) collective-permute-start(bf16[2,2,72,896]{3,2,1,0:T(8,128)(2,1)S(1)} %select_bitcast_fusion.2), channel_id=1, source_target_pairs={{0,4},{2,6},{4,0},{6,2},{8,12},{10,14},{12,8},{14,10},{16,20},{18,... | collective-permute-start | bytes 1548296 | tf_op jit(solution)/shard_map/ppermute | solution.py:246
  360.0 25.4 %collective-permute-start.18 = (bf16[2,4,72,896]{3,2,1,0:T(8,128)(2,1)S(1)}, bf16[2,4,72,896]{3,2,1,0:T(8,128)(2,1)S(1)}, u32[]{:S(2)}, u32[]{:S(2)}) collective-permute-start(bf16[2,4,72,896]{3,2,1,0:T(8,128)(2,1)S(1)} %bitcast.282), channel_id=1, source_target_pairs={{0,16},{2,18},{4,20},{6,22},{8,24},{10,26},{12,28},{14,30},{16,0},... | collective-permute-start | bytes 3096584 | tf_op jit(solution)/shard_map/ppermute | solution.py:246
  385.9 4.6 collective-permute-start.20
  392.5 43.9 %all-to-all-start.7 = ((bf16[4,256,1152]{2,1,0:T(8,128)(2,1)}), bf16[4,256,1152]{2,1,0:T(8,128)(2,1)}, u32[]{:S(2)}, u32[]{:S(2)}) async-start(bf16[4,256,1152]{2,1,0:T(8,128)(2,1)} %bitcast.47), calls=%async_computation.7 | async-start | bytes 4718592 | tf_op jit(solution)/shard_map/all_to_all | solution.py:298
  398.7 36.4 %collective-permute-start.22 = (bf16[2,4,72,896]{3,2,1,0:T(8,128)(2,1)S(1)}, bf16[2,4,72,896]{3,2,1,0:T(8,128)(2,1)S(1)}, u32[]{:S(2)}, u32[]{:S(2)}) collective-permute-start(bf16[2,4,72,896]{3,2,1,0:T(8,128)(2,1)S(1)} %bitcast.283), channel_id=1, source_target_pairs={{0,16},{2,18},{4,20},{6,22},{8,24},{10,26},{12,28},{14,30},{16,0},... | collective-permute-start | bytes 3096584 | tf_op jit(solution)/shard_map/ppermute | solution.py:246
  399.4 34.7 %collective-permute-start.21 = (bf16[2,2,72,896]{3,2,1,0:T(8,128)(2,1)S(1)}, bf16[2,2,72,896]{3,2,1,0:T(8,128)(2,1)S(1)}, u32[]{:S(2)}, u32[]{:S(2)}) collective-permute-start(bf16[2,2,72,896]{3,2,1,0:T(8,128)(2,1)S(1)} %select_bitcast_fusion.1), channel_id=1, source_target_pairs={{0,4},{2,6},{4,0},{6,2},{8,12},{10,14},{12,8},{14,10},{16,20},{18,... | collective-permute-start | bytes 1548296 | tf_op jit(solution)/shard_map/ppermute | solution.py:246
  436.5 25.1 %collective-permute-start.23 = (bf16[2,2,72,896]{3,2,1,0:T(8,128)(2,1)S(1)}, bf16[2,2,72,896]{3,2,1,0:T(8,128)(2,1)S(1)}, u32[]{:S(2)}, u32[]{:S(2)}) collective-permute-start(bf16[2,2,72,896]{3,2,1,0:T(8,128)(2,1)S(1)} %select_bitcast_fusion), channel_id=1, source_target_pairs={{0,4},{2,6},{4,0},{6,2},{8,12},{10,14},{12,8},{14,10},{16,20},{18,... | collective-permute-start | bytes 1548296 | tf_op jit(solution)/shard_map/ppermute | solution.py:246
  463.1 7.8 %collective-permute-start.27 = (bf16[1152,1024]{0,1:T(8,128)(2,1)S(1)}, bf16[1152,1024]{0,1:T(8,128)(2,1)S(1)}, u32[]{:S(2)}, u32[]{:S(2)}) collective-permute-start(bf16[1152,1024]{0,1:T(8,128)(2,1)S(1)} %pad_maximum_fusion.1), channel_id=1, source_target_pairs={{0,1},{1,0},{2,3},{3,2},{4,5},{5,4},{6,7},{7,6},{8,9},{9,8},{10,11... | collective-permute-start | bytes 7077896 | tf_op jit(solution)/shard_map/ppermute | solution.py:238
  465.4 16.3 %collective-permute-start.28 = (bf16[3,72,896]{2,1,0:T(8,128)(2,1)}, bf16[3,72,896]{2,1,0:T(8,128)(2,1)S(1)}, u32[]{:S(2)}, u32[]{:S(2)}) collective-permute-start(bf16[3,72,896]{2,1,0:T(8,128)(2,1)} %select_bitcast_fusion.7), channel_id=1, source_target_pairs={{0,2},{2,0},{4,6},{6,4},{8,10},{10,8},{12,14},{14,12},{16,18},{18,... | collective-permute-start | bytes 1161224 | tf_op jit(solution)/shard_map/ppermute | solution.py:246
  466.3 19.1 %collective-permute-start.29 = (bf16[3,72,896]{2,1,0:T(8,128)(2,1)}, bf16[3,72,896]{2,1,0:T(8,128)(2,1)}, u32[]{:S(2)}, u32[]{:S(2)}) collective-permute-start(bf16[3,72,896]{2,1,0:T(8,128)(2,1)} %get-tuple-element.359), channel_id=1, source_target_pairs={{0,8},{2,10},{4,12},{6,14},{8,0},{10,2},{12,4},{14,6},{16,24},{18,... | collective-permute-start | bytes 1161224 | tf_op jit(solution)/shard_map/ppermute | solution.py:246
  467.7 17.7 %collective-permute-start.30 = (bf16[3,72,896]{2,1,0:T(8,128)(2,1)}, bf16[3,72,896]{2,1,0:T(8,128)(2,1)}, u32[]{:S(2)}, u32[]{:S(2)}) collective-permute-start(bf16[3,72,896]{2,1,0:T(8,128)(2,1)} %get-tuple-element.360), channel_id=1, source_target_pairs={{0,10},{2,8},{4,14},{6,12},{8,2},{10,0},{12,6},{14,4},{16,26},{18,... | collective-permute-start | bytes 1161224 | tf_op jit(solution)/shard_map/ppermute | solution.py:246
  469.8 16.8 %collective-permute-start.24 = (bf16[2,384,512]{2,1,0:T(8,128)(2,1)}, bf16[2,384,512]{2,1,0:T(8,128)(2,1)}, u32[]{:S(2)}, u32[]{:S(2)}) collective-permute-start(bf16[2,384,512]{2,1,0:T(8,128)(2,1)} %get-tuple-element.133), channel_id=1, source_target_pairs={{0,1},{1,0},{2,3},{3,2},{4,5},{5,4},{6,7},{7,6},{8,9},{9,8},{10,11... | collective-permute-start | bytes 2359304 | tf_op jit(solution)/shard_map/ppermute | solution.py:238
  477.1 33.6 %all-to-all-start.8 = ((bf16[4,4,72,1024]{3,2,1,0:T(8,128)(2,1)}), bf16[4,4,72,1024]{3,2,1,0:T(8,128)(2,1)}, u32[]{:S(2)}, u32[]{:S(2)}) async-start(bf16[4,4,72,1024]{3,2,1,0:T(8,128)(2,1)} %bitcast.250), calls=%async_computation.8 | async-start | bytes 4718592 | tf_op jit(solution)/shard_map/all_to_all | solution.py:281
  488.2 10.6 %collective-permute-start.25 = (bf16[2,128,512]{2,1,0:T(8,128)(2,1)S(1)}, bf16[2,128,512]{2,1,0:T(8,128)(2,1)S(1)}, u32[]{:S(2)}, u32[]{:S(2)}) collective-permute-start(bf16[2,128,512]{2,1,0:T(8,128)(2,1)S(1)} %get-tuple-element.355), channel_id=1, source_target_pairs={{2,0},{4,2},{6,4},{3,1},{5,3},{7,5},{10,8},{12,10},{14,12},{11,9},... | collective-permute-start | bytes 786440 | tf_op jit(solution)/shard_map/ppermute | solution.py:252
  489.5 18.7 %collective-permute-start.26 = (bf16[2,128,512]{2,1,0:T(8,128)(2,1)S(1)}, bf16[2,128,512]{2,1,0:T(8,128)(2,1)S(1)}, u32[]{:S(2)}, u32[]{:S(2)}) collective-permute-start(bf16[2,128,512]{2,1,0:T(8,128)(2,1)S(1)} %get-tuple-element.356), channel_id=1, source_target_pairs={{4,0},{6,2},{5,1},{7,3},{12,8},{14,10},{13,9},{15,11},{20,16},{22,... | collective-permute-start | bytes 786440 | tf_op jit(solution)/shard_map/ppermute | solution.py:252
  513.9 19.9 %all-to-all-start.9 = ((bf16[4,72,1024]{2,1,0:T(8,128)(2,1)}), bf16[4,72,1024]{2,1,0:T(8,128)(2,1)S(1)}, u32[]{:S(2)}, u32[]{:S(2)}) async-start(bf16[4,72,1024]{2,1,0:T(8,128)(2,1)} %convert_reduce_fusion), calls=%async_computation.9 | async-start | bytes 1179648 | tf_op jit(solution)/shard_map/all_to_all | solution.py:281
  538.8 2.3 collective-permute-start.31
  542.1 13.5 %all-to-all-start.10 = ((bf16[4,4,80,256]{3,2,1,0:T(8,128)(2,1)}), bf16[4,4,80,256]{3,2,1,0:T(8,128)(2,1)S(1)}, u32[]{:S(2)}, u32[]{:S(2)}) async-start(bf16[4,4,80,256]{3,2,1,0:T(8,128)(2,1)} %bitcast.80), calls=%async_computation.10 | async-start | bytes 1310720 | tf_op jit(solution)/shard_map/all_to_all | solution.py:281
  556.4 9.7 %all-to-all-start.11 = ((bf16[4,80,256]{2,1,0:T(8,128)(2,1)}), bf16[4,80,256]{2,1,0:T(8,128)(2,1)S(1)}, u32[]{:S(2)}, u32[]{:S(2)}) async-start(bf16[4,80,256]{2,1,0:T(8,128)(2,1)} %reduce_sum.71), calls=%async_computation.11 | async-start | bytes 327680 | tf_op jit(solution)/shard_map/all_to_all | solution.py:281
  566.7 1.3 collective-permute-start.32
  (66 other events, 559.4 us)
